TPU v7x, 32 devices: a whole 2x2x4 slice. The times are simulated.
32 devices in a mesh: tm: 4 (over y, core), height: 2 (over x), head: 4 (over z).
Axes of the slice: x: 2, y: 2, z: 4, core: 2. Of those that a mesh axis runs over, the one named last changes fastest.
Arguments:
- queries: bfloat16 [3072, 3072], P(('tm', 'height'), 'head'), may hold values from -6 to 6
- keys: bfloat16 [3072, 3072], P(('tm', 'height'), 'head'), may hold values from -12 to 12
- values: bfloat16 [3072, 3072], P(('tm', 'height'), 'head'), may hold values from -6 to 6
- out_grad: bfloat16 [3072, 3072], P(('tm', 'height'), 'head'), may hold values from -6 to 6
- out_weight: bfloat16 [3072, 3072], P(None, 'head'), may hold values from -0.109375 to 0.109375
- window: int32 [8, 27], P(('tm', 'height')), may hold values from 0 to 1, as said below
- counts: int32 [8], P(('tm', 'height')), may hold values from 96 to 384, as said below
Outputs:
- query_grad: bfloat16 [3072, 3072], P(('tm', 'height'), 'head')
- key_grad: bfloat16 [3072, 3072], P(('tm', 'height'), 'head')
- value_grad: bfloat16 [3072, 3072], P(('tm', 'height'), 'head')
- weight_grad: float32 [3072, 3072], P(('tm', 'height'), 'head')
Inputs may be any that keep to these rules, and one draw needn't show every extreme that they name: `window`: entry 13, the tile itself, is 1 for every tile. `counts`: every tile outside the last row of height tiles holds 384 valid tokens.
All inputs are finite; a program needn't handle non-finite values.
Results may differ from a plain program's by a relative error of at most 0.023.
Values may be sent and summed in bfloat16 or wider, within the bound.
A program may use at most 128 MiB of HBM per device.

v0:
```python
from functools import reduce

import jax
import jax.numpy as jnp
from jax import lax
from jax.sharding import PartitionSpec as P

HDIM = 128
TILE = 384


neg_large = -1e30


def padded(cells, sides, width):
    for axis, dim in sides:
        count = lax.axis_size(axis)
        ends = count - 1
        head = lax.slice_in_dim(cells, 0, width, axis=dim)
        tail = lax.slice_in_dim(cells, cells.shape[dim] - width, cells.shape[dim], axis=dim)
        cells = jnp.concatenate(
            [
                lax.ppermute(tail, axis, [(i, (i + 1) % count) for i in range(ends)]),
                cells,
                lax.ppermute(head, axis, [((i + 1) % count, i) for i in range(ends)]),
            ],
            axis=dim,
        )
    return cells


def shifted(x, axis, by):
    size = lax.axis_size(axis)
    pairs = [(i, i + by) for i in range(size) if 0 <= i + by < size]
    return lax.ppermute(x, axis, pairs)


def offset_table():
    across = (0,)
    return [
        (time_step, height_step, width_step)
        for time_step in (-1, 0, 1)
        for height_step in (-1, 0, 1)
        for width_step in across
    ]


def offset_index(offset):
    return (offset[0] + 1) * 9 + (offset[1] + 1) * 3 + offset[2] + 1


def head_cols(source, head_number):
    return lax.dynamic_slice_in_dim(source, head_number * HDIM, HDIM, source.ndim - 1)


def put_cols(target, piece, head_number):
    return lax.dynamic_update_slice_in_dim(target, piece, head_number * HDIM, target.ndim - 1)


def on_device(queries, keys, values, out_grad, out_weight, window, counts):
    row_count, width_local = queries.shape
    heads_local = width_local // HDIM
    width_tiles = row_count // TILE
    score_scale = HDIM ** (-0.5)
    offsets = offset_table()
    full_grad = lax.all_gather(out_grad, "head", axis=1, tiled=True)
    grad_out = jnp.dot(full_grad, out_weight, preferred_element_type=jnp.float32).astype(
        jnp.bfloat16
    )
    positions = jnp.arange(TILE, dtype=jnp.int32)
    key_valid = (positions[None, :] < counts[:, None]).astype(jnp.bfloat16)
    key_block = keys.reshape(1, 1, width_tiles, TILE, width_local)
    value_block = values.reshape(1, 1, width_tiles, TILE, width_local)
    key_rim, value_rim, valid_rim = (
        padded(key_block, (("tm", 0), ("height", 1)), 1),
        padded(value_block, (("tm", 0), ("height", 1)), 1),
        padded(key_valid.reshape(1, 1, width_tiles, TILE), (("tm", 0), ("height", 1)), 1),
    )
    allowed = [
        (window[:, offset_index(offset)] > 0)[:, None]
        & (valid_rim[1 + offset[0], 1 + offset[1]] > 0)
        for offset in offsets
    ]
    query_tiles = queries.reshape(width_tiles, TILE, width_local)
    grad_tiles = grad_out.reshape(width_tiles, TILE, width_local)

    def head_step(head_number, carry):
        query_head = head_cols(query_tiles, head_number)
        grad_head = head_cols(grad_tiles, head_number)
        key_list = [
            head_cols(key_rim[1 + offset[0], 1 + offset[1]], head_number) for offset in offsets
        ]
        value_list = [
            head_cols(value_rim[1 + offset[0], 1 + offset[1]], head_number) for offset in offsets
        ]
        score_list = [
            jnp.where(
                allowed[number][:, None, :],
                jnp.einsum(
                    "nid,njd->nij", query_head, key_list[number], preferred_element_type=jnp.float32
                )
                * score_scale,
                neg_large,
            )
            for number in range(len(offsets))
        ]
        row_max = reduce(
            jnp.maximum, [jnp.max(block, axis=2, keepdims=True) for block in score_list]
        )
        row_total = reduce(
            jnp.add,
            [jnp.sum(jnp.exp(block - row_max), axis=2, keepdims=True) for block in score_list],
        )
        log_total = row_max + jnp.log(row_total)
        weight_list = [jnp.exp(block - log_total) for block in score_list]
        low_list = [block.astype(jnp.bfloat16) for block in weight_list]
        attended = reduce(
            jnp.add,
            [
                jnp.einsum(
                    "nij,njd->nid",
                    low_list[number],
                    value_list[number],
                    preferred_element_type=jnp.float32,
                )
                for number in range(len(offsets))
            ],
        ).astype(jnp.bfloat16)
        row_delta = jnp.sum(
            grad_head.astype(jnp.float32) * attended.astype(jnp.float32), axis=2, keepdims=True
        )
        grad_list = [
            (
                weight_list[number]
                * (
                    jnp.einsum(
                        "nid,njd->nij",
                        grad_head,
                        value_list[number],
                        preferred_element_type=jnp.float32,
                    )
                    - row_delta
                )
            ).astype(jnp.bfloat16)
            for number in range(len(offsets))
        ]
        query_grad = (
            reduce(
                jnp.add,
                [
                    jnp.einsum(
                        "nij,njd->nid",
                        grad_list[number],
                        key_list[number],
                        preferred_element_type=jnp.float32,
                    )
                    for number in range(len(offsets))
                ],
            )
            * score_scale
        ).astype(jnp.bfloat16)
        query_acc = put_cols(carry[0], query_grad, head_number)
        attended_acc = put_cols(carry[1], attended, head_number)
        key_slots = [[None, None, None] for slot in range(3)]
        value_slots = [[None, None, None] for slot in range(3)]
        for number, offset in enumerate(offsets):
            key_part = jnp.einsum(
                "nij,nid->njd", grad_list[number], query_head, preferred_element_type=jnp.float32
            )
            value_part = jnp.einsum(
                "nij,nid->njd", low_list[number], grad_head, preferred_element_type=jnp.float32
            )
            time_slot, height_slot = (1 + offset[0], 1 + offset[1])
            previous = key_slots[time_slot][height_slot]
            key_slots[time_slot][height_slot] = (
                key_part if previous is None else previous + key_part
            )
            previous = value_slots[time_slot][height_slot]
            value_slots[time_slot][height_slot] = (
                value_part if previous is None else previous + value_part
            )
        key_grid = jnp.stack([jnp.stack(row, axis=0) for row in key_slots], axis=0)
        value_grid = jnp.stack([jnp.stack(row, axis=0) for row in value_slots], axis=0)
        return (
            query_acc,
            attended_acc,
            put_cols(carry[2], key_grid, head_number),
            put_cols(carry[3], value_grid, head_number),
        )

    query_zero = jnp.zeros((width_tiles, TILE, width_local), jnp.bfloat16)
    grid_zero = jnp.zeros((3, 3, width_tiles, TILE, width_local), jnp.float32)
    start = (query_zero, query_zero, grid_zero, grid_zero)
    results = lax.fori_loop(0, heads_local, head_step, start)
    query_out = results[0].reshape(row_count, width_local)
    attended_all = results[1].reshape(row_count, width_local)
    key_ext = results[2]
    value_ext = results[3]
    key_sum = key_ext[:, 1]
    value_sum = value_ext[:, 1]
    for step_sign, source_slot in ((1, 2), (-1, 0)):
        got_key, got_value = (
            shifted(key_ext[:, source_slot].astype(jnp.bfloat16), "height", step_sign).astype(
                jnp.float32
            ),
            shifted(value_ext[:, source_slot].astype(jnp.bfloat16), "height", step_sign).astype(
                jnp.float32
            ),
        )
        key_sum = key_sum + got_key
        value_sum = value_sum + got_value
    key_final = key_sum[1]
    value_final = value_sum[1]
    for step_sign, source_slot in ((1, 2), (-1, 0)):
        got_key, got_value = (
            shifted(key_sum[source_slot].astype(jnp.bfloat16), "tm", step_sign).astype(jnp.float32),
            shifted(value_sum[source_slot].astype(jnp.bfloat16), "tm", step_sign).astype(
                jnp.float32
            ),
        )
        key_final = key_final + got_key
        value_final = value_final + got_value
    key_out = (key_final * score_scale).astype(jnp.bfloat16).reshape(row_count, width_local)
    value_out = value_final.astype(jnp.bfloat16).reshape(row_count, width_local)
    group_count = lax.axis_size("tm") * lax.axis_size("height")
    token_share = (row_count * group_count) ** (-0.5)
    weight_out = lax.psum_scatter(
        (
            lax.dot_general(
                full_grad,
                attended_all,
                (((0,), (0,)), ((), ())),
                preferred_element_type=jnp.float32,
            )
            * token_share
        ).astype(jnp.bfloat16),
        ("tm", "height"),
        scatter_dimension=0,
        tiled=True,
    ).astype(jnp.float32)
    return (query_out, key_out, value_out, weight_out)


def solution(mesh):
    placed = (
        P(("tm", "height"), "head"),
        P(("tm", "height"), "head"),
        P(("tm", "height"), "head"),
        P(("tm", "height"), "head"),
        P(None, "head"),
        P(("tm", "height"), None),
        P(("tm", "height")),
    )
    return jax.shard_map(
        on_device,
        mesh=mesh,
        in_specs=placed,
        out_specs=(
            P(("tm", "height"), "head"),
            P(("tm", "height"), "head"),
            P(("tm", "height"), "head"),
            P(("tm", "height"), "head"),
        ),
        check_vma=False,
    )
```

profile of v0, /device:TPU:1, one launch (start us, length us, event | category | flops | bytes accessed | tf_op | source)
XLA Modules:
  0.0 502.1 jit_solution(5615271395219883456)
XLA Ops:
  7.9 2.0 collective-permute-start.4
  9.9 4.5 collective-permute-start.3
  14.4 1.9 collective-permute-start.9
  16.4 3.6 collective-permute-start.8
  22.4 2.5 pad_maximum_fusion.2
  26.3 5.3 %collective-permute-start.5 = (bf16[3,1,1,384,768]{4,3,2,1,0:T(8,128)(2,1)}, bf16[3,1,1,384,768]{4,3,2,1,0:T(8,128)(2,1)}, u32[]{:S(2)}, u32[]{:S(2)}) collective-permute-start(bf16[3,1,1,384,768]{4,3,2,1,0:T(8,128)(2,1)} %pad_maximum_fusion.2), channel_id=1, source_target_pairs={{0,4},{1,5},{2,6},{3,7},{8,12},{9,13},{10,14},{11,15},{16,20},{17,... | collective-permute-start | bytes 5308424 | tf_op jit(solution)/shard_map/ppermute | solution.py:23
  31.6 1.7 pad_maximum_fusion.3
  34.6 6.5 %collective-permute-start.10 = (bf16[3,1,1,384,768]{4,3,2,1,0:T(8,128)(2,1)}, bf16[3,1,1,384,768]{4,3,2,1,0:T(8,128)(2,1)}, u32[]{:S(2)}, u32[]{:S(2)}) collective-permute-start(bf16[3,1,1,384,768]{4,3,2,1,0:T(8,128)(2,1)} %pad_maximum_fusion.3), channel_id=1, source_target_pairs={{0,4},{1,5},{2,6},{3,7},{8,12},{9,13},{10,14},{11,15},{16,20},{17,... | collective-permute-start | bytes 5308424 | tf_op jit(solution)/shard_map/ppermute | solution.py:23
  41.1 1.9 collective-permute-start.1
  44.2 3.9 collective-permute-done.1
  48.1 1.9 collective-permute-start
  56.4 47.6 %collective-permute-done.6 = bf16[3,1,1,384]{3,2,1,0:T(2,128)(2,1)S(1)} collective-permute-done((bf16[3,1,1,384]{3,2,1,0:T(2,128)(2,1)S(1)}, bf16[3,1,1,384]{3,2,1,0:T(2,128)(2,1)S(1)}, u32[]{:S(2)}, u32[]{:S(2)}) %collective-permute-start.6) | collective-permute-done | bytes 2336 | tf_op jit(solution)/shard_map/ppermute | solution.py:25
  106.2 5.9 %fusion.205 = bf16[1,384,768]{2,1,0:T(8,128)(2,1)} fusion(bf16[384,3072]{1,0:T(8,128)(2,1)} %all-gather.2.cloned.1.call-done, bf16[3072,768]{1,0:T(8,128)(2,1)} %param.13), kind=kOutput, calls=%fused_computation.286 | convolution fusion | flops 1812234240 | bytes 7667712 | tf_op jit(solution)/shard_map/dot_general | solution.py:67
  113.8 4.8 broadcast_in_dim.236.clone2
  118.6 4.9 broadcast_in_dim.236.clone
  123.5 209.6 %while.20 = (s32[]{:T(128)}, bf16[1,384,768]{2,1,0:T(8,128)(2,1)}, bf16[1,384,768]{1,2,0:T(8,128)(2,1)}, f32[3,3,1,384,768]{4,3,0,2,1:T(8,128)}, f32[3,3,1,384,7...) while((s32[]{:T(128)}, bf16[1,384,768]{2,1,0:T(8,128)(2,1)}, ...), condition=%wide.region_20.21_spmd.clone, body=%wide.region_0.20_spmd.clone.sunk | while | flops 2060355072 | bytes 80758632 | solution.py:194
  128.0 1.5 fusion.467
  129.6 1.5 fusion.456
  132.1 1.5 fusion.454
  156.2 2.3 copy_dynamic-update-slice_fusion.3
  163.0 1.5 fusion.467
  164.5 1.5 fusion.456
  167.1 1.5 fusion.454
  191.2 2.2 copy_dynamic-update-slice_fusion.3
  226.1 2.1 copy_dynamic-update-slice_fusion.3
  261.0 2.2 copy_dynamic-update-slice_fusion.3
  296.0 2.2 copy_dynamic-update-slice_fusion.3
  330.9 2.1 copy_dynamic-update-slice_fusion.3
  333.1 6.7 %fusion.204 = bf16[3072,768]{0,1:T(8,128)(2,1)} fusion(bf16[384,3072]{1,0:T(8,128)(2,1)} %all-gather.2.cloned.1.call-done, bf16[1,384,768]{1,2,0:T(8,128)(2,1)} %get-tuple-element.419), kind=kOutput, calls=%fused_computation.274 | convolution fusion | flops 1816657920 | bytes 7667712 | tf_op jit(solution)/shard_map/dot_general | solution.py:229
  339.7 6.6 %copy.56 = bf16[3072,768]{1,0:T(8,128)(2,1)} copy(bf16[3072,768]{0,1:T(8,128)(2,1)} %fusion.204) | data formatting | bytes 9437184
  346.4 7.5 %convert.19 = bf16[3,3,1,384,768]{4,3,0,2,1:T(8,128)(2,1)} convert(f32[3,3,1,384,768]{4,3,0,2,1:T(8,128)} %get-tuple-element.418) | non-fusion elementwise | flops 2654208 | bytes 15925248 | tf_op jit(solution)/shard_map/convert.4
  353.9 5.3 %slice_bitcast_fusion.1 = (bf16[3,1,384,768]{3,2,0,1:T(8,128)(2,1)}, bf16[3,1,384,768]{3,2,1,0:T(8,128)(2,1)}) fusion(bf16[3,3,1,384,768]{4,3,0,2,1:T(8,128)(2,1)} %convert.19), kind=kLoop, calls=%fused_computation.280 | loop fusion | bytes 7077888 | tf_op jit(solution)/shard_map/convert_element_type | solution.py:206
  359.2 3.7 collective-permute-start.16
  364.2 2.9 convert.17
  367.2 2.2 slice_bitcast_fusion.3
  369.4 6.1 %collective-permute-start.12 = (bf16[3,1,384,768]{3,2,0,1:T(8,128)(2,1)S(1)}, bf16[3,1,384,768]{3,2,0,1:T(8,128)(2,1)S(1)}, u32[]{:S(2)}, u32[]{:S(2)}) collective-permute-start(bf16[3,1,384,768]{3,2,0,1:T(8,128)(2,1)S(1)} %get-tuple-element.643), channel_id=1, source_target_pairs={{0,4},{1,5},{2,6},{3,7},{8,12},{9,13},{10,14},{11,15},{16,20},{17,... | collective-permute-start | bytes 5308424 | tf_op jit(solution)/shard_map/ppermute | solution.py:35
  376.8 43.2 %collective-permute-done.16 = bf16[3,1,384,768]{3,2,0,1:T(8,128)(2,1)S(1)} collective-permute-done((bf16[3,1,384,768]{3,2,0,1:T(8,128)(2,1)}, bf16[3,1,384,768]{3,2,0,1:T(8,128)(2,1)S(1)}, u32[]{:S(2)}, u32[]{:S(2)}) %collective-permute-start.16) | collective-permute-done | bytes 1769504 | tf_op jit(solution)/shard_map/ppermute | solution.py:35
  420.1 3.9 collective-permute-done.17
  424.0 33.9 %collective-permute-done.12 = bf16[3,1,384,768]{3,2,0,1:T(8,128)(2,1)S(1)} collective-permute-done((bf16[3,1,384,768]{3,2,0,1:T(8,128)(2,1)S(1)}, bf16[3,1,384,768]{3,2,0,1:T(8,128)(2,1)S(1)}, u32[]{:S(2)}, u32[]{:S(2)}) %collective-permute-start.12) | collective-permute-done | bytes 1769504 | tf_op jit(solution)/shard_map/ppermute | solution.py:35
  459.1 2.8 collective-permute-done.13
  461.9 8.9 %fusion.216 = (bf16[3,1,384,768]{3,2,1,0:T(8,128)(2,1)}, f32[3,1,384,768]{3,2,1,0:T(8,128)}, bf16[3,1,384,768]{3,2,1,0:T(8,128)(2,1)S(1)}, f32[3,1,384,768]{3,2,1,0:T(8,128)S(1)}) fusion(bf16[3,1,384,768]{3,2,1,0:T(8,128)(2,1)} %collective-permute-done.17, bf16[3,1,384,768]{3,2,0,1:T(8,128)(2,1)} %copy-done.5, ...), kind=kLoop, calls=%fused_computation.313 | loop fusion | flops 8847360 | bytes 24772608 | tf_op jit(solution)/shard_map/convert.2
  472.1 1.9 collective-permute-start.18
  474.0 2.5 collective-permute-start.19
  476.6 3.1 collective-permute-start.14
  479.7 1.9 collective-permute-start.15
  481.6 3.6 collective-permute-done.19
  485.2 2.3 fusion.214
  487.5 4.0 collective-permute-done.15
  (529 shorter events, 204.8 us)
Async XLA Ops:
  7.2 99.0 %all-gather.2.cloned.1.call-start = ((), (), s32[]{:S(2)}) async-start(), calls=%async_computation.1 | async-start | bytes 2949120 | tf_op jit(solution)/shard_map/all_gather | solution.py:66
  7.9 484.7 %reduce-scatter.4.cloned.1.call-start = ((), (), s32[]{:S(2)}) async-start(), calls=%async_computation.2 | async-start | bytes 5308416
  7.9 12.7 %collective-permute-start.4 = (bf16[1,1,1,384,768]{4,3,2,1,0:T(8,128)(2,1)}, bf16[1,1,1,384,768]{4,3,2,1,0:T(8,128)(2,1)S(1)}, u32[]{:S(2)}, u32[]{:S(2)}) collective-permute-start(bf16[1,1,1,384,768]{4,3,2,1,0:T(8,128)(2,1)} %bitcast.605), channel_id=1, source_target_pairs={{8,0},{16,8},{24,16},{9,1},{17,9},{25,17},{10,2},{18,10},{26,18},{... | collective-permute-start | bytes 1769480 | tf_op jit(solution)/shard_map/ppermute | solution.py:25
  9.9 11.6 %collective-permute-start.3 = (bf16[1,1,1,384,768]{4,3,2,1,0:T(8,128)(2,1)}, bf16[1,1,1,384,768]{4,3,2,1,0:T(8,128)(2,1)S(1)}, u32[]{:S(2)}, u32[]{:S(2)}) collective-permute-start(bf16[1,1,1,384,768]{4,3,2,1,0:T(8,128)(2,1)} %bitcast.606), channel_id=1, source_target_pairs={{0,8},{8,16},{16,24},{1,9},{9,17},{17,25},{2,10},{10,18},{18,26},{... | collective-permute-start | bytes 1769480 | tf_op jit(solution)/shard_map/ppermute | solution.py:23
  14.4 17.2 %collective-permute-start.9 = (bf16[1,1,1,384,768]{4,3,2,1,0:T(8,128)(2,1)}, bf16[1,1,1,384,768]{4,3,2,1,0:T(8,128)(2,1)S(1)}, u32[]{:S(2)}, u32[]{:S(2)}) collective-permute-start(bf16[1,1,1,384,768]{4,3,2,1,0:T(8,128)(2,1)} %bitcast.608), channel_id=1, source_target_pairs={{8,0},{16,8},{24,16},{9,1},{17,9},{25,17},{10,2},{18,10},{26,18},{... | collective-permute-start | bytes 1769480 | tf_op jit(solution)/shard_map/ppermute | solution.py:25
  16.4 15.3 %collective-permute-start.8 = (bf16[1,1,1,384,768]{4,3,2,1,0:T(8,128)(2,1)}, bf16[1,1,1,384,768]{4,3,2,1,0:T(8,128)(2,1)S(1)}, u32[]{:S(2)}, u32[]{:S(2)}) collective-permute-start(bf16[1,1,1,384,768]{4,3,2,1,0:T(8,128)(2,1)} %bitcast.609), channel_id=1, source_target_pairs={{0,8},{8,16},{16,24},{1,9},{9,17},{17,25},{2,10},{10,18},{18,26},{... | collective-permute-start | bytes 1769480 | tf_op jit(solution)/shard_map/ppermute | solution.py:23
  20.7 11.0 %copy-start.2 = (bf16[384,768]{1,0:T(8,128)(2,1)S(1)}, bf16[384,768]{1,0:T(8,128)(2,1)}, u32[]{:S(2)}) copy-start(bf16[384,768]{1,0:T(8,128)(2,1)} %param.11) | copy-start | bytes 1769476
  21.5 0.8 copy-start.1
  24.8 18.1 %copy-start.7 = (s32[1,27]{1,0:T(1,128)S(1)}, s32[1,27]{1,0:T(1,128)}, u32[]{:S(2)}) copy-start(s32[1,27]{1,0:T(1,128)} %param.14) | copy-start | bytes 328
  24.8 87.2 %collective-permute-start.7 = (bf16[3,1,1,384,768]{4,3,2,1,0:T(8,128)(2,1)}, bf16[3,1,1,384,768]{4,3,2,1,0:T(8,128)(2,1)S(1)}, u32[]{:S(2)}, u32[]{:S(2)}) collective-permute-start(bf16[3,1,1,384,768]{4,3,2,1,0:T(8,128)(2,1)} %pad_maximum_fusion.2), channel_id=1, source_target_pairs={{4,0},{5,1},{6,2},{7,3},{12,8},{13,9},{14,10},{15,11},{20,16},{21,... | collective-permute-start | bytes 5308424 | tf_op jit(solution)/shard_map/ppermute | solution.py:25
  26.3 85.8 %collective-permute-start.5 = (bf16[3,1,1,384,768]{4,3,2,1,0:T(8,128)(2,1)}, bf16[3,1,1,384,768]{4,3,2,1,0:T(8,128)(2,1)}, u32[]{:S(2)}, u32[]{:S(2)}) collective-permute-start(bf16[3,1,1,384,768]{4,3,2,1,0:T(8,128)(2,1)} %pad_maximum_fusion.2), channel_id=1, source_target_pairs={{0,4},{1,5},{2,6},{3,7},{8,12},{9,13},{10,14},{11,15},{16,20},{17,... | collective-permute-start | bytes 5308424 | tf_op jit(solution)/shard_map/ppermute | solution.py:23
  31.6 1.7 copy-start.3
  31.6 1.7 copy-start.4
  33.3 78.7 %collective-permute-start.11 = (bf16[3,1,1,384,768]{4,3,2,1,0:T(8,128)(2,1)}, bf16[3,1,1,384,768]{4,3,2,1,0:T(8,128)(2,1)}, u32[]{:S(2)}, u32[]{:S(2)}) collective-permute-start(bf16[3,1,1,384,768]{4,3,2,1,0:T(8,128)(2,1)} %pad_maximum_fusion.3), channel_id=1, source_target_pairs={{4,0},{5,1},{6,2},{7,3},{12,8},{13,9},{14,10},{15,11},{20,16},{21,... | collective-permute-start | bytes 5308424 | tf_op jit(solution)/shard_map/ppermute | solution.py:25
  34.6 77.5 %collective-permute-start.10 = (bf16[3,1,1,384,768]{4,3,2,1,0:T(8,128)(2,1)}, bf16[3,1,1,384,768]{4,3,2,1,0:T(8,128)(2,1)}, u32[]{:S(2)}, u32[]{:S(2)}) collective-permute-start(bf16[3,1,1,384,768]{4,3,2,1,0:T(8,128)(2,1)} %pad_maximum_fusion.3), channel_id=1, source_target_pairs={{0,4},{1,5},{2,6},{3,7},{8,12},{9,13},{10,14},{11,15},{16,20},{17,... | collective-permute-start | bytes 5308424 | tf_op jit(solution)/shard_map/ppermute | solution.py:23
  41.1 7.0 %collective-permute-start.1 = (bf16[1,1,1,384]{3,2,1,0:T(2,128)(2,1)S(1)}, bf16[1,1,1,384]{3,2,1,0:T(2,128)(2,1)S(1)}, u32[]{:S(2)}, u32[]{:S(2)}) collective-permute-start(bf16[1,1,1,384]{3,2,1,0:T(2,128)(2,1)S(1)} %compare_convert_fusion.1), channel_id=1, source_target_pairs={{8,0},{16,8},{24,16},{9,1},{17,9},{25,17},{10,2},{18,10},{26,18},{... | collective-permute-start | bytes 2312 | tf_op jit(solution)/shard_map/ppermute | solution.py:25
  48.1 6.9 %collective-permute-start = (bf16[1,1,1,384]{3,2,1,0:T(2,128)(2,1)S(1)}, bf16[1,1,1,384]{3,2,1,0:T(2,128)(2,1)S(1)}, u32[]{:S(2)}, u32[]{:S(2)}) collective-permute-start(bf16[1,1,1,384]{3,2,1,0:T(2,128)(2,1)S(1)} %compare_convert_fusion.1), channel_id=1, source_target_pairs={{0,8},{8,16},{16,24},{1,9},{9,17},{17,25},{2,10},{10,18},{18,26},{... | collective-permute-start | bytes 2312 | tf_op jit(solution)/shard_map/ppermute | solution.py:23
  55.0 48.9 %collective-permute-start.6 = (bf16[3,1,1,384]{3,2,1,0:T(2,128)(2,1)S(1)}, bf16[3,1,1,384]{3,2,1,0:T(2,128)(2,1)S(1)}, u32[]{:S(2)}, u32[]{:S(2)}) collective-permute-start(bf16[3,1,1,384]{3,2,1,0:T(2,128)(2,1)S(1)} %pad_maximum_fusion.4), channel_id=1, source_target_pairs={{4,0},{5,1},{6,2},{7,3},{12,8},{13,9},{14,10},{15,11},{20,16},{21,... | collective-permute-start | bytes 6920 | tf_op jit(solution)/shard_map/ppermute | solution.py:25
  103.9 2.2 collective-permute-start.2
  118.6 4.9 copy-start
  346.4 17.9 %slice-start = ((s8[10616832]{0:T(1024)(128)(4,1)}), s8[4194304]{0:T(1024)(128)(4,1)S(1)}, s32[]{:S(2)}) async-start(s8[10616832]{0:T(1024)(128)(4,1)} %bitcast.603), calls=%async_computation.3 | async-start | bytes 8388608
  346.4 17.9 %slice-start.1 = ((s8[10616832]{0:T(1024)(128)(4,1)}), s8[4194304]{0:T(1024)(128)(4,1)S(1)}, s32[]{:S(2)}) async-start(s8[10616832]{0:T(1024)(128)(4,1)} %bitcast.603), calls=%async_computation.4 | async-start | bytes 8388608
  346.4 17.9 %slice-start.2 = ((s8[10616832]{0:T(1024)(128)(4,1)}), s8[2228224]{0:T(1024)(128)(4,1)S(1)}, s32[]{:S(2)}) async-start(s8[10616832]{0:T(1024)(128)(4,1)} %bitcast.603), calls=%async_computation.5 | async-start | bytes 4456448
  359.2 60.8 %collective-permute-start.16 = (bf16[3,1,384,768]{3,2,0,1:T(8,128)(2,1)}, bf16[3,1,384,768]{3,2,0,1:T(8,128)(2,1)S(1)}, u32[]{:S(2)}, u32[]{:S(2)}) collective-permute-start(bf16[3,1,384,768]{3,2,0,1:T(8,128)(2,1)} %get-tuple-element.641), channel_id=1, source_target_pairs={{0,4},{1,5},{2,6},{3,7},{8,12},{9,13},{10,14},{11,15},{16,20},{17,... | collective-permute-start | bytes 5308424 | tf_op jit(solution)/shard_map/ppermute | solution.py:35
  362.9 61.0 %collective-permute-start.17 = (bf16[3,1,384,768]{3,2,1,0:T(8,128)(2,1)}, bf16[3,1,384,768]{3,2,1,0:T(8,128)(2,1)}, u32[]{:S(2)}, u32[]{:S(2)}) collective-permute-start(bf16[3,1,384,768]{3,2,1,0:T(8,128)(2,1)} %get-tuple-element.642), channel_id=1, source_target_pairs={{4,0},{5,1},{6,2},{7,3},{12,8},{13,9},{14,10},{15,11},{20,16},{21,... | collective-permute-start | bytes 5308424 | tf_op jit(solution)/shard_map/ppermute | solution.py:35
  369.4 88.4 %collective-permute-start.12 = (bf16[3,1,384,768]{3,2,0,1:T(8,128)(2,1)S(1)}, bf16[3,1,384,768]{3,2,0,1:T(8,128)(2,1)S(1)}, u32[]{:S(2)}, u32[]{:S(2)}) collective-permute-start(bf16[3,1,384,768]{3,2,0,1:T(8,128)(2,1)S(1)} %get-tuple-element.643), channel_id=1, source_target_pairs={{0,4},{1,5},{2,6},{3,7},{8,12},{9,13},{10,14},{11,15},{16,20},{17,... | collective-permute-start | bytes 5308424 | tf_op jit(solution)/shard_map/ppermute | solution.py:35
  375.5 86.4 %collective-permute-start.13 = (bf16[3,1,384,768]{3,2,1,0:T(8,128)(2,1)S(1)}, bf16[3,1,384,768]{3,2,1,0:T(8,128)(2,1)}, u32[]{:S(2)}, u32[]{:S(2)}) collective-permute-start(bf16[3,1,384,768]{3,2,1,0:T(8,128)(2,1)S(1)} %get-tuple-element.644), channel_id=1, source_target_pairs={{4,0},{5,1},{6,2},{7,3},{12,8},{13,9},{14,10},{15,11},{20,16},{21,... | collective-permute-start | bytes 5308424 | tf_op jit(solution)/shard_map/ppermute | solution.py:35
  420.0 37.8 %copy-start.5 = (bf16[3,1,384,768]{3,2,0,1:T(8,128)(2,1)}, bf16[3,1,384,768]{3,2,0,1:T(8,128)(2,1)S(1)}, u32[]{:S(2)}) copy-start(bf16[3,1,384,768]{3,2,0,1:T(8,128)(2,1)S(1)} %collective-permute-done.16) | copy-start | bytes 5308420
  457.9 1.2 copy-start.6
  472.1 9.5 %collective-permute-start.18 = (bf16[1,384,768]{2,1,0:T(8,128)(2,1)S(1)}, bf16[1,384,768]{2,1,0:T(8,128)(2,1)S(1)}, u32[]{:S(2)}, u32[]{:S(2)}) collective-permute-start(bf16[1,384,768]{2,1,0:T(8,128)(2,1)S(1)} %get-tuple-element.645), channel_id=1, source_target_pairs={{0,8},{8,16},{16,24},{1,9},{9,17},{17,25},{2,10},{10,18},{18,26},{... | collective-permute-start | bytes 1769480 | tf_op jit(solution)/shard_map/ppermute | solution.py:35
  474.0 11.2 %collective-permute-start.19 = (bf16[1,384,768]{2,1,0:T(8,128)(2,1)S(1)}, bf16[1,384,768]{2,1,0:T(8,128)(2,1)S(1)}, u32[]{:S(2)}, u32[]{:S(2)}) collective-permute-start(bf16[1,384,768]{2,1,0:T(8,128)(2,1)S(1)} %get-tuple-element.646), channel_id=1, source_target_pairs={{8,0},{16,8},{24,16},{9,1},{17,9},{25,17},{10,2},{18,10},{26,18},{... | collective-permute-start | bytes 1769480 | tf_op jit(solution)/shard_map/ppermute | solution.py:35
  476.6 10.9 %collective-permute-start.14 = (bf16[1,384,768]{2,1,0:T(8,128)(2,1)S(1)}, bf16[1,384,768]{2,1,0:T(8,128)(2,1)S(1)}, u32[]{:S(2)}, u32[]{:S(2)}) collective-permute-start(bf16[1,384,768]{2,1,0:T(8,128)(2,1)S(1)} %get-tuple-element.647), channel_id=1, source_target_pairs={{0,8},{8,16},{16,24},{1,9},{9,17},{17,25},{2,10},{10,18},{18,26},{... | collective-permute-start | bytes 1769480 | tf_op jit(solution)/shard_map/ppermute | solution.py:35
  479.7 11.9 %collective-permute-start.15 = (bf16[1,384,768]{2,1,0:T(8,128)(2,1)S(1)}, bf16[1,384,768]{2,1,0:T(8,128)(2,1)S(1)}, u32[]{:S(2)}, u32[]{:S(2)}) collective-permute-start(bf16[1,384,768]{2,1,0:T(8,128)(2,1)S(1)} %get-tuple-element.648), channel_id=1, source_target_pairs={{8,0},{16,8},{24,16},{9,1},{17,9},{25,17},{10,2},{18,10},{26,18},{... | collective-permute-start | bytes 1769480 | tf_op jit(solution)/shard_map/ppermute | solution.py:35
Sparse Core Ops, SparseCore 0:
  9.6 52.5 all-gather.1
  346.5 73.5 reduce-scatter.3
where the time goes:
time: 506 us; the launch traced here: 502 us
  matrix products  157 us (31%)
  waiting for transfers between devices  145 us (29%)
  local copies, waits for them, and re-layouts  70.9 us (14%)
  starting transfers between devices  54.9 us (11%)
  other arithmetic  51 us (10%)
  between operations  20.6 us (4%)
    ppermute x8, waiting for transfers between devices, shifted(): return lax.ppermute(x, axis, pairs)  91.5 us
    ppermute x6, waiting for transfers between devices, padded(): lax.ppermute(head, axis, [((i + 1) % count, i) for i in range(ends)])  51.5 us
    dot_general x54, matrix products, head_step(): jnp.einsum('nij,njd->nid', low_list[number], value_list[number], preferre...  31.4 us
    dot_general x54, matrix products, head_step(): jnp.einsum('nid,njd->nij', grad_head, value_list[number], preferred_eleme...  30.6 us
    dot_general x54, matrix products, head_step(): jnp.einsum('nij,njd->nid', grad_list[number], key_list[number], preferred...  29.7 us
    dot_general x54, matrix products, head_step(): jnp.einsum('nid,njd->nij', query_head, key_list[number], preferred_elemen...  26.1 us
    ppermute x6, starting transfers between devices, padded(): lax.ppermute(tail, axis, [(i, (i + 1) % count) for i in range(ends)])  23.3 us
    ppermute x8, starting transfers between devices, shifted(): return lax.ppermute(x, axis, pairs)  21.8 us
  transfers between devices with their start and end apart: 22, of which 10 were waited for; matrix products, arithmetic and copies ran while one was open for 8% of the time, Pallas kernels for 0%

commit v1 on v0

v1 whole, which is shorter than its diff:
```python
import functools

import jax
import jax.numpy as jnp
from jax import lax
from jax.experimental import pallas as pl
from jax.experimental.pallas import tpu as pltpu
from jax.sharding import PartitionSpec as P

HDIM = 128
TILE = 384
CHUNKS = 2
LOG2E = 1.4426950408889634

neg_large = -1e30


def attention_kernel(slots, bias_ref, query_ref, grad_ref, *refs):
    pair_refs = refs[:slots]
    query_out, attended_out, pair_out, score_ref = refs[slots:]
    scale = HDIM ** (-0.5)
    nt = (((1,), (1,)), ((), ()))
    tn = (((0,), (0,)), ((), ()))
    query = query_ref[...]
    grad = grad_ref[...]
    row_max = None
    for slot in range(slots):
        scores = lax.dot_general(
            query, pair_refs[slot][:TILE], nt, preferred_element_type=jnp.float32
        ) * (scale * LOG2E) + bias_ref[slot]
        score_ref[slot] = scores
        part = jnp.max(scores, axis=1, keepdims=True)
        row_max = part if row_max is None else jnp.maximum(row_max, part)
    total = None
    for slot in range(slots):
        raised = jnp.exp2(score_ref[slot] - row_max)
        score_ref[slot] = raised
        part = jnp.sum(raised, axis=1, keepdims=True)
        total = part if total is None else total + part
    inverse = 1.0 / total
    attended = None
    for slot in range(slots):
        weights = score_ref[slot] * inverse
        score_ref[slot] = weights
        low = weights.astype(jnp.bfloat16)
        part = jnp.dot(low, pair_refs[slot][TILE:], preferred_element_type=jnp.float32)
        attended = part if attended is None else attended + part
        pair_out[slot, TILE:] = lax.dot_general(
            low, grad, tn, preferred_element_type=jnp.float32
        ).astype(jnp.bfloat16)
    attended = attended.astype(jnp.bfloat16)
    attended_out[...] = attended
    delta = jnp.sum(
        grad.astype(jnp.float32) * attended.astype(jnp.float32), axis=1, keepdims=True
    )
    query_sum = None
    for slot in range(slots):
        grad_weights = lax.dot_general(
            grad, pair_refs[slot][TILE:], nt, preferred_element_type=jnp.float32
        )
        grad_scores = (score_ref[slot] * (grad_weights - delta)).astype(jnp.bfloat16)
        part = jnp.dot(grad_scores, pair_refs[slot][:TILE], preferred_element_type=jnp.float32)
        query_sum = part if query_sum is None else query_sum + part
        pair_out[slot, :TILE] = (
            lax.dot_general(grad_scores, query, tn, preferred_element_type=jnp.float32) * scale
        ).astype(jnp.bfloat16)
    query_out[...] = (query_sum * scale).astype(jnp.bfloat16)


def attention(bias, query, grad, pairs):
    slots = len(pairs)
    width = query.shape[1]
    heads = width // HDIM
    rows = pl.BlockSpec((TILE, HDIM), lambda h: (0, h))
    pair = pl.BlockSpec((2 * TILE, HDIM), lambda h: (0, h))
    return pl.pallas_call(
        functools.partial(attention_kernel, slots),
        grid=(heads,),
        in_specs=[pl.BlockSpec((slots, 1, TILE), lambda h: (0, 0, 0)), rows, rows]
        + [pair] * slots,
        out_specs=[rows, rows, pl.BlockSpec((slots, 2 * TILE, HDIM), lambda h: (0, 0, h))],
        out_shape=[
            jax.ShapeDtypeStruct((TILE, width), jnp.bfloat16),
            jax.ShapeDtypeStruct((TILE, width), jnp.bfloat16),
            jax.ShapeDtypeStruct((slots, 2 * TILE, width), jnp.bfloat16),
        ],
        scratch_shapes=[pltpu.VMEM((slots, TILE, TILE), jnp.float32)],
        compiler_params=pltpu.CompilerParams(vmem_limit_bytes=40 * 2**20),
        cost_estimate=pl.CostEstimate(
            flops=heads * slots * 20 * TILE * TILE * HDIM,
            bytes_accessed=heads * slots * 8 * TILE * HDIM,
            transcendentals=heads * slots * TILE * TILE,
        ),
    )(bias, query, grad, *pairs)


def moved(x, axis, by):
    size = lax.axis_size(axis)
    pairs = [(i, i + by) for i in range(size) if 0 <= i + by < size]
    return lax.ppermute(x, axis, pairs)


def swapped(x, axis, bit):
    size = lax.axis_size(axis)
    return lax.ppermute(x, axis, [(i, i ^ (1 << bit)) for i in range(size)])


def height_sends():
    if lax.axis_size("height") == 2:
        swap = functools.partial(swapped, axis="height", bit=0)
        return [(swap, swap)]
    down = functools.partial(moved, axis="height", by=1)
    up = functools.partial(moved, axis="height", by=-1)
    return [(down, up), (up, down)]


def height_steps():
    place = lax.axis_index("height")
    if lax.axis_size("height") == 2:
        return [jnp.int32(0), 1 - 2 * place]
    return [jnp.int32(0), jnp.int32(-1), jnp.int32(1)]


def reduce_scattered(gathered, attended):
    time_size, height_size = lax.axis_size("tm"), lax.axis_size("height")
    time_place, height_place = lax.axis_index("tm"), lax.axis_index("height")
    rows, features = gathered.shape
    block = features // (time_size * height_size)

    def product(part):
        return lax.dot_general(
            part.reshape(rows, -1), attended, (((0,), (0,)), ((), ())),
            preferred_element_type=jnp.float32,
        )

    if time_size & (time_size - 1) or height_size & (height_size - 1) or time_size < 2:
        return lax.psum_scatter(
            product(gathered).astype(jnp.bfloat16), ("tm", "height"),
            scatter_dimension=0, tiled=True,
        ).astype(jnp.float32)
    width = attended.shape[1]
    split = gathered.reshape(rows, time_size // 2, 2, height_size, block)
    bit = time_place % 2

    def half(which):
        part = lax.dynamic_index_in_dim(split, which, 2, keepdims=False)
        return product(part)

    sent = swapped(half(1 - bit).astype(jnp.bfloat16), "tm", 0)
    held = (half(bit) + sent.astype(jnp.float32)).reshape(
        time_size // 2, height_size, block, width
    )
    stages = [("height", number) for number in range(height_size.bit_length() - 1)]
    stages += [("tm", number) for number in range(1, time_size.bit_length() - 1)]
    for axis, number in stages:
        place = height_place if axis == "height" else time_place
        dim = 1 if axis == "height" else 0
        bit = (place // (1 << number)) % 2
        shape = held.shape
        wide = held.reshape(shape[:dim] + (shape[dim] // 2, 2) + shape[dim + 1 :])
        sent = lax.dynamic_index_in_dim(wide, 1 - bit, dim + 1, keepdims=False)
        kept = lax.dynamic_index_in_dim(wide, bit, dim + 1, keepdims=False)
        got = swapped(sent.astype(jnp.bfloat16), axis, number)
        held = kept + got.astype(jnp.float32)
    return held.reshape(block, width)


def on_device(queries, keys, values, out_grad, out_weight, window, counts):
    row_count, width_local = queries.shape
    heads_local = width_local // HDIM
    chunks = CHUNKS if heads_local % CHUNKS == 0 else 1
    width = width_local // chunks
    time_size, height_size = lax.axis_size("tm"), lax.axis_size("height")
    time_place, height_place = lax.axis_index("tm"), lax.axis_index("height")
    sends = height_sends()
    steps = height_steps()
    full_grad = lax.all_gather(out_grad, "head", axis=1, tiled=True)

    def columns(x, chunk):
        return x[:, chunk * width : (chunk + 1) * width]

    packs = []
    for chunk in range(chunks):
        pair = jnp.concatenate([columns(keys, chunk), columns(values, chunk)], axis=0)
        near = [pair] + [fetch(pair) for fetch, _ in sends]
        packs.append(
            near + [moved(x, "tm", 1) for x in near] + [moved(x, "tm", -1) for x in near]
        )
    count_near = [counts] + [fetch(counts) for fetch, _ in sends]
    count_all = (
        count_near
        + [moved(x, "tm", 1) for x in count_near]
        + [moved(x, "tm", -1) for x in count_near]
    )
    positions = jnp.arange(TILE, dtype=jnp.int32)
    rows = []
    number = 0
    for time_step in (0, -1, 1):
        for height_step in steps:
            index = (time_step + 1) * 9 + (height_step + 1) * 3 + 1
            time_at, height_at = time_place + time_step, height_place + height_step
            open_tile = (
                (lax.dynamic_index_in_dim(window[0], index, 0, keepdims=False) > 0)
                & (time_at >= 0)
                & (time_at < time_size)
                & (height_at >= 0)
                & (height_at < height_size)
            )
            rows.append(
                jnp.where(open_tile & (positions < count_all[number]), 0.0, neg_large)[None]
            )
            number += 1
    bias = jnp.stack(rows, axis=0).astype(jnp.float32)
    grad_out = jnp.dot(full_grad, out_weight, preferred_element_type=jnp.float32).astype(
        jnp.bfloat16
    )
    token_share = (row_count * time_size * height_size) ** (-0.5)
    outs = []
    per = len(steps)
    for chunk in range(chunks):
        query_out, attended, pair_out = attention(
            bias, columns(queries, chunk), columns(grad_out, chunk), packs[chunk]
        )
        back = moved(pair_out[per : 2 * per], "tm", -1).astype(jnp.float32)
        ahead = moved(pair_out[2 * per :], "tm", 1).astype(jnp.float32)
        own = pair_out[:per].astype(jnp.float32) + back + ahead
        final = own[0]
        for place, (_, give) in enumerate(sends):
            final = final + give(own[1 + place].astype(jnp.bfloat16)).astype(jnp.float32)
        final = final.astype(jnp.bfloat16)
        weight_out = reduce_scattered(full_grad, attended) * token_share
        outs.append((query_out, final[:TILE], final[TILE:], weight_out))
    return tuple(jnp.concatenate([out[i] for out in outs], axis=1) for i in range(4))


def solution(mesh):
    whole = P(("tm", "height"), "head")
    return jax.shard_map(
        on_device,
        mesh=mesh,
        in_specs=(
            whole,
            whole,
            whole,
            whole,
            P(None, "head"),
            P(("tm", "height"), None),
            P(("tm", "height")),
        ),
        out_specs=(whole,) * 4,
        check_vma=False,
    )
```

time: 506 us -> 228 us (0.45)
  matrix products: 157 us -> 15.6 us
  waiting for transfers between devices: 145 us -> 60.5 us
  other arithmetic: 51 us -> 12.3 us
  local copies, waits for them, and re-layouts: 70.9 us -> 36.5 us
  Pallas kernels: 0 us -> 30.1 us
    dot_general x325 -> x4, matrix products: 151 us -> 10.6 us  [product(): lax.dot_general(part.reshape(rows, -1), attended, (((0,), (0,)), ((), ())...]
    ppermute x20 -> x27, waiting for transfers between devices: 145 us -> 49.7 us  [the longest x11 39.6 us: swapped(): return lax.ppermute(x, axis, [(i, i ^ 1 << bit) for i in range(size)])]
    pallas_call x0 -> x2, Pallas kernels: none -> 30.1 us  [attention(): pl.pallas_call(functools.partial(attention_kernel, slots), grid=(heads,),...]
    slice x25 -> x7, local copies, waits for them, and re-layouts: 29 us -> 6.64 us  [the longest x2 3.47 us: on_device(): back = moved(pair_out[per:2 * per], 'tm', -1).astype(jnp.float32)]
    another operation x39 -> x1, other arithmetic: 20.8 us -> 0.7 us  [on_device(): bias = jnp.stack(rows, axis=0).astype(jnp.float32)]
    reshape x0 -> x3, local copies, waits for them, and re-layouts: none -> 14.2 us  [the longest x2 7.65 us: product(): part.reshape(rows, -1)]
    dynamic_update_slice x6 -> x0, other arithmetic: 13.1 us -> none  [put_cols(): lax.dynamic_update_slice_in_dim(target, piece, head_number * HDIM, target...]
    broadcast_in_dim x4 -> x0, local copies, waits for them, and re-layouts: 11.4 us -> none  [the longest x2 9.7 us: on_device(): grid_zero = jnp.zeros((3, 3, width_tiles, TILE, width_local), jnp.float32)]
  transfers between devices with their start and end apart: 22 -> 28, of which waited for: 10 -> 9; matrix products, arithmetic and copies ran while one was open for 8% -> 23% of each run, Pallas kernels for 0% -> 13%
where the time goes in v1:
time: 228 us; the launch traced here: 227 us
  waiting for transfers between devices  60.5 us (27%)
  starting transfers between devices  52.5 us (23%)
  local copies, waits for them, and re-layouts  36.5 us (16%)
  Pallas kernels  30.1 us (13%)
  between operations  19.2 us (8%)
  matrix products  15.6 us (7%)
  other arithmetic  12.3 us (5%)
    ppermute x16, starting transfers between devices, moved(): return lax.ppermute(x, axis, pairs)  44.1 us
    ppermute x11, waiting for transfers between devices, swapped(): return lax.ppermute(x, axis, [(i, i ^ 1 << bit) for i in range(size)])  39.6 us
    pallas_call x2, Pallas kernels, attention(): pl.pallas_call(functools.partial(attention_kernel, slots), grid=(heads,),...  30.1 us
    dot_general x4, matrix products, product(): lax.dot_general(part.reshape(rows, -1), attended, (((0,), (0,)), ((), ())...  10.6 us
    ppermute x16, waiting for transfers between devices, moved(): return lax.ppermute(x, axis, pairs)  10.1 us
    all_gather x1, waiting for transfers between devices, on_device(): full_grad = lax.all_gather(out_grad, 'head', axis=1, tiled=True)  10.1 us
    unnamed x52, local copies, waits for them, and re-layouts  10 us
    ppermute x11, starting transfers between devices, swapped(): return lax.ppermute(x, axis, [(i, i ^ 1 << bit) for i in range(size)])  8.4 us
  transfers between devices with their start and end apart: 28, of which 9 were waited for; matrix products, arithmetic and copies ran while one was open for 23% of the time, Pallas kernels for 13%

profile of v1, /device:TPU:1, one launch (start us, length us, event | category | flops | bytes accessed | tf_op | source)
XLA Modules:
  0.0 226.8 jit_solution(18241306947016534531)
XLA Ops:
  7.9 2.1 collective-permute-start
  10.0 2.9 %collective-permute-start.3 = (s32[1]{0:T(128)}, s32[1]{0:T(128)}, u32[]{:S(2)}, u32[]{:S(2)}) collective-permute-start(s32[1]{0:T(128)} %param.13), channel_id=1, source_target_pairs={{8,0},{16,8},{24,16},{9,1},{17,9},{25,17},{10,2},{18,10},{26,18},{... | collective-permute-start | bytes 20 | tf_op jit(solution)/shard_map/ppermute | solution.py:100
  12.9 3.0 %collective-permute-start.1 = (s32[1]{0:T(128)}, s32[1]{0:T(128)}, u32[]{:S(2)}, u32[]{:S(2)}) collective-permute-start(s32[1]{0:T(128)} %param.13), channel_id=1, source_target_pairs={{0,8},{8,16},{16,24},{1,9},{9,17},{17,25},{2,10},{10,18},{18,26},{... | collective-permute-start | bytes 20 | tf_op jit(solution)/shard_map/ppermute | solution.py:100
  15.9 1.4 fusion.12
  17.4 2.1 collective-permute-start.13
  26.7 3.9 %collective-permute-start.11 = (bf16[768,384]{1,0:T(8,128)(2,1)S(1)}, bf16[768,384]{1,0:T(8,128)(2,1)S(1)}, u32[]{:S(2)}, u32[]{:S(2)}) collective-permute-start(bf16[768,384]{1,0:T(8,128)(2,1)S(1)} %pad_maximum_fusion.2.refs_0_), channel_id=1, source_target_pairs={{0,8},{8,16},{16,24},{1,9},{9,17},{17,25},{2,10},{10,18},{18,26},{... | collective-permute-start | bytes 1769480 | tf_op jit(solution)/shard_map/ppermute | solution.py:100
  31.3 1.9 collective-permute-start.2
  34.0 3.5 %collective-permute-done.2 = s32[1]{0:T(128)} collective-permute-done((s32[1]{0:T(128)}, s32[1]{0:T(128)}, u32[]{:S(2)}, u32[]{:S(2)}) %collective-permute-start.2) | collective-permute-done | bytes 36 | tf_op jit(solution)/shard_map/ppermute | solution.py:100
  37.5 1.2 collective-permute-start.5
  39.4 1.9 collective-permute-start.4
  41.9 3.8 %collective-permute-done.4 = s32[1]{0:T(128)} collective-permute-done((s32[1]{0:T(128)}, s32[1]{0:T(128)}, u32[]{:S(2)}, u32[]{:S(2)}) %collective-permute-start.4) | collective-permute-done | bytes 36 | tf_op jit(solution)/shard_map/ppermute | solution.py:100
  46.4 1.9 collective-permute-start.14
  48.4 3.6 %collective-permute-start.12 = (bf16[768,384]{1,0:T(8,128)(2,1)S(1)}, bf16[768,384]{1,0:T(8,128)(2,1)S(1)}, u32[]{:S(2)}, u32[]{:S(2)}) collective-permute-start(bf16[768,384]{1,0:T(8,128)(2,1)S(1)} %collective-permute-done.10.refs_1_), channel_id=1, source_target_pairs={{0,8},{8,16},{16,24},{1,9},{9,17},{17,25},{2,10},{10,18},{18,26},{... | collective-permute-start | bytes 1769480 | tf_op jit(solution)/shard_map/ppermute | solution.py:100
  52.0 10.1 %all-gather.2.cloned.1.call-done = bf16[384,3072]{1,0:T(8,128)(2,1)} async-done(((bf16[384,768]{1,0:T(8,128)(2,1)}), bf16[384,3072]{1,0:T(8,128)(2,1)}) %all-gather.2.cloned.1.call-update) | async-done | bytes 2359312 | tf_op jit(solution)/shard_map/all_gather | solution.py:177
  62.1 5.0 %convolution_convert_fusion.2 = bf16[384,768]{1,0:T(8,128)(2,1)S(1)} fusion(bf16[384,3072]{1,0:T(8,128)(2,1)} %all-gather.2.cloned.1.call-done, bf16[3072,768]{1,0:T(8,128)(2,1)} %param.11), kind=kOutput, calls=%fused_computation.6 | convolution fusion | flops 1812234240 | bytes 7667712 | tf_op jit(solution)/shard_map/dot_general | solution.py:214
  68.9 2.6 %collective-permute-start.8 = (bf16[768,384]{1,0:T(8,128)(2,1)}, bf16[768,384]{1,0:T(8,128)(2,1)}, u32[]{:S(2)}, u32[]{:S(2)}) collective-permute-start(bf16[768,384]{1,0:T(8,128)(2,1)} %pad_maximum_fusion.1.refs_0_), channel_id=1, source_target_pairs={{8,0},{16,8},{24,16},{9,1},{17,9},{25,17},{10,2},{18,10},{26,18},{... | collective-permute-start | bytes 1769480 | tf_op jit(solution)/shard_map/ppermute | solution.py:100
  72.3 3.0 %collective-permute-start.6 = (bf16[768,384]{1,0:T(8,128)(2,1)}, bf16[768,384]{1,0:T(8,128)(2,1)}, u32[]{:S(2)}, u32[]{:S(2)}) collective-permute-start(bf16[768,384]{1,0:T(8,128)(2,1)} %pad_maximum_fusion.1.refs_0_), channel_id=1, source_target_pairs={{0,8},{8,16},{16,24},{1,9},{9,17},{17,25},{2,10},{10,18},{18,26},{... | collective-permute-start | bytes 1769480 | tf_op jit(solution)/shard_map/ppermute | solution.py:100
  75.3 2.2 collective-permute-start.9
  78.2 3.6 %collective-permute-start.7 = (bf16[768,384]{1,0:T(8,128)(2,1)}, bf16[768,384]{1,0:T(8,128)(2,1)}, u32[]{:S(2)}, u32[]{:S(2)}) collective-permute-start(bf16[768,384]{1,0:T(8,128)(2,1)} %collective-permute-done.5.refs_1_), channel_id=1, source_target_pairs={{0,8},{8,16},{16,24},{1,9},{9,17},{17,25},{2,10},{10,18},{18,26},{... | collective-permute-start | bytes 1769480 | tf_op jit(solution)/shard_map/ppermute | solution.py:100
  82.7 1.1 copy-done.13
  84.8 1.1 copy-done.17
  88.0 14.6 %shard_map.103 = (bf16[384,384]{1,0:T(8,128)(2,1)S(1)}, bf16[384,384]{1,0:T(8,128)(2,1)S(1)}, bf16[6,768,384]{2,1,0:T(8,128)(2,1)S(1)}) custom-call(f32[6,1,384]{2,1,0:T(1,128)S(1)} %constant_dynamic-update-slice_fusion.bias_ref, bf16[384,384]{1,0:T(8,128)(2,1)S(1)} %copy-done.8, bf16[384,384]{1,0:T(8,128)(2,1)S(1)} %get-tuple-element.31.grad_ref, ...), custom_call_target="tpu_custom_call" | custom-call | flops 6794772480 | bytes 7077888 | tf_op jit(solution)/shard_map/pallas_call | solution.py:76
  104.0 6.5 %reshape.172 = bf16[384,2,2,2,384]{4,3,2,1,0:T(2,128)(2,1)} reshape(bf16[384,3072]{1,0:T(8,128)(2,1)} %all-gather.2.cloned.1.call-done) | data formatting | bytes 4718592 | tf_op jit(solution)/shard_map/reshape | solution.py:142
  110.5 4.7 %constant_dynamic-slice_fusion = (bf16[384,2,1,2,384]{4,3,2,1,0:T(2,128)(2,1)}, bf16[384,2,1,2,384]{4,3,2,1,0:T(2,128)(2,1)}) fusion(bf16[384,2,2,2,384]{4,3,2,1,0:T(2,128)(2,1)} %reshape.172, s32[]{:T(128)S(6)} %select_n.140, s32[]{:T(128)S(6)} %select_n.139), kind=kLoop, calls=%fused_computation.45 | loop fusion | bytes 4718600 | tf_op jit(solution)/shard_map/jit(dynamic_index_in_dim)/dynamic_slice | solution.py:146
  115.2 3.8 %reshape.174 = bf16[384,1536]{1,0:T(8,128)(2,1)} reshape(bf16[384,2,1,2,384]{4,3,2,1,0:T(2,128)(2,1)} %get-tuple-element.20) | data formatting | bytes 2359296 | tf_op jit(solution)/shard_map/reshape | solution.py:132
  119.0 3.3 %convolution_convert_fusion = bf16[1536,384]{1,0:T(8,128)(2,1)} fusion(bf16[384,1536]{1,0:T(8,128)(2,1)} %reshape.174, bf16[384,384]{1,0:T(8,128)(2,1)} %copy-done.3), kind=kOutput, calls=%fused_computation.2 | convolution fusion | flops 453574656 | bytes 2654208 | tf_op jit(solution)/shard_map/dot_general | solution.py:131
  122.4 15.6 %shard_map.102 = (bf16[384,384]{1,0:T(8,128)(2,1)S(1)}, bf16[384,384]{1,0:T(8,128)(2,1)S(1)}, bf16[6,768,384]{2,1,0:T(8,128)(2,1)S(1)}) custom-call(f32[6,1,384]{2,1,0:T(1,128)S(1)} %constant_dynamic-update-slice_fusion.bias_ref, bf16[384,384]{1,0:T(8,128)(2,1)S(1)} %copy-done.7, bf16[384,384]{1,0:T(8,128)(2,1)S(1)} %copy-done.10, ...), custom_call_target="tpu_custom_call" | custom-call | flops 6794772480 | bytes 7077888 | tf_op jit(solution)/shard_map/pallas_call | solution.py:76
  138.0 2.3 %convolution_convert_fusion.1 = bf16[1536,384]{1,0:T(8,128)(2,1)} fusion(bf16[384,1536]{1,0:T(8,128)(2,1)S(1)} %copy-done.23, bf16[384,384]{1,0:T(8,128)(2,1)S(1)} %get-tuple-element.14), kind=kOutput, calls=%fused_computation.3 | convolution fusion | flops 453574656 | bytes 2654208 | tf_op jit(solution)/shard_map/dot_general | solution.py:131
  140.9 1.8 fusion.8
  142.6 1.9 collective-permute-start.15
  144.6 3.6 %collective-permute-start.16 = (bf16[2,768,384]{2,1,0:T(8,128)(2,1)}, bf16[2,768,384]{2,1,0:T(8,128)(2,1)}, u32[]{:S(2)}, u32[]{:S(2)}) collective-permute-start(bf16[2,768,384]{2,1,0:T(8,128)(2,1)} %get-tuple-element.17), channel_id=1, source_target_pairs={{0,8},{8,16},{16,24},{1,9},{9,17},{17,25},{2,10},{10,18},{18,26},{... | collective-permute-start | bytes 3538952 | tf_op jit(solution)/shard_map/ppermute | solution.py:100
  148.2 1.7 fusion.9
  149.9 3.8 %reshape.173 = bf16[384,1536]{1,0:T(8,128)(2,1)} reshape(bf16[384,2,1,2,384]{4,3,2,1,0:T(2,128)(2,1)} %get-tuple-element.21) | data formatting | bytes 2359296 | tf_op jit(solution)/shard_map/reshape | solution.py:132
  153.8 2.0 collective-permute-start.18
  155.8 1.9 pad_maximum_fusion.3
  157.7 3.9 %collective-permute-start.19 = (bf16[2,768,384]{2,1,0:T(8,128)(2,1)}, bf16[2,768,384]{2,1,0:T(8,128)(2,1)S(1)}, u32[]{:S(2)}, u32[]{:S(2)}) collective-permute-start(bf16[2,768,384]{2,1,0:T(8,128)(2,1)} %get-tuple-element.19), channel_id=1, source_target_pairs={{0,8},{8,16},{16,24},{1,9},{9,17},{17,25},{2,10},{10,18},{18,26},{... | collective-permute-start | bytes 3538952 | tf_op jit(solution)/shard_map/ppermute | solution.py:100
  161.6 2.7 %convolution_add_fusion = f32[1536,384]{1,0:T(8,128)S(1)} fusion(bf16[384,1536]{1,0:T(8,128)(2,1)} %reshape.173, bf16[384,384]{1,0:T(8,128)(2,1)S(1)} %copy-done.4, bf16[1536,384]{1,0:T(8,128)(2,1)} %collective-permute-done.24), kind=kOutput, calls=%fused_computation | convolution fusion | flops 454164480 | bytes 5013504 | tf_op jit(solution)/shard_map/dot_general | solution.py:131
  164.4 1.3 collective-permute-start.25
  165.7 2.2 convolution_add_fusion.1
  168.9 2.4 %convert_add_fusion.1 = f32[2,768,384]{2,1,0:T(8,128)S(1)} fusion(bf16[2,768,384]{2,1,0:T(8,128)(2,1)} %collective-permute-done.16, bf16[2,768,384]{2,1,0:T(8,128)(2,1)} %collective-permute-done.15, bf16[6,768,384]{2,1,0:T(8,128)(2,1)} %copy-done), kind=kLoop, calls=%fused_computation.5 | loop fusion | flops 2949120 | bytes 5898240 | tf_op jit(solution)/shard_map/add | solution.py:226
  172.1 1.3 collective-permute-done.18
  173.3 1.5 collective-permute-done.19
  175.3 1.3 collective-permute-start.20
  176.5 3.3 %collective-permute-done.25 = bf16[2,1,384,384]{3,2,1,0:T(8,128)(2,1)S(1)} collective-permute-done((bf16[2,1,384,384]{3,2,1,0:T(8,128)(2,1)S(1)}, bf16[2,1,384,384]{3,2,1,0:T(8,128)(2,1)S(1)}, u32[]{:S(2)}, u32[]{:S(2)}) %collective-permute-start.25) | collective-permute-done | bytes 589856 | tf_op jit(solution)/shard_map/ppermute | solution.py:105
  180.0 12.4 %collective-permute-done.22 = bf16[2,1,384,384]{3,2,1,0:T(8,128)(2,1)S(1)} collective-permute-done((bf16[2,1,384,384]{3,2,1,0:T(8,128)(2,1)S(1)}, bf16[2,1,384,384]{3,2,1,0:T(8,128)(2,1)S(1)}, u32[]{:S(2)}, u32[]{:S(2)}) %collective-permute-start.22) | collective-permute-done | bytes 589856 | tf_op jit(solution)/shard_map/ppermute | solution.py:105
  192.7 12.4 %collective-permute-done.17 = bf16[768,384]{1,0:T(8,128)(2,1)S(1)} collective-permute-done((bf16[768,384]{1,0:T(8,128)(2,1)S(1)}, bf16[768,384]{1,0:T(8,128)(2,1)S(1)}, u32[]{:S(2)}, u32[]{:S(2)}) %collective-permute-start.17) | collective-permute-done | bytes 589856 | tf_op jit(solution)/shard_map/ppermute | solution.py:105
  205.3 11.5 %collective-permute-done.20 = bf16[768,384]{1,0:T(8,128)(2,1)S(1)} collective-permute-done((bf16[768,384]{1,0:T(8,128)(2,1)S(1)}, bf16[768,384]{1,0:T(8,128)(2,1)S(1)}, u32[]{:S(2)}, u32[]{:S(2)}) %collective-permute-start.20) | collective-permute-done | bytes 589856 | tf_op jit(solution)/shard_map/ppermute | solution.py:105
  218.9 1.1 pad_maximum_fusion
  (106 shorter events, 21.0 us)
Async XLA Ops:
  7.2 55.0 %all-gather.2.cloned.1.call-start = ((), (), s32[]{:S(2)}) async-start(), calls=%async_computation | async-start | bytes 2949120 | tf_op jit(solution)/shard_map/all_gather | solution.py:177
  7.9 18.8 %collective-permute-start = (s32[1]{0:T(128)}, s32[1]{0:T(128)}, u32[]{:S(2)}, u32[]{:S(2)}) collective-permute-start(s32[1]{0:T(128)} %param.13), channel_id=1, source_target_pairs={{0,4},{4,0},{1,5},{5,1},{2,6},{6,2},{3,7},{7,3},{8,12},{12,8},{9,1... | collective-permute-start | bytes 20 | tf_op jit(solution)/shard_map/ppermute | solution.py:105
  10.0 29.4 %collective-permute-start.3 = (s32[1]{0:T(128)}, s32[1]{0:T(128)}, u32[]{:S(2)}, u32[]{:S(2)}) collective-permute-start(s32[1]{0:T(128)} %param.13), channel_id=1, source_target_pairs={{8,0},{16,8},{24,16},{9,1},{17,9},{25,17},{10,2},{18,10},{26,18},{... | collective-permute-start | bytes 20 | tf_op jit(solution)/shard_map/ppermute | solution.py:100
  12.9 18.5 %collective-permute-start.1 = (s32[1]{0:T(128)}, s32[1]{0:T(128)}, u32[]{:S(2)}, u32[]{:S(2)}) collective-permute-start(s32[1]{0:T(128)} %param.13), channel_id=1, source_target_pairs={{0,8},{8,16},{16,24},{1,9},{9,17},{17,25},{2,10},{10,18},{18,26},{... | collective-permute-start | bytes 20 | tf_op jit(solution)/shard_map/ppermute | solution.py:100
  17.3 3.1 %copy-start.25 = (s32[1,27]{1,0:T(1,128)S(1)}, s32[1,27]{1,0:T(1,128)}, u32[]{:S(2)}) copy-start(s32[1,27]{1,0:T(1,128)} %param.12) | copy-start | bytes 328
  17.3 5.3 %copy-start.24 = (bf16[384,768]{1,0:T(8,128)(2,1)S(1)}, bf16[384,768]{1,0:T(8,128)(2,1)}, u32[]{:S(2)}) copy-start(bf16[384,768]{1,0:T(8,128)(2,1)} %param.7) | copy-start | bytes 1769476
  17.4 9.4 %copy-start.1 = (bf16[768,384]{1,0:T(8,128)(2,1)}, bf16[768,384]{1,0:T(8,128)(2,1)S(1)}, u32[]{:S(2)}) copy-start(bf16[768,384]{1,0:T(8,128)(2,1)S(1)} %pad_maximum_fusion.2.refs_0_) | copy-start | bytes 1769476
  17.4 50.6 %collective-permute-start.13 = (bf16[768,384]{1,0:T(8,128)(2,1)S(1)}, bf16[768,384]{1,0:T(8,128)(2,1)S(1)}, u32[]{:S(2)}, u32[]{:S(2)}) collective-permute-start(bf16[768,384]{1,0:T(8,128)(2,1)S(1)} %pad_maximum_fusion.2.refs_0_), channel_id=1, source_target_pairs={{8,0},{16,8},{24,16},{9,1},{17,9},{25,17},{10,2},{18,10},{26,18},{... | collective-permute-start | bytes 1769480 | tf_op jit(solution)/shard_map/ppermute | solution.py:100
  19.4 27.0 %collective-permute-start.10 = (bf16[768,384]{1,0:T(8,128)(2,1)S(1)}, bf16[768,384]{1,0:T(8,128)(2,1)S(1)}, u32[]{:S(2)}, u32[]{:S(2)}) collective-permute-start(bf16[768,384]{1,0:T(8,128)(2,1)S(1)} %pad_maximum_fusion.2.refs_0_), channel_id=1, source_target_pairs={{0,4},{4,0},{1,5},{5,1},{2,6},{6,2},{3,7},{7,3},{8,12},{12,8},{9,1... | collective-permute-start | bytes 1769480 | tf_op jit(solution)/shard_map/ppermute | solution.py:105
  26.7 44.7 %collective-permute-start.11 = (bf16[768,384]{1,0:T(8,128)(2,1)S(1)}, bf16[768,384]{1,0:T(8,128)(2,1)S(1)}, u32[]{:S(2)}, u32[]{:S(2)}) collective-permute-start(bf16[768,384]{1,0:T(8,128)(2,1)S(1)} %pad_maximum_fusion.2.refs_0_), channel_id=1, source_target_pairs={{0,8},{8,16},{16,24},{1,9},{9,17},{17,25},{2,10},{10,18},{18,26},{... | collective-permute-start | bytes 1769480 | tf_op jit(solution)/shard_map/ppermute | solution.py:100
  31.3 6.2 %collective-permute-start.2 = (s32[1]{0:T(128)}, s32[1]{0:T(128)}, u32[]{:S(2)}, u32[]{:S(2)}) collective-permute-start(s32[1]{0:T(128)} %collective-permute-done), channel_id=1, source_target_pairs={{0,8},{8,16},{16,24},{1,9},{9,17},{17,25},{2,10},{10,18},{18,26},{... | collective-permute-start | bytes 20 | tf_op jit(solution)/shard_map/ppermute | solution.py:100
  37.5 37.7 %collective-permute-start.5 = (bf16[768,384]{1,0:T(8,128)(2,1)}, bf16[768,384]{1,0:T(8,128)(2,1)}, u32[]{:S(2)}, u32[]{:S(2)}) collective-permute-start(bf16[768,384]{1,0:T(8,128)(2,1)} %pad_maximum_fusion.1.refs_0_), channel_id=1, source_target_pairs={{0,4},{4,0},{1,5},{5,1},{2,6},{6,2},{3,7},{7,3},{8,12},{12,8},{9,1... | collective-permute-start | bytes 1769480 | tf_op jit(solution)/shard_map/ppermute | solution.py:105
  39.4 6.3 %collective-permute-start.4 = (s32[1]{0:T(128)}, s32[1]{0:T(128)}, u32[]{:S(2)}, u32[]{:S(2)}) collective-permute-start(s32[1]{0:T(128)} %collective-permute-done), channel_id=1, source_target_pairs={{8,0},{16,8},{24,16},{9,1},{17,9},{25,17},{10,2},{18,10},{26,18},{... | collective-permute-start | bytes 20 | tf_op jit(solution)/shard_map/ppermute | solution.py:100
  46.4 20.8 %copy-start.14 = (bf16[768,384]{1,0:T(8,128)(2,1)}, bf16[768,384]{1,0:T(8,128)(2,1)S(1)}, u32[]{:S(2)}) copy-start(bf16[768,384]{1,0:T(8,128)(2,1)S(1)} %collective-permute-done.10.refs_1_) | copy-start | bytes 1769476
  46.4 31.0 %collective-permute-start.14 = (bf16[768,384]{1,0:T(8,128)(2,1)S(1)}, bf16[768,384]{1,0:T(8,128)(2,1)S(1)}, u32[]{:S(2)}, u32[]{:S(2)}) collective-permute-start(bf16[768,384]{1,0:T(8,128)(2,1)S(1)} %collective-permute-done.10.refs_1_), channel_id=1, source_target_pairs={{8,0},{16,8},{24,16},{9,1},{17,9},{25,17},{10,2},{18,10},{26,18},{... | collective-permute-start | bytes 1769480 | tf_op jit(solution)/shard_map/ppermute | solution.py:100
  48.4 33.5 %collective-permute-start.12 = (bf16[768,384]{1,0:T(8,128)(2,1)S(1)}, bf16[768,384]{1,0:T(8,128)(2,1)S(1)}, u32[]{:S(2)}, u32[]{:S(2)}) collective-permute-start(bf16[768,384]{1,0:T(8,128)(2,1)S(1)} %collective-permute-done.10.refs_1_), channel_id=1, source_target_pairs={{0,8},{8,16},{16,24},{1,9},{9,17},{17,25},{2,10},{10,18},{18,26},{... | collective-permute-start | bytes 1769480 | tf_op jit(solution)/shard_map/ppermute | solution.py:100
  67.2 15.5 %copy-start.2 = (bf16[768,384]{1,0:T(8,128)(2,1)S(1)}, bf16[768,384]{1,0:T(8,128)(2,1)}, u32[]{:S(2)}) copy-start(bf16[768,384]{1,0:T(8,128)(2,1)} %copy-done.1) | copy-start | bytes 1769476
  67.2 15.5 %copy-start.8 = (bf16[384,384]{1,0:T(8,128)(2,1)S(1)}, bf16[384,384]{1,0:T(8,128)(2,1)}, u32[]{:S(2)}) copy-start(bf16[384,384]{1,0:T(8,128)(2,1)} %get-tuple-element.33.query_ref) | copy-start | bytes 884740
  68.9 53.5 %collective-permute-start.8 = (bf16[768,384]{1,0:T(8,128)(2,1)}, bf16[768,384]{1,0:T(8,128)(2,1)}, u32[]{:S(2)}, u32[]{:S(2)}) collective-permute-start(bf16[768,384]{1,0:T(8,128)(2,1)} %pad_maximum_fusion.1.refs_0_), channel_id=1, source_target_pairs={{8,0},{16,8},{24,16},{9,1},{17,9},{25,17},{10,2},{18,10},{26,18},{... | collective-permute-start | bytes 1769480 | tf_op jit(solution)/shard_map/ppermute | solution.py:100
  72.3 50.1 %collective-permute-start.6 = (bf16[768,384]{1,0:T(8,128)(2,1)}, bf16[768,384]{1,0:T(8,128)(2,1)}, u32[]{:S(2)}, u32[]{:S(2)}) collective-permute-start(bf16[768,384]{1,0:T(8,128)(2,1)} %pad_maximum_fusion.1.refs_0_), channel_id=1, source_target_pairs={{0,8},{8,16},{16,24},{1,9},{9,17},{17,25},{2,10},{10,18},{18,26},{... | collective-permute-start | bytes 1769480 | tf_op jit(solution)/shard_map/ppermute | solution.py:100
  75.3 47.1 %collective-permute-start.9 = (bf16[768,384]{1,0:T(8,128)(2,1)}, bf16[768,384]{1,0:T(8,128)(2,1)}, u32[]{:S(2)}, u32[]{:S(2)}) collective-permute-start(bf16[768,384]{1,0:T(8,128)(2,1)} %collective-permute-done.5.refs_1_), channel_id=1, source_target_pairs={{8,0},{16,8},{24,16},{9,1},{17,9},{25,17},{10,2},{18,10},{26,18},{... | collective-permute-start | bytes 1769480 | tf_op jit(solution)/shard_map/ppermute | solution.py:100
  78.2 44.1 %collective-permute-start.7 = (bf16[768,384]{1,0:T(8,128)(2,1)}, bf16[768,384]{1,0:T(8,128)(2,1)}, u32[]{:S(2)}, u32[]{:S(2)}) collective-permute-start(bf16[768,384]{1,0:T(8,128)(2,1)} %collective-permute-done.5.refs_1_), channel_id=1, source_target_pairs={{0,8},{8,16},{16,24},{1,9},{9,17},{17,25},{2,10},{10,18},{18,26},{... | collective-permute-start | bytes 1769480 | tf_op jit(solution)/shard_map/ppermute | solution.py:100
  82.7 1.1 copy-start.13
  83.7 1.1 copy-start.15
  84.8 1.1 copy-start.17
  85.9 1.1 copy-start.19
  86.9 1.1 copy-start.21
  119.0 3.4 %copy-start.7 = (bf16[384,384]{1,0:T(8,128)(2,1)S(1)}, bf16[384,384]{1,0:T(8,128)(2,1)}, u32[]{:S(2)}) copy-start(bf16[384,384]{1,0:T(8,128)(2,1)} %get-tuple-element.32.query_ref) | copy-start | bytes 884740
  119.0 3.4 %copy-start.10 = (bf16[384,384]{1,0:T(8,128)(2,1)S(1)}, bf16[384,384]{1,0:T(8,128)(2,1)}, u32[]{:S(2)}) copy-start(bf16[384,384]{1,0:T(8,128)(2,1)} %get-tuple-element.30.grad_ref) | copy-start | bytes 884740
  122.3 35.4 %collective-permute-start.24 = (bf16[1536,384]{1,0:T(8,128)(2,1)}, bf16[1536,384]{1,0:T(8,128)(2,1)}, u32[]{:S(2)}, u32[]{:S(2)}) collective-permute-start(bf16[1536,384]{1,0:T(8,128)(2,1)} %convolution_convert_fusion), channel_id=1, source_target_pairs={{0,8},{8,0},{16,24},{24,16},{1,9},{9,1},{17,25},{25,17},{2,10},{10... | collective-permute-start | bytes 3538952 | tf_op jit(solution)/shard_map/ppermute | solution.py:105
  122.4 15.6 %copy-start.23 = (bf16[384,1536]{1,0:T(8,128)(2,1)S(1)}, bf16[384,1536]{1,0:T(8,128)(2,1)}, u32[]{:S(2)}) copy-start(bf16[384,1536]{1,0:T(8,128)(2,1)} %reshape.174) | copy-start | bytes 3538948
  138.0 4.7 %copy-start = (bf16[6,768,384]{2,1,0:T(8,128)(2,1)}, bf16[6,768,384]{2,1,0:T(8,128)(2,1)S(1)}, u32[]{:S(2)}) copy-start(bf16[6,768,384]{2,1,0:T(8,128)(2,1)S(1)} %get-tuple-element.12) | copy-start | bytes 10616836
  138.0 4.7 %copy-start.5 = (bf16[384,384]{1,0:T(8,128)(2,1)}, bf16[384,384]{1,0:T(8,128)(2,1)S(1)}, u32[]{:S(2)}) copy-start(bf16[384,384]{1,0:T(8,128)(2,1)S(1)} %get-tuple-element.14) | copy-start | bytes 884740
  138.0 4.7 %copy-start.11 = (bf16[384,384]{1,0:T(8,128)(2,1)}, bf16[384,384]{1,0:T(8,128)(2,1)S(1)}, u32[]{:S(2)}) copy-start(bf16[384,384]{1,0:T(8,128)(2,1)S(1)} %get-tuple-element.10) | copy-start | bytes 884740
  140.4 24.1 %collective-permute-start.21 = (bf16[1536,384]{1,0:T(8,128)(2,1)}, bf16[1536,384]{1,0:T(8,128)(2,1)}, u32[]{:S(2)}, u32[]{:S(2)}) collective-permute-start(bf16[1536,384]{1,0:T(8,128)(2,1)} %convolution_convert_fusion.1), channel_id=1, source_target_pairs={{0,8},{8,0},{16,24},{24,16},{1,9},{9,1},{17,25},{25,17},{2,10},{10... | collective-permute-start | bytes 3538952 | tf_op jit(solution)/shard_map/ppermute | solution.py:105
  142.6 25.4 %collective-permute-start.15 = (bf16[2,768,384]{2,1,0:T(8,128)(2,1)}, bf16[2,768,384]{2,1,0:T(8,128)(2,1)}, u32[]{:S(2)}, u32[]{:S(2)}) collective-permute-start(bf16[2,768,384]{2,1,0:T(8,128)(2,1)} %get-tuple-element.16), channel_id=1, source_target_pairs={{8,0},{16,8},{24,16},{9,1},{17,9},{25,17},{10,2},{18,10},{26,18},{... | collective-permute-start | bytes 3538952 | tf_op jit(solution)/shard_map/ppermute | solution.py:100
  144.6 24.3 %collective-permute-start.16 = (bf16[2,768,384]{2,1,0:T(8,128)(2,1)}, bf16[2,768,384]{2,1,0:T(8,128)(2,1)}, u32[]{:S(2)}, u32[]{:S(2)}) collective-permute-start(bf16[2,768,384]{2,1,0:T(8,128)(2,1)} %get-tuple-element.17), channel_id=1, source_target_pairs={{0,8},{8,16},{16,24},{1,9},{9,17},{17,25},{2,10},{10,18},{18,26},{... | collective-permute-start | bytes 3538952 | tf_op jit(solution)/shard_map/ppermute | solution.py:100
  153.7 7.9 %copy-start.4 = (bf16[384,384]{1,0:T(8,128)(2,1)S(1)}, bf16[384,384]{1,0:T(8,128)(2,1)}, u32[]{:S(2)}) copy-start(bf16[384,384]{1,0:T(8,128)(2,1)} %copy-done.3) | copy-start | bytes 884740
  153.8 19.6 %collective-permute-start.18 = (bf16[2,768,384]{2,1,0:T(8,128)(2,1)}, bf16[2,768,384]{2,1,0:T(8,128)(2,1)S(1)}, u32[]{:S(2)}, u32[]{:S(2)}) collective-permute-start(bf16[2,768,384]{2,1,0:T(8,128)(2,1)} %get-tuple-element.18), channel_id=1, source_target_pairs={{8,0},{16,8},{24,16},{9,1},{17,9},{25,17},{10,2},{18,10},{26,18},{... | collective-permute-start | bytes 3538952 | tf_op jit(solution)/shard_map/ppermute | solution.py:100
  157.7 17.1 %collective-permute-start.19 = (bf16[2,768,384]{2,1,0:T(8,128)(2,1)}, bf16[2,768,384]{2,1,0:T(8,128)(2,1)S(1)}, u32[]{:S(2)}, u32[]{:S(2)}) collective-permute-start(bf16[2,768,384]{2,1,0:T(8,128)(2,1)} %get-tuple-element.19), channel_id=1, source_target_pairs={{0,8},{8,16},{16,24},{1,9},{9,17},{17,25},{2,10},{10,18},{18,26},{... | collective-permute-start | bytes 3538952 | tf_op jit(solution)/shard_map/ppermute | solution.py:100
  161.6 4.1 %copy-start.22 = (bf16[384,1536]{1,0:T(8,128)(2,1)S(1)}, bf16[384,1536]{1,0:T(8,128)(2,1)}, u32[]{:S(2)}) copy-start(bf16[384,1536]{1,0:T(8,128)(2,1)} %reshape.173) | copy-start | bytes 3538948
  164.3 1.4 copy-start.6
  164.4 15.4 %collective-permute-start.25 = (bf16[2,1,384,384]{3,2,1,0:T(8,128)(2,1)S(1)}, bf16[2,1,384,384]{3,2,1,0:T(8,128)(2,1)S(1)}, u32[]{:S(2)}, u32[]{:S(2)}) collective-permute-start(bf16[2,1,384,384]{3,2,1,0:T(8,128)(2,1)S(1)} %fusion.5), channel_id=1, source_target_pairs={{0,4},{4,0},{1,5},{5,1},{2,6},{6,2},{3,7},{7,3},{8,12},{12,8},{9,1... | collective-permute-start | bytes 1769480 | tf_op jit(solution)/shard_map/ppermute | solution.py:105
  168.0 24.4 %collective-permute-start.22 = (bf16[2,1,384,384]{3,2,1,0:T(8,128)(2,1)S(1)}, bf16[2,1,384,384]{3,2,1,0:T(8,128)(2,1)S(1)}, u32[]{:S(2)}, u32[]{:S(2)}) collective-permute-start(bf16[2,1,384,384]{3,2,1,0:T(8,128)(2,1)S(1)} %fusion.4), channel_id=1, source_target_pairs={{0,4},{4,0},{1,5},{5,1},{2,6},{6,2},{3,7},{7,3},{8,12},{12,8},{9,1... | collective-permute-start | bytes 1769480 | tf_op jit(solution)/shard_map/ppermute | solution.py:105
  171.3 33.8 %collective-permute-start.17 = (bf16[768,384]{1,0:T(8,128)(2,1)S(1)}, bf16[768,384]{1,0:T(8,128)(2,1)S(1)}, u32[]{:S(2)}, u32[]{:S(2)}) collective-permute-start(bf16[768,384]{1,0:T(8,128)(2,1)S(1)} %fusion.6), channel_id=1, source_target_pairs={{0,4},{4,0},{1,5},{5,1},{2,6},{6,2},{3,7},{7,3},{8,12},{12,8},{9,1... | collective-permute-start | bytes 1769480 | tf_op jit(solution)/shard_map/ppermute | solution.py:105
  175.3 41.5 %collective-permute-start.20 = (bf16[768,384]{1,0:T(8,128)(2,1)S(1)}, bf16[768,384]{1,0:T(8,128)(2,1)S(1)}, u32[]{:S(2)}, u32[]{:S(2)}) collective-permute-start(bf16[768,384]{1,0:T(8,128)(2,1)S(1)} %fusion.7), channel_id=1, source_target_pairs={{0,4},{4,0},{1,5},{5,1},{2,6},{6,2},{3,7},{7,3},{8,12},{12,8},{9,1... | collective-permute-start | bytes 1769480 | tf_op jit(solution)/shard_map/ppermute | solution.py:105
  180.0 38.8 %collective-permute-start.26 = (bf16[1,1,384,384]{3,2,1,0:T(8,128)(2,1)S(1)}, bf16[1,1,384,384]{3,2,1,0:T(8,128)(2,1)S(1)}, u32[]{:S(2)}, u32[]{:S(2)}) collective-permute-start(bf16[1,1,384,384]{3,2,1,0:T(8,128)(2,1)S(1)} %dynamic-slice_convert_fusion), channel_id=1, source_target_pairs={{0,16},{8,24},{16,0},{24,8},{1,17},{9,25},{17,1},{25,9},{2,18},{10... | collective-permute-start | bytes 884744 | tf_op jit(solution)/shard_map/ppermute | solution.py:105
  192.6 26.2 %collective-permute-start.23 = (bf16[1,1,384,384]{3,2,1,0:T(8,128)(2,1)S(1)}, bf16[1,1,384,384]{3,2,1,0:T(8,128)(2,1)S(1)}, u32[]{:S(2)}, u32[]{:S(2)}) collective-permute-start(bf16[1,1,384,384]{3,2,1,0:T(8,128)(2,1)S(1)} %dynamic-slice_convert_fusion.1), channel_id=1, source_target_pairs={{0,16},{8,24},{16,0},{24,8},{1,17},{9,25},{17,1},{25,9},{2,18},{10... | collective-permute-start | bytes 884744 | tf_op jit(solution)/shard_map/ppermute | solution.py:105
  (6 other events, 4.7 us)
Sparse Core Ops, SparseCore 0:
  9.6 52.5 all-gather.1

commit v2 on v1

--- a/solution.py
+++ b/solution.py
@@ -15,14 +15,15 @@
 neg_large = -1e30
 
 
-def attention_kernel(slots, bias_ref, query_ref, grad_ref, *refs):
+nt = (((1,), (1,)), ((), ()))
+tn = (((0,), (0,)), ((), ()))
+scale = HDIM ** (-0.5)
+
+
+def forward_kernel(slots, bias_ref, query_ref, *refs):
     pair_refs = refs[:slots]
-    query_out, attended_out, pair_out, score_ref = refs[slots:]
-    scale = HDIM ** (-0.5)
-    nt = (((1,), (1,)), ((), ()))
-    tn = (((0,), (0,)), ((), ()))
+    attended_out, total_out, score_ref = refs[slots:]
     query = query_ref[...]
-    grad = grad_ref[...]
     row_max = None
     for slot in range(slots):
         scores = lax.dot_general(
@@ -37,29 +38,38 @@
         score_ref[slot] = raised
         part = jnp.sum(raised, axis=1, keepdims=True)
         total = part if total is None else total + part
+    total_out[...] = jnp.broadcast_to(row_max + jnp.log2(total), (TILE, HDIM))
     inverse = 1.0 / total
     attended = None
     for slot in range(slots):
-        weights = score_ref[slot] * inverse
-        score_ref[slot] = weights
-        low = weights.astype(jnp.bfloat16)
+        low = (score_ref[slot] * inverse).astype(jnp.bfloat16)
         part = jnp.dot(low, pair_refs[slot][TILE:], preferred_element_type=jnp.float32)
         attended = part if attended is None else attended + part
+    attended_out[...] = attended.astype(jnp.bfloat16)
+
+
+def backward_kernel(slots, bias_ref, query_ref, grad_ref, attended_ref, total_ref, *refs):
+    pair_refs = refs[:slots]
+    query_out, pair_out = refs[slots:]
+    query = query_ref[...]
+    grad = grad_ref[...]
+    log_total = total_ref[:, :1]
+    delta = jnp.sum(
+        grad.astype(jnp.float32) * attended_ref[...].astype(jnp.float32), axis=1, keepdims=True
+    )
+    query_sum = None
+    for slot in range(slots):
+        key, value = pair_refs[slot][:TILE], pair_refs[slot][TILE:]
+        scores = lax.dot_general(query, key, nt, preferred_element_type=jnp.float32) * (
+            scale * LOG2E
+        ) + bias_ref[slot]
+        weights = jnp.exp2(scores - log_total)
         pair_out[slot, TILE:] = lax.dot_general(
-            low, grad, tn, preferred_element_type=jnp.float32
+            weights.astype(jnp.bfloat16), grad, tn, preferred_element_type=jnp.float32
         ).astype(jnp.bfloat16)
-    attended = attended.astype(jnp.bfloat16)
-    attended_out[...] = attended
-    delta = jnp.sum(
-        grad.astype(jnp.float32) * attended.astype(jnp.float32), axis=1, keepdims=True
-    )
-    query_sum = None
-    for slot in range(slots):
-        grad_weights = lax.dot_general(
-            grad, pair_refs[slot][TILE:], nt, preferred_element_type=jnp.float32
-        )
-        grad_scores = (score_ref[slot] * (grad_weights - delta)).astype(jnp.bfloat16)
-        part = jnp.dot(grad_scores, pair_refs[slot][:TILE], preferred_element_type=jnp.float32)
+        grad_weights = lax.dot_general(grad, value, nt, preferred_element_type=jnp.float32)
+        grad_scores = (weights * (grad_weights - delta)).astype(jnp.bfloat16)
+        part = jnp.dot(grad_scores, key, preferred_element_type=jnp.float32)
         query_sum = part if query_sum is None else query_sum + part
         pair_out[slot, :TILE] = (
             lax.dot_general(grad_scores, query, tn, preferred_element_type=jnp.float32) * scale
@@ -67,31 +77,55 @@
     query_out[...] = (query_sum * scale).astype(jnp.bfloat16)
 
 
-def attention(bias, query, grad, pairs):
-    slots = len(pairs)
-    width = query.shape[1]
-    heads = width // HDIM
+def specs_of(slots):
     rows = pl.BlockSpec((TILE, HDIM), lambda h: (0, h))
     pair = pl.BlockSpec((2 * TILE, HDIM), lambda h: (0, h))
+    return pl.BlockSpec((slots, 1, TILE), lambda h: (0, 0, 0)), rows, [pair] * slots
+
+
+def forward(bias, query, pairs):
+    slots, width = len(pairs), query.shape[1]
+    heads = width // HDIM
+    bias_spec, rows, pair_specs = specs_of(slots)
     return pl.pallas_call(
-        functools.partial(attention_kernel, slots),
+        functools.partial(forward_kernel, slots),
         grid=(heads,),
-        in_specs=[pl.BlockSpec((slots, 1, TILE), lambda h: (0, 0, 0)), rows, rows]
-        + [pair] * slots,
-        out_specs=[rows, rows, pl.BlockSpec((slots, 2 * TILE, HDIM), lambda h: (0, 0, h))],
+        in_specs=[bias_spec, rows] + pair_specs,
+        out_specs=[rows, rows],
         out_shape=[
             jax.ShapeDtypeStruct((TILE, width), jnp.bfloat16),
+            jax.ShapeDtypeStruct((TILE, width), jnp.float32),
+        ],
+        scratch_shapes=[pltpu.VMEM((slots, TILE, TILE), jnp.float32)],
+        compiler_params=pltpu.CompilerParams(vmem_limit_bytes=32 * 2**20),
+        cost_estimate=pl.CostEstimate(
+            flops=heads * slots * 32 * TILE * TILE * HDIM,
+            bytes_accessed=heads * slots * 8 * TILE * HDIM,
+            transcendentals=heads * slots * TILE * TILE,
+        ),
+    )(bias, query, *pairs)
+
+
+def backward(bias, query, grad, attended, total, pairs):
+    slots, width = len(pairs), query.shape[1]
+    heads = width // HDIM
+    bias_spec, rows, pair_specs = specs_of(slots)
+    return pl.pallas_call(
+        functools.partial(backward_kernel, slots),
+        grid=(heads,),
+        in_specs=[bias_spec, rows, rows, rows, rows] + pair_specs,
+        out_specs=[rows, pl.BlockSpec((slots, 2 * TILE, HDIM), lambda h: (0, 0, h))],
+        out_shape=[
             jax.ShapeDtypeStruct((TILE, width), jnp.bfloat16),
             jax.ShapeDtypeStruct((slots, 2 * TILE, width), jnp.bfloat16),
         ],
-        scratch_shapes=[pltpu.VMEM((slots, TILE, TILE), jnp.float32)],
-        compiler_params=pltpu.CompilerParams(vmem_limit_bytes=40 * 2**20),
+        compiler_params=pltpu.CompilerParams(vmem_limit_bytes=32 * 2**20),
         cost_estimate=pl.CostEstimate(
-            flops=heads * slots * 20 * TILE * TILE * HDIM,
+            flops=heads * slots * 48 * TILE * TILE * HDIM,
             bytes_accessed=heads * slots * 8 * TILE * HDIM,
             transcendentals=heads * slots * TILE * TILE,
         ),
-    )(bias, query, grad, *pairs)
+    )(bias, query, grad, attended, total, *pairs)
 
 
 def moved(x, axis, by):
@@ -134,35 +168,37 @@
         )
 
     if time_size & (time_size - 1) or height_size & (height_size - 1) or time_size < 2:
-        return lax.psum_scatter(
+        return [], lax.psum_scatter(
             product(gathered).astype(jnp.bfloat16), ("tm", "height"),
             scatter_dimension=0, tiled=True,
         ).astype(jnp.float32)
-    width = attended.shape[1]
-    split = gathered.reshape(rows, time_size // 2, 2, height_size, block)
     bit = time_place % 2
 
-    def half(which):
-        part = lax.dynamic_index_in_dim(split, which, 2, keepdims=False)
-        return product(part)
-
-    sent = swapped(half(1 - bit).astype(jnp.bfloat16), "tm", 0)
-    held = (half(bit) + sent.astype(jnp.float32)).reshape(
-        time_size // 2, height_size, block, width
-    )
-    stages = [("height", number) for number in range(height_size.bit_length() - 1)]
-    stages += [("tm", number) for number in range(1, time_size.bit_length() - 1)]
-    for axis, number in stages:
-        place = height_place if axis == "height" else time_place
-        dim = 1 if axis == "height" else 0
-        bit = (place // (1 << number)) % 2
-        shape = held.shape
-        wide = held.reshape(shape[:dim] + (shape[dim] // 2, 2) + shape[dim + 1 :])
-        sent = lax.dynamic_index_in_dim(wide, 1 - bit, dim + 1, keepdims=False)
-        kept = lax.dynamic_index_in_dim(wide, bit, dim + 1, keepdims=False)
-        got = swapped(sent.astype(jnp.bfloat16), axis, number)
-        held = kept + got.astype(jnp.float32)
-    return held.reshape(block, width)
+    def product_of(high, which):
+        start = (2 * high + which) * height_size * block
+        return product(lax.dynamic_slice_in_dim(gathered, start, height_size * block, 1))
+
+    highs = range(time_size // 2)
+    first = [product_of(high, 1 - bit).astype(jnp.bfloat16) for high in highs]
+    kept = [product_of(high, bit) for high in highs]
+    got = [swapped(x, "tm", 0) for x in first]
+    held = [k + g.astype(jnp.float32) for k, g in zip(kept, got)]
+    for number in range(height_size.bit_length() - 1):
+        bit = (height_place // (1 << number)) % 2
+        count = held[0].shape[0] // (2 * block)
+        wide = [x.reshape(count, 2, block, -1) for x in held]
+        sent = [lax.dynamic_index_in_dim(x, 1 - bit, 1, keepdims=False) for x in wide]
+        kept = [lax.dynamic_index_in_dim(x, bit, 1, keepdims=False) for x in wide]
+        got = [swapped(x.astype(jnp.bfloat16), "height", number) for x in sent]
+        held = [(k + g.astype(jnp.float32)).reshape(count * block, -1) for k, g in zip(kept, got)]
+    for number in range(1, time_size.bit_length() - 1):
+        bit = (time_place // (1 << number)) % 2
+        low, high = held[0::2], held[1::2]
+        sent = [jnp.where(bit == 0, y, x) for x, y in zip(low, high)]
+        kept = [jnp.where(bit == 0, x, y) for x, y in zip(low, high)]
+        got = [swapped(x.astype(jnp.bfloat16), "tm", number) for x in sent]
+        held = [k + g.astype(jnp.float32) for k, g in zip(kept, got)]
+    return first, held[0]
 
 
 def on_device(queries, keys, values, out_grad, out_weight, window, counts):
@@ -215,11 +251,16 @@
         jnp.bfloat16
     )
     token_share = (row_count * time_size * height_size) ** (-0.5)
+    per = len(steps)
+    ahead_of = [forward(bias, columns(queries, c), packs[c]) for c in range(chunks)]
+    attended_all = jnp.concatenate([x[0] for x in ahead_of], axis=1)
+    first, weight_out = reduce_scattered(full_grad, attended_all)
+    grad_out, first = lax.optimization_barrier((grad_out, first))
     outs = []
-    per = len(steps)
     for chunk in range(chunks):
-        query_out, attended, pair_out = attention(
-            bias, columns(queries, chunk), columns(grad_out, chunk), packs[chunk]
+        attended, total = ahead_of[chunk]
+        query_out, pair_out = backward(
+            bias, columns(queries, chunk), columns(grad_out, chunk), attended, total, packs[chunk]
         )
         back = moved(pair_out[per : 2 * per], "tm", -1).astype(jnp.float32)
         ahead = moved(pair_out[2 * per :], "tm", 1).astype(jnp.float32)
@@ -228,9 +269,9 @@
         for place, (_, give) in enumerate(sends):
             final = final + give(own[1 + place].astype(jnp.bfloat16)).astype(jnp.float32)
         final = final.astype(jnp.bfloat16)
-        weight_out = reduce_scattered(full_grad, attended) * token_share
-        outs.append((query_out, final[:TILE], final[TILE:], weight_out))
-    return tuple(jnp.concatenate([out[i] for out in outs], axis=1) for i in range(4))
+        outs.append((query_out, final[:TILE], final[TILE:]))
+    joined = tuple(jnp.concatenate([out[i] for out in outs], axis=1) for i in range(3))
+    return joined + (weight_out * token_share,)
 
 
 def solution(mesh):

time: 228 us -> 195 us (0.86)
  local copies, waits for them, and re-layouts: 36.5 us -> 8.56 us
  Pallas kernels: 30.1 us -> 42.5 us
  waiting for transfers between devices: 60.5 us -> 52 us
  other arithmetic: 12.3 us -> 8.64 us
  matrix products: 15.6 us -> 12.3 us
    reshape x3 -> x0, local copies, waits for them, and re-layouts: 14.2 us -> none  [the longest x2 7.65 us: product(): part.reshape(rows, -1)]
    pallas_call x2 -> x4, Pallas kernels: 30.1 us -> 42.5 us  [the longest x2 28.8 us: backward(): pl.pallas_call(functools.partial(backward_kernel, slots), grid=(heads,),...]
    all_gather x1, waiting for transfers between devices: 10.1 us -> 0.01 us  [on_device(): full_grad = lax.all_gather(out_grad, 'head', axis=1, tiled=True)]
    unnamed x52 -> x37, local copies, waits for them, and re-layouts: 10 us -> 4.77 us
    dynamic_slice x1 -> x0, local copies, waits for them, and re-layouts: 4.66 us -> none  [half(): part = lax.dynamic_index_in_dim(split, which, 2, keepdims=False)]
    slice x2, local copies, waits for them, and re-layouts: 3.47 us -> 0.48 us  [on_device(): back = moved(pair_out[per:2 * per], 'tm', -1).astype(jnp.float32)]
    dot_general x4, matrix products: 10.6 us -> 7.87 us  [product(): lax.dot_general(part.reshape(rows, -1), attended, (((0,), (0,)), ((), ())...]
    concatenate x4 -> x3, other arithmetic: 4.76 us -> 2.59 us  [on_device(): jnp.concatenate([out[i] for out in outs], axis=1)]
  transfers between devices with their start and end apart: 28 -> 27, of which waited for: 9 -> 8; matrix products, arithmetic and copies ran while one was open for 23% -> 11% of each run, Pallas kernels for 13% -> 22%
where the time goes in v2:
time: 195 us
  waiting for transfers between devices  52 us (27%)
  starting transfers between devices  51.1 us (26%)
  Pallas kernels  42.5 us (22%)
  between operations  19.3 us (10%)
  matrix products  12.3 us (6%)
  other arithmetic  8.64 us (4%)
  local copies, waits for them, and re-layouts  8.56 us (4%)
    ppermute x16, starting transfers between devices, moved(): return lax.ppermute(x, axis, pairs)  44.7 us
    ppermute x10, waiting for transfers between devices, swapped(): return lax.ppermute(x, axis, [(i, i ^ 1 << bit) for i in range(size)])  41.6 us
    pallas_call x2, Pallas kernels, backward(): pl.pallas_call(functools.partial(backward_kernel, slots), grid=(heads,),...  28.8 us
    pallas_call x2, Pallas kernels, forward(): pl.pallas_call(functools.partial(forward_kernel, slots), grid=(heads,), i...  13.8 us
    ppermute x16, waiting for transfers between devices, moved(): return lax.ppermute(x, axis, pairs)  10.3 us
    dot_general x4, matrix products, product(): lax.dot_general(part.reshape(rows, -1), attended, (((0,), (0,)), ((), ())...  7.87 us
    ppermute x10, starting transfers between devices, swapped(): return lax.ppermute(x, axis, [(i, i ^ 1 << bit) for i in range(size)])  6.4 us
    unnamed x37, local copies, waits for them, and re-layouts  4.77 us
  transfers between devices with their start and end apart: 27, of which 8 were waited for; matrix products, arithmetic and copies ran while one was open for 11% of the time, Pallas kernels for 22%

profile of v2, /device:TPU:1, one launch (start us, length us, event | category | flops | bytes accessed | tf_op | source)
XLA Modules:
  0.0 194.5 jit_solution(4609231420460440190)
XLA Ops:
  7.2 1.4 fusion.23
  8.7 2.1 %collective-permute-start.5 = (bf16[768,384]{1,0:T(8,128)(2,1)S(1)}, bf16[768,384]{1,0:T(8,128)(2,1)S(1)}, u32[]{:S(2)}, u32[]{:S(2)}) collective-permute-start(bf16[768,384]{1,0:T(8,128)(2,1)S(1)} %pad_maximum_fusion.refs_0_), channel_id=1, source_target_pairs={{0,4},{4,0},{1,5},{5,1},{2,6},{6,2},{3,7},{7,3},{8,12},{12,8},{9,1... | collective-permute-start | bytes 1769480 | tf_op jit(solution)/shard_map/ppermute | solution.py:139
  10.9 2.9 %collective-permute-start.3 = (s32[1]{0:T(128)}, s32[1]{0:T(128)}, u32[]{:S(2)}, u32[]{:S(2)}) collective-permute-start(s32[1]{0:T(128)} %param.13), channel_id=1, source_target_pairs={{8,0},{16,8},{24,16},{9,1},{17,9},{25,17},{10,2},{18,10},{26,18},{... | collective-permute-start | bytes 20 | tf_op jit(solution)/shard_map/ppermute | solution.py:134
  13.7 3.6 %collective-permute-start.1 = (s32[1]{0:T(128)}, s32[1]{0:T(128)}, u32[]{:S(2)}, u32[]{:S(2)}) collective-permute-start(s32[1]{0:T(128)} %param.13), channel_id=1, source_target_pairs={{0,8},{8,16},{16,24},{1,9},{9,17},{17,25},{2,10},{10,18},{18,26},{... | collective-permute-start | bytes 20 | tf_op jit(solution)/shard_map/ppermute | solution.py:134
  17.3 1.9 collective-permute-start.8
  21.4 2.5 %collective-permute-done = s32[1]{0:T(128)} collective-permute-done((s32[1]{0:T(128)}, s32[1]{0:T(128)}, u32[]{:S(2)}, u32[]{:S(2)}) %collective-permute-start) | collective-permute-done | bytes 36 | tf_op jit(solution)/shard_map/ppermute | solution.py:139
  23.9 4.6 %collective-permute-start.6 = (bf16[768,384]{1,0:T(8,128)(2,1)S(1)}, bf16[768,384]{1,0:T(8,128)(2,1)S(1)}, u32[]{:S(2)}, u32[]{:S(2)}) collective-permute-start(bf16[768,384]{1,0:T(8,128)(2,1)S(1)} %pad_maximum_fusion.refs_0_), channel_id=1, source_target_pairs={{0,8},{8,16},{16,24},{1,9},{9,17},{17,25},{2,10},{10,18},{18,26},{... | collective-permute-start | bytes 1769480 | tf_op jit(solution)/shard_map/ppermute | solution.py:134
  28.5 1.3 collective-permute-start.10
  29.8 1.9 collective-permute-start.4
  31.7 3.5 %collective-permute-done.4 = s32[1]{0:T(128)} collective-permute-done((s32[1]{0:T(128)}, s32[1]{0:T(128)}, u32[]{:S(2)}, u32[]{:S(2)}) %collective-permute-start.4) | collective-permute-done | bytes 36 | tf_op jit(solution)/shard_map/ppermute | solution.py:134
  35.2 1.9 collective-permute-start.2
  37.2 3.0 %collective-permute-start.9 = (bf16[768,384]{1,0:T(8,128)(2,1)S(1)}, bf16[768,384]{1,0:T(8,128)(2,1)}, u32[]{:S(2)}, u32[]{:S(2)}) collective-permute-start(bf16[768,384]{1,0:T(8,128)(2,1)S(1)} %collective-permute-done.5.refs_1_), channel_id=1, source_target_pairs={{8,0},{16,8},{24,16},{9,1},{17,9},{25,17},{10,2},{18,10},{26,18},{... | collective-permute-start | bytes 1769480 | tf_op jit(solution)/shard_map/ppermute | solution.py:134
  40.1 2.6 %collective-permute-start.7 = (bf16[768,384]{1,0:T(8,128)(2,1)S(1)}, bf16[768,384]{1,0:T(8,128)(2,1)}, u32[]{:S(2)}, u32[]{:S(2)}) collective-permute-start(bf16[768,384]{1,0:T(8,128)(2,1)S(1)} %collective-permute-done.5.refs_1_), channel_id=1, source_target_pairs={{0,8},{8,16},{16,24},{1,9},{9,17},{17,25},{2,10},{10,18},{18,26},{... | collective-permute-start | bytes 1769480 | tf_op jit(solution)/shard_map/ppermute | solution.py:134
  48.7 0.7 constant_dynamic-update-slice_fusion.bias_ref
  49.4 2.5 %collective-permute-start.13 = (bf16[768,384]{1,0:T(8,128)(2,1)S(1)}, bf16[768,384]{1,0:T(8,128)(2,1)S(1)}, u32[]{:S(2)}, u32[]{:S(2)}) collective-permute-start(bf16[768,384]{1,0:T(8,128)(2,1)S(1)} %pad_maximum_fusion.1.refs_0_), channel_id=1, source_target_pairs={{8,0},{16,8},{24,16},{9,1},{17,9},{25,17},{10,2},{18,10},{26,18},{... | collective-permute-start | bytes 1769480 | tf_op jit(solution)/shard_map/ppermute | solution.py:134
  51.9 0.8 copy-done
  52.7 3.1 %collective-permute-start.11 = (bf16[768,384]{1,0:T(8,128)(2,1)S(1)}, bf16[768,384]{1,0:T(8,128)(2,1)S(1)}, u32[]{:S(2)}, u32[]{:S(2)}) collective-permute-start(bf16[768,384]{1,0:T(8,128)(2,1)S(1)} %pad_maximum_fusion.1.refs_0_), channel_id=1, source_target_pairs={{0,8},{8,16},{16,24},{1,9},{9,17},{17,25},{2,10},{10,18},{18,26},{... | collective-permute-start | bytes 1769480 | tf_op jit(solution)/shard_map/ppermute | solution.py:134
  55.8 1.9 collective-permute-start.14
  57.7 3.6 %collective-permute-start.12 = (bf16[768,384]{1,0:T(8,128)(2,1)}, bf16[768,384]{1,0:T(8,128)(2,1)S(1)}, u32[]{:S(2)}, u32[]{:S(2)}) collective-permute-start(bf16[768,384]{1,0:T(8,128)(2,1)} %collective-permute-done.10.refs_1_), channel_id=1, source_target_pairs={{0,8},{8,16},{16,24},{1,9},{9,17},{17,25},{2,10},{10,18},{18,26},{... | collective-permute-start | bytes 1769480 | tf_op jit(solution)/shard_map/ppermute | solution.py:134
  61.4 1.1 copy-done.1
  62.5 6.8 %shard_map.102 = (bf16[384,384]{1,0:T(8,128)(2,1)S(1)}, f32[384,384]{1,0:T(8,128)S(1)}) custom-call(f32[6,1,384]{2,1,0:T(1,128)S(1)} %constant_dynamic-update-slice_fusion.bias_ref, bf16[384,384]{1,0:T(8,128)(2,1)S(1)} %get-tuple-element.36.query_ref, bf16[768,384]{1,0:T(8,128)(2,1)S(1)} %pad_maximum_fusion.refs_0_, ...), custom_call_target="tpu_custom_call" | custom-call | flops 10871635968 | bytes 7077888 | tf_op jit(solution)/shard_map/pallas_call | solution.py:90
  69.3 0.8 constant_dynamic-update-slice_fusion.7
  70.3 6.9 %shard_map.103 = (bf16[384,384]{1,0:T(8,128)(2,1)S(1)}, f32[384,384]{1,0:T(8,128)S(1)}) custom-call(f32[6,1,384]{2,1,0:T(1,128)S(1)} %constant_dynamic-update-slice_fusion.bias_ref, bf16[384,384]{1,0:T(8,128)(2,1)S(1)} %get-tuple-element.37.query_ref, bf16[768,384]{1,0:T(8,128)(2,1)S(1)} %pad_maximum_fusion.1.refs_0_, ...), custom_call_target="tpu_custom_call" | custom-call | flops 10871635968 | bytes 7077888 | tf_op jit(solution)/shard_map/pallas_call | solution.py:90
  77.3 0.8 copy-done.13
  78.1 0.8 constant_dynamic-update-slice_fusion.6
  78.8 2.2 %convolution_convert_fusion.1 = bf16[768,768]{1,0:T(8,128)(2,1)S(1)} fusion(bf16[384,768]{1,0:T(8,128)(2,1)} %constant_dynamic-update-slice_fusion.6, bf16[384,3072]{1,0:T(8,128)(2,1)} %all-gather.2.cloned.1.call-done, s32[]{:T(128)S(6)} %select_n.141), kind=kOutput, calls=%fused_computation.5 | convolution fusion | flops 453574656 | bytes 2359300 | tf_op jit(solution)/shard_map/dot_general | solution.py:165
  81.1 1.9 convolution_convert_fusion
  83.6 4.5 %convolution_convert_fusion.2 = bf16[384,768]{1,0:T(8,128)(2,1)S(1)} fusion(bf16[384,3072]{1,0:T(8,128)(2,1)S(1)} %copy-done.15, bf16[3072,768]{1,0:T(8,128)(2,1)} %param.11), kind=kOutput, calls=%fused_computation.6 | convolution fusion | flops 1812234240 | bytes 7667712 | tf_op jit(solution)/shard_map/dot_general | solution.py:250
  88.2 0.9 copy-done.4
  89.3 14.3 %shard_map.105 = (bf16[384,384]{1,0:T(8,128)(2,1)S(1)}, bf16[6,768,384]{2,1,0:T(8,128)(2,1)S(1)}) custom-call(f32[6,1,384]{2,1,0:T(1,128)S(1)} %constant_dynamic-update-slice_fusion.bias_ref, bf16[384,384]{1,0:T(8,128)(2,1)S(1)} %get-tuple-element.37.query_ref, bf16[384,384]{1,0:T(8,128)(2,1)S(1)} %get-tuple-element.31.grad_ref, ...), custom_call_target="tpu_custom_call" | custom-call | flops 16307453952 | bytes 7077888 | tf_op jit(solution)/shard_map/pallas_call | solution.py:113
  103.9 2.1 %collective-permute-start.18 = (bf16[2,768,384]{2,1,0:T(8,128)(2,1)S(1)}, bf16[2,768,384]{2,1,0:T(8,128)(2,1)S(1)}, u32[]{:S(2)}, u32[]{:S(2)}) collective-permute-start(bf16[2,768,384]{2,1,0:T(8,128)(2,1)S(1)} %get-tuple-element.24), channel_id=1, source_target_pairs={{8,0},{16,8},{24,16},{9,1},{17,9},{25,17},{10,2},{18,10},{26,18},{... | collective-permute-start | bytes 3538952 | tf_op jit(solution)/shard_map/ppermute | solution.py:134
  106.0 3.6 %collective-permute-start.19 = (bf16[2,768,384]{2,1,0:T(8,128)(2,1)S(1)}, bf16[2,768,384]{2,1,0:T(8,128)(2,1)S(1)}, u32[]{:S(2)}, u32[]{:S(2)}) collective-permute-start(bf16[2,768,384]{2,1,0:T(8,128)(2,1)S(1)} %get-tuple-element.25), channel_id=1, source_target_pairs={{0,8},{8,16},{16,24},{1,9},{9,17},{17,25},{2,10},{10,18},{18,26},{... | collective-permute-start | bytes 3538952 | tf_op jit(solution)/shard_map/ppermute | solution.py:134
  109.6 14.5 %shard_map.104 = (bf16[384,384]{1,0:T(8,128)(2,1)S(1)}, bf16[6,768,384]{2,1,0:T(8,128)(2,1)S(1)}) custom-call(f32[6,1,384]{2,1,0:T(1,128)S(1)} %constant_dynamic-update-slice_fusion.bias_ref, bf16[384,384]{1,0:T(8,128)(2,1)S(1)} %get-tuple-element.36.query_ref, bf16[384,384]{1,0:T(8,128)(2,1)S(1)} %get-tuple-element.30.grad_ref, ...), custom_call_target="tpu_custom_call" | custom-call | flops 16307453952 | bytes 7077888 | tf_op jit(solution)/shard_map/pallas_call | solution.py:113
  124.4 1.9 collective-permute-start.15
  126.3 3.6 %collective-permute-start.16 = (bf16[2,768,384]{2,1,0:T(8,128)(2,1)S(1)}, bf16[2,768,384]{2,1,0:T(8,128)(2,1)S(1)}, u32[]{:S(2)}, u32[]{:S(2)}) collective-permute-start(bf16[2,768,384]{2,1,0:T(8,128)(2,1)S(1)} %get-tuple-element.23), channel_id=1, source_target_pairs={{0,8},{8,16},{16,24},{1,9},{9,17},{17,25},{2,10},{10,18},{18,26},{... | collective-permute-start | bytes 3538952 | tf_op jit(solution)/shard_map/ppermute | solution.py:134
  129.9 1.9 convert_add_fusion.1
  132.3 1.9 convert_add_fusion
  134.3 1.3 collective-permute-start.24
  136.3 5.9 %collective-permute-done.15 = bf16[2,768,384]{2,1,0:T(8,128)(2,1)S(1)} collective-permute-done((bf16[2,768,384]{2,1,0:T(8,128)(2,1)S(1)}, bf16[2,768,384]{2,1,0:T(8,128)(2,1)S(1)}, u32[]{:S(2)}, u32[]{:S(2)}) %collective-permute-start.15) | collective-permute-done | bytes 1179680 | tf_op jit(solution)/shard_map/ppermute | solution.py:134
  142.2 0.9 collective-permute-done.16
  143.9 0.9 pad_maximum_fusion.2
  144.7 2.6 %collective-permute-done.22 = bf16[1,384,768]{2,1,0:T(8,128)(2,1)S(1)} collective-permute-done((bf16[1,384,768]{2,1,0:T(8,128)(2,1)S(1)}, bf16[1,384,768]{2,1,0:T(8,128)(2,1)S(1)}, u32[]{:S(2)}, u32[]{:S(2)}) %collective-permute-start.22) | collective-permute-done | bytes 589856 | tf_op jit(solution)/shard_map/ppermute | solution.py:139
  147.3 12.6 %collective-permute-done.24 = bf16[1,384,768]{2,1,0:T(8,128)(2,1)S(1)} collective-permute-done((bf16[1,384,768]{2,1,0:T(8,128)(2,1)S(1)}, bf16[1,384,768]{2,1,0:T(8,128)(2,1)S(1)}, u32[]{:S(2)}, u32[]{:S(2)}) %collective-permute-start.24) | collective-permute-done | bytes 589856 | tf_op jit(solution)/shard_map/ppermute | solution.py:139
  160.3 12.3 %collective-permute-done.20 = bf16[768,384]{1,0:T(8,128)(2,1)S(1)} collective-permute-done((bf16[768,384]{1,0:T(8,128)(2,1)S(1)}, bf16[768,384]{1,0:T(8,128)(2,1)S(1)}, u32[]{:S(2)}, u32[]{:S(2)}) %collective-permute-start.20) | collective-permute-done | bytes 589856 | tf_op jit(solution)/shard_map/ppermute | solution.py:139
  172.7 11.5 %collective-permute-done.17 = bf16[768,384]{1,0:T(8,128)(2,1)S(1)} collective-permute-done((bf16[768,384]{1,0:T(8,128)(2,1)S(1)}, bf16[768,384]{1,0:T(8,128)(2,1)S(1)}, u32[]{:S(2)}, u32[]{:S(2)}) %collective-permute-start.17) | collective-permute-done | bytes 589856 | tf_op jit(solution)/shard_map/ppermute | solution.py:139
  184.6 0.9 pad_maximum_fusion.4
  185.4 0.9 pad_maximum_fusion.3
  186.3 1.4 fusion.4
  (83 shorter events, 7.8 us)
Async XLA Ops:
  7.2 71.7 %all-gather.2.cloned.1.call-start = ((), (), s32[]{:S(2)}) async-start(), calls=%async_computation | async-start | bytes 2949120 | tf_op jit(solution)/shard_map/all_gather | solution.py:213
  8.6 11.3 %copy-start.17 = (s32[1,27]{1,0:T(1,128)S(1)}, s32[1,27]{1,0:T(1,128)}, u32[]{:S(2)}) copy-start(s32[1,27]{1,0:T(1,128)} %param.12) | copy-start | bytes 328
  8.6 12.7 %copy-start.16 = (bf16[384,768]{1,0:T(8,128)(2,1)S(1)}, bf16[384,768]{1,0:T(8,128)(2,1)}, u32[]{:S(2)}) copy-start(bf16[384,768]{1,0:T(8,128)(2,1)} %param.7) | copy-start | bytes 1769476
  8.7 28.5 %collective-permute-start.5 = (bf16[768,384]{1,0:T(8,128)(2,1)S(1)}, bf16[768,384]{1,0:T(8,128)(2,1)S(1)}, u32[]{:S(2)}, u32[]{:S(2)}) collective-permute-start(bf16[768,384]{1,0:T(8,128)(2,1)S(1)} %pad_maximum_fusion.refs_0_), channel_id=1, source_target_pairs={{0,4},{4,0},{1,5},{5,1},{2,6},{6,2},{3,7},{7,3},{8,12},{12,8},{9,1... | collective-permute-start | bytes 1769480 | tf_op jit(solution)/shard_map/ppermute | solution.py:139
  10.8 13.1 %collective-permute-start = (s32[1]{0:T(128)}, s32[1]{0:T(128)}, u32[]{:S(2)}, u32[]{:S(2)}) collective-permute-start(s32[1]{0:T(128)} %param.13), channel_id=1, source_target_pairs={{0,4},{4,0},{1,5},{5,1},{2,6},{6,2},{3,7},{7,3},{8,12},{12,8},{9,1... | collective-permute-start | bytes 20 | tf_op jit(solution)/shard_map/ppermute | solution.py:139
  10.9 17.6 %collective-permute-start.3 = (s32[1]{0:T(128)}, s32[1]{0:T(128)}, u32[]{:S(2)}, u32[]{:S(2)}) collective-permute-start(s32[1]{0:T(128)} %param.13), channel_id=1, source_target_pairs={{8,0},{16,8},{24,16},{9,1},{17,9},{25,17},{10,2},{18,10},{26,18},{... | collective-permute-start | bytes 20 | tf_op jit(solution)/shard_map/ppermute | solution.py:134
  13.7 16.0 %collective-permute-start.1 = (s32[1]{0:T(128)}, s32[1]{0:T(128)}, u32[]{:S(2)}, u32[]{:S(2)}) collective-permute-start(s32[1]{0:T(128)} %param.13), channel_id=1, source_target_pairs={{0,8},{8,16},{16,24},{1,9},{9,17},{17,25},{2,10},{10,18},{18,26},{... | collective-permute-start | bytes 20 | tf_op jit(solution)/shard_map/ppermute | solution.py:134
  17.3 32.1 %collective-permute-start.8 = (bf16[768,384]{1,0:T(8,128)(2,1)S(1)}, bf16[768,384]{1,0:T(8,128)(2,1)S(1)}, u32[]{:S(2)}, u32[]{:S(2)}) collective-permute-start(bf16[768,384]{1,0:T(8,128)(2,1)S(1)} %pad_maximum_fusion.refs_0_), channel_id=1, source_target_pairs={{8,0},{16,8},{24,16},{9,1},{17,9},{25,17},{10,2},{18,10},{26,18},{... | collective-permute-start | bytes 1769480 | tf_op jit(solution)/shard_map/ppermute | solution.py:134
  23.9 27.9 %collective-permute-start.6 = (bf16[768,384]{1,0:T(8,128)(2,1)S(1)}, bf16[768,384]{1,0:T(8,128)(2,1)S(1)}, u32[]{:S(2)}, u32[]{:S(2)}) collective-permute-start(bf16[768,384]{1,0:T(8,128)(2,1)S(1)} %pad_maximum_fusion.refs_0_), channel_id=1, source_target_pairs={{0,8},{8,16},{16,24},{1,9},{9,17},{17,25},{2,10},{10,18},{18,26},{... | collective-permute-start | bytes 1769480 | tf_op jit(solution)/shard_map/ppermute | solution.py:134
  28.5 27.3 %collective-permute-start.10 = (bf16[768,384]{1,0:T(8,128)(2,1)S(1)}, bf16[768,384]{1,0:T(8,128)(2,1)}, u32[]{:S(2)}, u32[]{:S(2)}) collective-permute-start(bf16[768,384]{1,0:T(8,128)(2,1)S(1)} %pad_maximum_fusion.1.refs_0_), channel_id=1, source_target_pairs={{0,4},{4,0},{1,5},{5,1},{2,6},{6,2},{3,7},{7,3},{8,12},{12,8},{9,1... | collective-permute-start | bytes 1769480 | tf_op jit(solution)/shard_map/ppermute | solution.py:139
  29.8 5.5 %collective-permute-start.4 = (s32[1]{0:T(128)}, s32[1]{0:T(128)}, u32[]{:S(2)}, u32[]{:S(2)}) collective-permute-start(s32[1]{0:T(128)} %collective-permute-done), channel_id=1, source_target_pairs={{8,0},{16,8},{24,16},{9,1},{17,9},{25,17},{10,2},{18,10},{26,18},{... | collective-permute-start | bytes 20 | tf_op jit(solution)/shard_map/ppermute | solution.py:134
  35.2 4.9 %collective-permute-start.2 = (s32[1]{0:T(128)}, s32[1]{0:T(128)}, u32[]{:S(2)}, u32[]{:S(2)}) collective-permute-start(s32[1]{0:T(128)} %collective-permute-done), channel_id=1, source_target_pairs={{0,8},{8,16},{16,24},{1,9},{9,17},{17,25},{2,10},{10,18},{18,26},{... | collective-permute-start | bytes 20 | tf_op jit(solution)/shard_map/ppermute | solution.py:134
  37.2 20.6 %collective-permute-start.9 = (bf16[768,384]{1,0:T(8,128)(2,1)S(1)}, bf16[768,384]{1,0:T(8,128)(2,1)}, u32[]{:S(2)}, u32[]{:S(2)}) collective-permute-start(bf16[768,384]{1,0:T(8,128)(2,1)S(1)} %collective-permute-done.5.refs_1_), channel_id=1, source_target_pairs={{8,0},{16,8},{24,16},{9,1},{17,9},{25,17},{10,2},{18,10},{26,18},{... | collective-permute-start | bytes 1769480 | tf_op jit(solution)/shard_map/ppermute | solution.py:134
  40.1 21.2 %collective-permute-start.7 = (bf16[768,384]{1,0:T(8,128)(2,1)S(1)}, bf16[768,384]{1,0:T(8,128)(2,1)}, u32[]{:S(2)}, u32[]{:S(2)}) collective-permute-start(bf16[768,384]{1,0:T(8,128)(2,1)S(1)} %collective-permute-done.5.refs_1_), channel_id=1, source_target_pairs={{0,8},{8,16},{16,24},{1,9},{9,17},{17,25},{2,10},{10,18},{18,26},{... | collective-permute-start | bytes 1769480 | tf_op jit(solution)/shard_map/ppermute | solution.py:134
  49.4 20.8 %collective-permute-start.13 = (bf16[768,384]{1,0:T(8,128)(2,1)S(1)}, bf16[768,384]{1,0:T(8,128)(2,1)S(1)}, u32[]{:S(2)}, u32[]{:S(2)}) collective-permute-start(bf16[768,384]{1,0:T(8,128)(2,1)S(1)} %pad_maximum_fusion.1.refs_0_), channel_id=1, source_target_pairs={{8,0},{16,8},{24,16},{9,1},{17,9},{25,17},{10,2},{18,10},{26,18},{... | collective-permute-start | bytes 1769480 | tf_op jit(solution)/shard_map/ppermute | solution.py:134
  51.9 0.8 copy-start
  52.7 17.5 %collective-permute-start.11 = (bf16[768,384]{1,0:T(8,128)(2,1)S(1)}, bf16[768,384]{1,0:T(8,128)(2,1)S(1)}, u32[]{:S(2)}, u32[]{:S(2)}) collective-permute-start(bf16[768,384]{1,0:T(8,128)(2,1)S(1)} %pad_maximum_fusion.1.refs_0_), channel_id=1, source_target_pairs={{0,8},{8,16},{16,24},{1,9},{9,17},{17,25},{2,10},{10,18},{18,26},{... | collective-permute-start | bytes 1769480 | tf_op jit(solution)/shard_map/ppermute | solution.py:134
  55.8 14.4 %collective-permute-start.14 = (bf16[768,384]{1,0:T(8,128)(2,1)}, bf16[768,384]{1,0:T(8,128)(2,1)S(1)}, u32[]{:S(2)}, u32[]{:S(2)}) collective-permute-start(bf16[768,384]{1,0:T(8,128)(2,1)} %collective-permute-done.10.refs_1_), channel_id=1, source_target_pairs={{8,0},{16,8},{24,16},{9,1},{17,9},{25,17},{10,2},{18,10},{26,18},{... | collective-permute-start | bytes 1769480 | tf_op jit(solution)/shard_map/ppermute | solution.py:134
  57.7 12.5 %collective-permute-start.12 = (bf16[768,384]{1,0:T(8,128)(2,1)}, bf16[768,384]{1,0:T(8,128)(2,1)S(1)}, u32[]{:S(2)}, u32[]{:S(2)}) collective-permute-start(bf16[768,384]{1,0:T(8,128)(2,1)} %collective-permute-done.10.refs_1_), channel_id=1, source_target_pairs={{0,8},{8,16},{16,24},{1,9},{9,17},{17,25},{2,10},{10,18},{18,26},{... | collective-permute-start | bytes 1769480 | tf_op jit(solution)/shard_map/ppermute | solution.py:134
  61.4 1.1 copy-start.1
  69.3 1.0 copy-start.11
  70.2 7.0 %copy-start.3 = (bf16[768,384]{1,0:T(8,128)(2,1)}, bf16[768,384]{1,0:T(8,128)(2,1)S(1)}, u32[]{:S(2)}) copy-start(bf16[768,384]{1,0:T(8,128)(2,1)S(1)} %collective-permute-done.13.refs_4_) | copy-start | bytes 1769476
  70.2 7.0 %copy-start.5 = (bf16[768,384]{1,0:T(8,128)(2,1)}, bf16[768,384]{1,0:T(8,128)(2,1)S(1)}, u32[]{:S(2)}) copy-start(bf16[768,384]{1,0:T(8,128)(2,1)S(1)} %collective-permute-done.11.refs_2_) | copy-start | bytes 1769476
  70.2 7.0 %copy-start.7 = (bf16[768,384]{1,0:T(8,128)(2,1)}, bf16[768,384]{1,0:T(8,128)(2,1)S(1)}, u32[]{:S(2)}) copy-start(bf16[768,384]{1,0:T(8,128)(2,1)S(1)} %collective-permute-done.14.refs_5_) | copy-start | bytes 1769476
  70.3 7.0 %copy-start.9 = (bf16[768,384]{1,0:T(8,128)(2,1)}, bf16[768,384]{1,0:T(8,128)(2,1)S(1)}, u32[]{:S(2)}) copy-start(bf16[768,384]{1,0:T(8,128)(2,1)S(1)} %collective-permute-done.12.refs_3_) | copy-start | bytes 1769476
  77.2 0.8 copy-start.13
  78.8 2.3 %copy-start.15 = (bf16[384,3072]{1,0:T(8,128)(2,1)S(1)}, bf16[384,3072]{1,0:T(8,128)(2,1)}, u32[]{:S(2)}) copy-start(bf16[384,3072]{1,0:T(8,128)(2,1)} %all-gather.2.cloned.1.call-done) | copy-start | bytes 7077892
  81.0 45.2 %collective-permute-start.21 = (bf16[768,768]{1,0:T(8,128)(2,1)S(1)}, bf16[768,768]{1,0:T(8,128)(2,1)S(1)}, u32[]{:S(2)}, u32[]{:S(2)}) collective-permute-start(bf16[768,768]{1,0:T(8,128)(2,1)S(1)} %convolution_convert_fusion.1), channel_id=1, source_target_pairs={{0,8},{8,0},{16,24},{24,16},{1,9},{9,1},{17,25},{25,17},{2,10},{10... | collective-permute-start | bytes 3538952 | tf_op jit(solution)/shard_map/ppermute | solution.py:139
  83.0 48.9 %collective-permute-start.23 = (bf16[768,768]{1,0:T(8,128)(2,1)S(1)}, bf16[768,768]{1,0:T(8,128)(2,1)S(1)}, u32[]{:S(2)}, u32[]{:S(2)}) collective-permute-start(bf16[768,768]{1,0:T(8,128)(2,1)S(1)} %convolution_convert_fusion), channel_id=1, source_target_pairs={{0,8},{8,0},{16,24},{24,16},{1,9},{9,1},{17,25},{25,17},{2,10},{10... | collective-permute-start | bytes 3538952 | tf_op jit(solution)/shard_map/ppermute | solution.py:139
  83.6 4.6 %copy-start.8 = (bf16[768,384]{1,0:T(8,128)(2,1)S(1)}, bf16[768,384]{1,0:T(8,128)(2,1)}, u32[]{:S(2)}) copy-start(bf16[768,384]{1,0:T(8,128)(2,1)} %copy-done.7) | copy-start | bytes 1769476
  83.6 4.6 %copy-start.10 = (bf16[768,384]{1,0:T(8,128)(2,1)S(1)}, bf16[768,384]{1,0:T(8,128)(2,1)}, u32[]{:S(2)}) copy-start(bf16[768,384]{1,0:T(8,128)(2,1)} %copy-done.9) | copy-start | bytes 1769476
  83.6 4.6 %copy-start.14 = (f32[384,384]{1,0:T(8,128)S(1)}, f32[384,384]{1,0:T(8,128)}, u32[]{:S(2)}) copy-start(f32[384,384]{1,0:T(8,128)} %copy-done.13) | copy-start | bytes 1769476
  88.1 1.1 copy-start.4
  88.1 1.2 copy-start.6
  103.6 6.0 %copy-start.2 = (bf16[768,384]{1,0:T(8,128)(2,1)S(1)}, bf16[768,384]{1,0:T(8,128)(2,1)}, u32[]{:S(2)}) copy-start(bf16[768,384]{1,0:T(8,128)(2,1)} %copy-done) | copy-start | bytes 1769476
  103.6 6.0 %copy-start.12 = (f32[384,384]{1,0:T(8,128)S(1)}, f32[384,384]{1,0:T(8,128)}, u32[]{:S(2)}) copy-start(f32[384,384]{1,0:T(8,128)} %copy-done.11) | copy-start | bytes 1769476
  103.9 30.4 %collective-permute-start.18 = (bf16[2,768,384]{2,1,0:T(8,128)(2,1)S(1)}, bf16[2,768,384]{2,1,0:T(8,128)(2,1)S(1)}, u32[]{:S(2)}, u32[]{:S(2)}) collective-permute-start(bf16[2,768,384]{2,1,0:T(8,128)(2,1)S(1)} %get-tuple-element.24), channel_id=1, source_target_pairs={{8,0},{16,8},{24,16},{9,1},{17,9},{25,17},{10,2},{18,10},{26,18},{... | collective-permute-start | bytes 3538952 | tf_op jit(solution)/shard_map/ppermute | solution.py:134
  106.0 29.5 %collective-permute-start.19 = (bf16[2,768,384]{2,1,0:T(8,128)(2,1)S(1)}, bf16[2,768,384]{2,1,0:T(8,128)(2,1)S(1)}, u32[]{:S(2)}, u32[]{:S(2)}) collective-permute-start(bf16[2,768,384]{2,1,0:T(8,128)(2,1)S(1)} %get-tuple-element.25), channel_id=1, source_target_pairs={{0,8},{8,16},{16,24},{1,9},{9,17},{17,25},{2,10},{10,18},{18,26},{... | collective-permute-start | bytes 3538952 | tf_op jit(solution)/shard_map/ppermute | solution.py:134
  124.4 17.8 %collective-permute-start.15 = (bf16[2,768,384]{2,1,0:T(8,128)(2,1)S(1)}, bf16[2,768,384]{2,1,0:T(8,128)(2,1)S(1)}, u32[]{:S(2)}, u32[]{:S(2)}) collective-permute-start(bf16[2,768,384]{2,1,0:T(8,128)(2,1)S(1)} %get-tuple-element.22), channel_id=1, source_target_pairs={{8,0},{16,8},{24,16},{9,1},{17,9},{25,17},{10,2},{18,10},{26,18},{... | collective-permute-start | bytes 3538952 | tf_op jit(solution)/shard_map/ppermute | solution.py:134
  126.3 16.8 %collective-permute-start.16 = (bf16[2,768,384]{2,1,0:T(8,128)(2,1)S(1)}, bf16[2,768,384]{2,1,0:T(8,128)(2,1)S(1)}, u32[]{:S(2)}, u32[]{:S(2)}) collective-permute-start(bf16[2,768,384]{2,1,0:T(8,128)(2,1)S(1)} %get-tuple-element.23), channel_id=1, source_target_pairs={{0,8},{8,16},{16,24},{1,9},{9,17},{17,25},{2,10},{10,18},{18,26},{... | collective-permute-start | bytes 3538952 | tf_op jit(solution)/shard_map/ppermute | solution.py:134
  131.9 15.4 %collective-permute-start.22 = (bf16[1,384,768]{2,1,0:T(8,128)(2,1)S(1)}, bf16[1,384,768]{2,1,0:T(8,128)(2,1)S(1)}, u32[]{:S(2)}, u32[]{:S(2)}) collective-permute-start(bf16[1,384,768]{2,1,0:T(8,128)(2,1)S(1)} %fusion.5), channel_id=1, source_target_pairs={{0,4},{4,0},{1,5},{5,1},{2,6},{6,2},{3,7},{7,3},{8,12},{12,8},{9,1... | collective-permute-start | bytes 1769480 | tf_op jit(solution)/shard_map/ppermute | solution.py:139
  134.3 25.7 %collective-permute-start.24 = (bf16[1,384,768]{2,1,0:T(8,128)(2,1)S(1)}, bf16[1,384,768]{2,1,0:T(8,128)(2,1)S(1)}, u32[]{:S(2)}, u32[]{:S(2)}) collective-permute-start(bf16[1,384,768]{2,1,0:T(8,128)(2,1)S(1)} %fusion.6), channel_id=1, source_target_pairs={{0,4},{4,0},{1,5},{5,1},{2,6},{6,2},{3,7},{7,3},{8,12},{12,8},{9,1... | collective-permute-start | bytes 1769480 | tf_op jit(solution)/shard_map/ppermute | solution.py:139
  136.0 36.6 %collective-permute-start.20 = (bf16[768,384]{1,0:T(8,128)(2,1)S(1)}, bf16[768,384]{1,0:T(8,128)(2,1)S(1)}, u32[]{:S(2)}, u32[]{:S(2)}) collective-permute-start(bf16[768,384]{1,0:T(8,128)(2,1)S(1)} %fusion.9), channel_id=1, source_target_pairs={{0,4},{4,0},{1,5},{5,1},{2,6},{6,2},{3,7},{7,3},{8,12},{12,8},{9,1... | collective-permute-start | bytes 1769480 | tf_op jit(solution)/shard_map/ppermute | solution.py:139
  143.5 40.8 %collective-permute-start.17 = (bf16[768,384]{1,0:T(8,128)(2,1)S(1)}, bf16[768,384]{1,0:T(8,128)(2,1)S(1)}, u32[]{:S(2)}, u32[]{:S(2)}) collective-permute-start(bf16[768,384]{1,0:T(8,128)(2,1)S(1)} %fusion.8), channel_id=1, source_target_pairs={{0,4},{4,0},{1,5},{5,1},{2,6},{6,2},{3,7},{7,3},{8,12},{12,8},{9,1... | collective-permute-start | bytes 1769480 | tf_op jit(solution)/shard_map/ppermute | solution.py:139
  160.2 26.1 %collective-permute-start.25 = (bf16[384,768]{1,0:T(8,128)(2,1)S(1)}, bf16[384,768]{1,0:T(8,128)(2,1)S(1)}, u32[]{:S(2)}, u32[]{:S(2)}) collective-permute-start(bf16[384,768]{1,0:T(8,128)(2,1)S(1)} %fusion.7), channel_id=1, source_target_pairs={{0,16},{8,24},{16,0},{24,8},{1,17},{9,25},{17,1},{25,9},{2,18},{10... | collective-permute-start | bytes 1769480 | tf_op jit(solution)/shard_map/ppermute | solution.py:139
Sparse Core Ops, SparseCore 0:
  10.9 51.1 all-gather.1

commit v3 on v2

--- a/solution.py
+++ b/solution.py
@@ -168,43 +168,49 @@
         )
 
     if time_size & (time_size - 1) or height_size & (height_size - 1) or time_size < 2:
-        return [], lax.psum_scatter(
+        return [], [], lax.psum_scatter(
             product(gathered).astype(jnp.bfloat16), ("tm", "height"),
             scatter_dimension=0, tiled=True,
         ).astype(jnp.float32)
     bit = time_place % 2
-
-    def product_of(high, which):
-        start = (2 * high + which) * height_size * block
-        return product(lax.dynamic_slice_in_dim(gathered, start, height_size * block, 1))
-
-    highs = range(time_size // 2)
-    first = [product_of(high, 1 - bit).astype(jnp.bfloat16) for high in highs]
-    kept = [product_of(high, bit) for high in highs]
-    got = [swapped(x, "tm", 0) for x in first]
-    held = [k + g.astype(jnp.float32) for k, g in zip(kept, got)]
-    for number in range(height_size.bit_length() - 1):
-        bit = (height_place // (1 << number)) % 2
-        count = held[0].shape[0] // (2 * block)
-        wide = [x.reshape(count, 2, block, -1) for x in held]
-        sent = [lax.dynamic_index_in_dim(x, 1 - bit, 1, keepdims=False) for x in wide]
-        kept = [lax.dynamic_index_in_dim(x, bit, 1, keepdims=False) for x in wide]
-        got = [swapped(x.astype(jnp.bfloat16), "height", number) for x in sent]
-        held = [(k + g.astype(jnp.float32)).reshape(count * block, -1) for k, g in zip(kept, got)]
-    for number in range(1, time_size.bit_length() - 1):
-        bit = (time_place // (1 << number)) % 2
-        low, high = held[0::2], held[1::2]
-        sent = [jnp.where(bit == 0, y, x) for x, y in zip(low, high)]
-        kept = [jnp.where(bit == 0, x, y) for x, y in zip(low, high)]
-        got = [swapped(x.astype(jnp.bfloat16), "tm", number) for x in sent]
-        held = [k + g.astype(jnp.float32) for k, g in zip(kept, got)]
-    return first, held[0]
+    span = height_size * block
+
+    def product_of(which):
+        parts = [
+            lax.dynamic_slice_in_dim(gathered, (2 * high + which) * span, span, 1)
+            for high in range(time_size // 2)
+        ]
+        return product(jnp.concatenate(parts, axis=1))
+
+    got = swapped(product_of(1 - bit).astype(jnp.bfloat16), "tm", 0)
+    held = product_of(bit) + got.astype(jnp.float32)
+
+    def rows_for(time_mask, height_mask):
+        owner = (time_place // 2 ^ time_mask) * height_size + (height_place ^ height_mask)
+        return lax.dynamic_slice_in_dim(held, owner * block, block, 0)
+
+    masks = [(t, h) for t in range(time_size // 2) for h in range(height_size)][1:]
+    sent = [rows_for(*mask).astype(jnp.bfloat16) for mask in masks]
+    return masks, sent, rows_for(0, 0)
+
+
+def exchanged(masks, sent):
+    time_size, height_size = lax.axis_size("tm"), lax.axis_size("height")
+    got = []
+    for (time_mask, height_mask), x in zip(masks, sent):
+        pairs = [
+            (t * height_size + h, (t ^ (2 * time_mask)) * height_size + (h ^ height_mask))
+            for t in range(time_size)
+            for h in range(height_size)
+        ]
+        got.append(lax.ppermute(x, ("tm", "height"), pairs))
+    return got
 
 
 def on_device(queries, keys, values, out_grad, out_weight, window, counts):
     row_count, width_local = queries.shape
     heads_local = width_local // HDIM
-    chunks = CHUNKS if heads_local % CHUNKS == 0 else 1
+    chunks = CHUNKS if heads_local % CHUNKS == 0 and heads_local > CHUNKS else 1
     width = width_local // chunks
     time_size, height_size = lax.axis_size("tm"), lax.axis_size("height")
     time_place, height_place = lax.axis_index("tm"), lax.axis_index("height")
@@ -217,17 +223,22 @@
 
     packs = []
     for chunk in range(chunks):
-        pair = jnp.concatenate([columns(keys, chunk), columns(values, chunk)], axis=0)
+        parts = [columns(keys, chunk), columns(values, chunk)]
+        if chunk == 0:
+            parts.append(
+                jnp.where(jnp.arange(width) < HDIM, counts // 16, counts % 16)[None]
+                .astype(jnp.bfloat16)
+                .repeat(16, axis=0)
+            )
+        pair = jnp.concatenate(parts, axis=0)
         near = [pair] + [fetch(pair) for fetch, _ in sends]
         packs.append(
             near + [moved(x, "tm", 1) for x in near] + [moved(x, "tm", -1) for x in near]
         )
-    count_near = [counts] + [fetch(counts) for fetch, _ in sends]
-    count_all = (
-        count_near
-        + [moved(x, "tm", 1) for x in count_near]
-        + [moved(x, "tm", -1) for x in count_near]
-    )
+    count_all = [
+        (x[2 * TILE, 0].astype(jnp.int32) * 16 + x[2 * TILE, width - 1].astype(jnp.int32))
+        for x in packs[0]
+    ]
     positions = jnp.arange(TILE, dtype=jnp.int32)
     rows = []
     number = 0
@@ -254,13 +265,17 @@
     per = len(steps)
     ahead_of = [forward(bias, columns(queries, c), packs[c]) for c in range(chunks)]
     attended_all = jnp.concatenate([x[0] for x in ahead_of], axis=1)
-    first, weight_out = reduce_scattered(full_grad, attended_all)
-    grad_out, first = lax.optimization_barrier((grad_out, first))
+    masks, sent, kept = reduce_scattered(full_grad, attended_all)
+    grad_out, sent = lax.optimization_barrier((grad_out, sent))
+    got = exchanged(masks, sent)
     outs = []
     for chunk in range(chunks):
         attended, total = ahead_of[chunk]
+        grad_part = columns(grad_out, chunk)
+        if chunk > 0:
+            grad_part, got[:2] = lax.optimization_barrier((grad_part, got[:2]))
         query_out, pair_out = backward(
-            bias, columns(queries, chunk), columns(grad_out, chunk), attended, total, packs[chunk]
+            bias, columns(queries, chunk), grad_part, attended, total, packs[chunk]
         )
         back = moved(pair_out[per : 2 * per], "tm", -1).astype(jnp.float32)
         ahead = moved(pair_out[2 * per :], "tm", 1).astype(jnp.float32)
@@ -271,6 +286,7 @@
         final = final.astype(jnp.bfloat16)
         outs.append((query_out, final[:TILE], final[TILE:]))
     joined = tuple(jnp.concatenate([out[i] for out in outs], axis=1) for i in range(3))
+    weight_out = kept + sum(x.astype(jnp.float32) for x in got)
     return joined + (weight_out * token_share,)
 
 

time: 195 us -> 181 us (0.928); the launches traced: 195 us -> 178 us
  waiting for transfers between devices: 52 us -> 21.9 us
  local copies, waits for them, and re-layouts: 8.56 us -> 20.6 us
  between operations: 19.3 us -> 27.2 us
  starting transfers between devices: 51.1 us -> 45.6 us
  matrix products: 12.3 us -> 9.42 us
  other arithmetic: 8.64 us -> 10.6 us
    ppermute x10 -> x5, waiting for transfers between devices: 41.6 us -> 13.9 us  [swapped(): return lax.ppermute(x, axis, [(i, i ^ 1 << bit) for i in range(size)])]
    slice x0 -> x6, local copies, waits for them, and re-layouts: none -> 5.01 us  [on_device(): x[2 * TILE, width - 1].astype(jnp.int32)]
    ppermute x16 -> x12, starting transfers between devices: 44.7 us -> 40 us  [moved(): return lax.ppermute(x, axis, pairs)]
    add x2, other arithmetic: 0.77 us -> 4.37 us  [on_device(): own = pair_out[:per].astype(jnp.float32) + back + ahead]
    ppermute x10 -> x5, starting transfers between devices: 6.4 us -> 2.8 us  [swapped(): return lax.ppermute(x, axis, [(i, i ^ 1 << bit) for i in range(size)])]
    dot_general x4 -> x2, matrix products: 7.87 us -> 4.33 us  [product(): lax.dot_general(part.reshape(rows, -1), attended, (((0,), (0,)), ((), ())...]
    slice x2, local copies, waits for them, and re-layouts: 0.48 us -> 3.54 us  [on_device(): back = moved(pair_out[per:2 * per], 'tm', -1).astype(jnp.float32)]
    ppermute x0 -> x3, starting transfers between devices: none -> 2.71 us  [exchanged(): got.append(lax.ppermute(x, ('tm', 'height'), pairs))]
  transfers between devices with their start and end apart: 27 -> 21, of which waited for: 8 -> 5; matrix products, arithmetic and copies ran while one was open for 11% -> 14% of each run, Pallas kernels for 22% -> 24%
where the time goes in v3:
time: 181 us; the launch traced here: 178 us
  starting transfers between devices  45.6 us (25%)
  Pallas kernels  42.8 us (24%)
  between operations  27.2 us (15%)
  waiting for transfers between devices  21.9 us (12%)
  local copies, waits for them, and re-layouts  20.6 us (11%)
  other arithmetic  10.6 us (6%)
  matrix products  9.42 us (5%)
    ppermute x12, starting transfers between devices, moved(): return lax.ppermute(x, axis, pairs)  40 us
    pallas_call x2, Pallas kernels, backward(): pl.pallas_call(functools.partial(backward_kernel, slots), grid=(heads,),...  29 us
    ppermute x5, waiting for transfers between devices, swapped(): return lax.ppermute(x, axis, [(i, i ^ 1 << bit) for i in range(size)])  13.9 us
    pallas_call x2, Pallas kernels, forward(): pl.pallas_call(functools.partial(forward_kernel, slots), grid=(heads,), i...  13.7 us
    ppermute x12, waiting for transfers between devices, moved(): return lax.ppermute(x, axis, pairs)  7.94 us
    unnamed x79, local copies, waits for them, and re-layouts  5.53 us
    dot_general x1, matrix products, on_device(): jnp.dot(full_grad, out_weight, preferred_element_type=jnp.float32)  5.09 us
    slice x6, local copies, waits for them, and re-layouts, on_device(): x[2 * TILE, width - 1].astype(jnp.int32)  5.01 us
  transfers between devices with their start and end apart: 21, of which 5 were waited for; matrix products, arithmetic and copies ran while one was open for 14% of the time, Pallas kernels for 24%

profile of v3, /device:TPU:1, one launch (start us, length us, event | category | flops | bytes accessed | tf_op | source)
XLA Modules:
  0.0 178.0 jit_solution(14529125356917036194)
XLA Ops:
  7.9 1.4 fusion.24
  9.4 2.1 %collective-permute-start = (bf16[784,384]{1,0:T(8,128)(2,1)S(1)}, bf16[784,384]{1,0:T(8,128)(2,1)S(1)}, u32[]{:S(2)}, u32[]{:S(2)}) collective-permute-start(bf16[784,384]{1,0:T(8,128)(2,1)S(1)} %pad_maximum_fusion.refs_0_), channel_id=1, source_target_pairs={{0,4},{4,0},{1,5},{5,1},{2,6},{6,2},{3,7},{7,3},{8,12},{12,8},{9,1... | collective-permute-start | bytes 1806344 | tf_op jit(solution)/shard_map/ppermute | solution.py:139
  11.5 2.9 %collective-permute-start.3 = (bf16[784,384]{1,0:T(8,128)(2,1)S(1)}, bf16[784,384]{1,0:T(8,128)(2,1)S(1)}, u32[]{:S(2)}, u32[]{:S(2)}) collective-permute-start(bf16[784,384]{1,0:T(8,128)(2,1)S(1)} %pad_maximum_fusion.refs_0_), channel_id=1, source_target_pairs={{8,0},{16,8},{24,16},{9,1},{17,9},{25,17},{10,2},{18,10},{26,18},{... | collective-permute-start | bytes 1806344 | tf_op jit(solution)/shard_map/ppermute | solution.py:134
  14.4 1.9 %collective-permute-start.8 = (bf16[768,384]{1,0:T(8,128)(2,1)S(1)}, bf16[768,384]{1,0:T(8,128)(2,1)}, u32[]{:S(2)}, u32[]{:S(2)}) collective-permute-start(bf16[768,384]{1,0:T(8,128)(2,1)S(1)} %pad_maximum_fusion.1.refs_0_), channel_id=1, source_target_pairs={{8,0},{16,8},{24,16},{9,1},{17,9},{25,17},{10,2},{18,10},{26,18},{... | collective-permute-start | bytes 1769480 | tf_op jit(solution)/shard_map/ppermute | solution.py:134
  16.4 3.6 %collective-permute-start.1 = (bf16[784,384]{1,0:T(8,128)(2,1)S(1)}, bf16[784,384]{1,0:T(8,128)(2,1)}, u32[]{:S(2)}, u32[]{:S(2)}) collective-permute-start(bf16[784,384]{1,0:T(8,128)(2,1)S(1)} %pad_maximum_fusion.refs_0_), channel_id=1, source_target_pairs={{0,8},{8,16},{16,24},{1,9},{9,17},{17,25},{2,10},{10,18},{18,26},{... | collective-permute-start | bytes 1806344 | tf_op jit(solution)/shard_map/ppermute | solution.py:134
  20.1 0.7 constant_dynamic-slice_fusion.4
  20.8 1.1 fusion.26
  21.9 0.6 fusion.27
  24.8 4.0 %collective-permute-start.4 = (bf16[784,384]{1,0:T(8,128)(2,1)S(1)}, bf16[784,384]{1,0:T(8,128)(2,1)}, u32[]{:S(2)}, u32[]{:S(2)}) collective-permute-start(bf16[784,384]{1,0:T(8,128)(2,1)S(1)} %collective-permute-done.refs_1_), channel_id=1, source_target_pairs={{8,0},{16,8},{24,16},{9,1},{17,9},{25,17},{10,2},{18,10},{26,18},{... | collective-permute-start | bytes 1806344 | tf_op jit(solution)/shard_map/ppermute | solution.py:134
  32.1 3.6 %collective-permute-start.2 = (bf16[784,384]{1,0:T(8,128)(2,1)S(1)}, bf16[784,384]{1,0:T(8,128)(2,1)S(1)}, u32[]{:S(2)}, u32[]{:S(2)}) collective-permute-start(bf16[784,384]{1,0:T(8,128)(2,1)S(1)} %collective-permute-done.refs_1_), channel_id=1, source_target_pairs={{0,8},{8,16},{16,24},{1,9},{9,17},{17,25},{2,10},{10,18},{18,26},{... | collective-permute-start | bytes 1806344 | tf_op jit(solution)/shard_map/ppermute | solution.py:134
  37.6 4.4 %collective-permute-start.6 = (bf16[768,384]{1,0:T(8,128)(2,1)S(1)}, bf16[768,384]{1,0:T(8,128)(2,1)S(1)}, u32[]{:S(2)}, u32[]{:S(2)}) collective-permute-start(bf16[768,384]{1,0:T(8,128)(2,1)S(1)} %pad_maximum_fusion.1.refs_0_), channel_id=1, source_target_pairs={{0,8},{8,16},{16,24},{1,9},{9,17},{17,25},{2,10},{10,18},{18,26},{... | collective-permute-start | bytes 1769480 | tf_op jit(solution)/shard_map/ppermute | solution.py:134
  42.0 1.9 %collective-permute-start.9 = (bf16[768,384]{1,0:T(8,128)(2,1)}, bf16[768,384]{1,0:T(8,128)(2,1)S(1)}, u32[]{:S(2)}, u32[]{:S(2)}) collective-permute-start(bf16[768,384]{1,0:T(8,128)(2,1)} %collective-permute-done.5.refs_1_), channel_id=1, source_target_pairs={{8,0},{16,8},{24,16},{9,1},{17,9},{25,17},{10,2},{18,10},{26,18},{... | collective-permute-start | bytes 1769480 | tf_op jit(solution)/shard_map/ppermute | solution.py:134
  44.0 1.3 fusion.19
  48.5 3.6 %collective-permute-start.7 = (bf16[768,384]{1,0:T(8,128)(2,1)}, bf16[768,384]{1,0:T(8,128)(2,1)S(1)}, u32[]{:S(2)}, u32[]{:S(2)}) collective-permute-start(bf16[768,384]{1,0:T(8,128)(2,1)} %collective-permute-done.5.refs_1_), channel_id=1, source_target_pairs={{0,8},{8,16},{16,24},{1,9},{9,17},{17,25},{2,10},{10,18},{18,26},{... | collective-permute-start | bytes 1769480 | tf_op jit(solution)/shard_map/ppermute | solution.py:134
  52.2 1.3 fusion.16
  54.8 0.7 fusion.18
  56.8 6.8 %shard_map.102 = (bf16[384,384]{1,0:T(8,128)(2,1)S(1)}, f32[384,384]{1,0:T(8,128)S(1)}) custom-call(f32[6,1,384]{2,1,0:T(1,128)S(1)} %constant_dynamic-update-slice_fusion.bias_ref, bf16[384,384]{1,0:T(8,128)(2,1)S(1)} %get-tuple-element.65.query_ref, bf16[784,384]{1,0:T(8,128)(2,1)S(1)} %pad_maximum_fusion.refs_0_, ...), custom_call_target="tpu_custom_call" | custom-call | flops 10871635968 | bytes 7077888 | tf_op jit(solution)/shard_map/pallas_call | solution.py:90
  63.7 0.8 copy-done.29
  65.3 6.9 %shard_map.103 = (bf16[384,384]{1,0:T(8,128)(2,1)S(1)}, f32[384,384]{1,0:T(8,128)S(1)}) custom-call(f32[6,1,384]{2,1,0:T(1,128)S(1)} %constant_dynamic-update-slice_fusion.bias_ref, bf16[384,384]{1,0:T(8,128)(2,1)S(1)} %get-tuple-element.66.query_ref, bf16[768,384]{1,0:T(8,128)(2,1)S(1)} %pad_maximum_fusion.1.refs_0_, ...), custom_call_target="tpu_custom_call" | custom-call | flops 10871635968 | bytes 7077888 | tf_op jit(solution)/shard_map/pallas_call | solution.py:90
  72.2 0.8 copy-done.31
  73.1 0.7 copy-done.5
  73.8 2.0 %constant_dynamic-slice_fusion.3 = (bf16[384,768]{1,0:T(8,128)(2,1)S(1)}, bf16[384,768]{1,0:T(8,128)(2,1)S(1)}, bf16[384,768]{1,0:T(8,128)(2,1)S(1)}, bf16[384,768]{1,0:T(8,128)(2,1)S(1)}) fusion(bf16[384,3072]{1,0:T(8,128)(2,1)} %all-gather.2.cloned.1.call-done, s32[]{:T(128)S(6)} %select_n.142, s32[]{:T(128)S(6)} %select_n.145, s32[]{:T(128)S(6)} %select_n.144, ...), kind=kLoop, calls=%fused_computation.47 | loop fusion | bytes 4718608 | tf_op jit(solution)/shard_map/dynamic_slice | solution.py:180
  75.8 2.9 %convolution_convert_fusion = bf16[1536,768]{1,0:T(8,128)(2,1)} fusion(bf16[384,768]{1,0:T(8,128)(2,1)S(1)} %constant_dynamic-update-slice_fusion.6, bf16[384,768]{1,0:T(8,128)(2,1)S(1)} %get-tuple-element.42, bf16[384,768]{1,0:T(8,128)(2,1)S(1)} %get-tuple-element.43), kind=kOutput, calls=%fused_computation.1 | convolution fusion | flops 909508608 | bytes 4128768 | tf_op jit(solution)/shard_map/dot_general | solution.py:165
  78.7 5.1 %convolution_convert_fusion.1 = bf16[384,768]{1,0:T(8,128)(2,1)S(1)} fusion(bf16[384,3072]{1,0:T(8,128)(2,1)} %all-gather.2.cloned.1.call-done, bf16[3072,768]{1,0:T(8,128)(2,1)} %param.11), kind=kOutput, calls=%fused_computation.4 | convolution fusion | flops 1812234240 | bytes 7667712 | tf_op jit(solution)/shard_map/dot_general | solution.py:261
  83.8 1.5 convert_add_fusion
  85.3 1.0 dynamic-slice_convert_fusion
  86.4 1.3 collective-permute-start.11
  87.8 1.3 collective-permute-start.19
  89.2 14.6 %shard_map.104 = (bf16[384,384]{1,0:T(8,128)(2,1)S(1)}, bf16[6,768,384]{2,1,0:T(8,128)(2,1)S(1)}) custom-call(f32[6,1,384]{2,1,0:T(1,128)S(1)} %constant_dynamic-update-slice_fusion.bias_ref, bf16[384,384]{1,0:T(8,128)(2,1)S(1)} %copy-done.12, bf16[384,384]{1,0:T(8,128)(2,1)S(1)} %get-tuple-element.59.grad_ref, bf16[384,384]{1,0:T(8,128)(2,1)S(1)} %copy-done.8, ...), custom_call_target="tpu_custom_call" | custom-call | flops 16307453952 | bytes 7077888 | tf_op jit(solution)/shard_map/pallas_call | solution.py:113
  103.9 1.7 fusion.14
  105.6 3.4 %collective-permute-start.13 = (bf16[2,768,384]{2,1,0:T(8,128)(2,1)}, bf16[2,768,384]{2,1,0:T(8,128)(2,1)}, u32[]{:S(2)}, u32[]{:S(2)}) collective-permute-start(bf16[2,768,384]{2,1,0:T(8,128)(2,1)} %get-tuple-element.37), channel_id=1, source_target_pairs={{8,0},{16,8},{24,16},{9,1},{17,9},{25,17},{10,2},{18,10},{26,18},{... | collective-permute-start | bytes 3538952 | tf_op jit(solution)/shard_map/ppermute | solution.py:134
  108.9 2.3 %collective-permute-start.14 = (bf16[2,768,384]{2,1,0:T(8,128)(2,1)}, bf16[2,768,384]{2,1,0:T(8,128)(2,1)}, u32[]{:S(2)}, u32[]{:S(2)}) collective-permute-start(bf16[2,768,384]{2,1,0:T(8,128)(2,1)} %get-tuple-element.38), channel_id=1, source_target_pairs={{0,8},{8,16},{16,24},{1,9},{9,17},{17,25},{2,10},{10,18},{18,26},{... | collective-permute-start | bytes 3538952 | tf_op jit(solution)/shard_map/ppermute | solution.py:134
  111.3 0.8 copy-done.36
  112.3 14.4 %shard_map.105 = (bf16[384,384]{1,0:T(8,128)(2,1)S(1)}, bf16[6,768,384]{2,1,0:T(8,128)(2,1)S(1)}) custom-call(f32[6,1,384]{2,1,0:T(1,128)S(1)} %constant_dynamic-update-slice_fusion.bias_ref, bf16[384,384]{1,0:T(8,128)(2,1)S(1)} %copy-done.10, bf16[384,384]{1,0:T(8,128)(2,1)S(1)} %get-tuple-element.26.grad_ref, bf16[384,384]{1,0:T(8,128)(2,1)S(1)} %copy-done.6, ...), custom_call_target="tpu_custom_call" | custom-call | flops 16307453952 | bytes 7077888 | tf_op jit(solution)/shard_map/pallas_call | solution.py:113
  126.8 1.9 %fusion.15 = (bf16[2,768,384]{2,1,0:T(8,128)(2,1)}, bf16[2,768,384]{2,1,0:T(8,128)(2,1)}) fusion(bf16[6,768,384]{2,1,0:T(8,128)(2,1)S(1)} %get-tuple-element.30), kind=kLoop, calls=%fused_computation.56 | loop fusion | bytes 4718592 | tf_op jit(solution)/shard_map/slice | solution.py:280
  128.7 0.6 copy-done
  129.4 6.5 %collective-permute-start.16 = (bf16[2,768,384]{2,1,0:T(8,128)(2,1)}, bf16[2,768,384]{2,1,0:T(8,128)(2,1)}, u32[]{:S(2)}, u32[]{:S(2)}) collective-permute-start(bf16[2,768,384]{2,1,0:T(8,128)(2,1)} %get-tuple-element.39), channel_id=1, source_target_pairs={{8,0},{16,8},{24,16},{9,1},{17,9},{25,17},{10,2},{18,10},{26,18},{... | collective-permute-start | bytes 3538952 | tf_op jit(solution)/shard_map/ppermute | solution.py:134
  135.9 1.9 %collective-permute-start.17 = (bf16[2,768,384]{2,1,0:T(8,128)(2,1)}, bf16[2,768,384]{2,1,0:T(8,128)(2,1)}, u32[]{:S(2)}, u32[]{:S(2)}) collective-permute-start(bf16[2,768,384]{2,1,0:T(8,128)(2,1)} %get-tuple-element.40), channel_id=1, source_target_pairs={{0,8},{8,16},{16,24},{1,9},{9,17},{17,25},{2,10},{10,18},{18,26},{... | collective-permute-start | bytes 3538952 | tf_op jit(solution)/shard_map/ppermute | solution.py:134
  137.8 3.1 %add_multiply_fusion = f32[384,768]{1,0:T(8,128)} fusion(bf16[384,768]{1,0:T(8,128)(2,1)} %collective-permute-done.19, bf16[384,768]{1,0:T(8,128)(2,1)} %copy-done.37, bf16[384,768]{1,0:T(8,128)(2,1)} %copy-done.36, f32[1536,768]{1,0:T(8,128)} %copy-done.33, s32[]{:T(128)S(6)} %select_n.150), kind=kLoop, calls=%fused_computation.19 | loop fusion | flops 2064384 | bytes 4128772 | tf_op jit(solution)/shard_map/mul | solution.py:290
  140.9 2.0 %convert_add_fusion.2 = f32[2,768,384]{2,1,0:T(8,128)S(1)} fusion(bf16[2,768,384]{2,1,0:T(8,128)(2,1)} %collective-permute-done.14, bf16[2,768,384]{2,1,0:T(8,128)(2,1)} %collective-permute-done.13, bf16[6,768,384]{2,1,0:T(8,128)(2,1)S(1)} %get-tuple-element.29), kind=kLoop, calls=%fused_computation.3 | loop fusion | flops 2949120 | bytes 5898240 | tf_op jit(solution)/shard_map/add | solution.py:282
  143.3 6.9 %collective-permute-done.16 = bf16[2,768,384]{2,1,0:T(8,128)(2,1)} collective-permute-done((bf16[2,768,384]{2,1,0:T(8,128)(2,1)}, bf16[2,768,384]{2,1,0:T(8,128)(2,1)}, u32[]{:S(2)}, u32[]{:S(2)}) %collective-permute-start.16) | collective-permute-done | bytes 1179680 | tf_op jit(solution)/shard_map/ppermute | solution.py:134
  150.3 1.0 collective-permute-done.17
  151.2 2.4 %convert_add_fusion.1 = f32[2,768,384]{2,1,0:T(8,128)S(1)} fusion(bf16[2,768,384]{2,1,0:T(8,128)(2,1)} %collective-permute-done.17, bf16[2,768,384]{2,1,0:T(8,128)(2,1)} %collective-permute-done.16, bf16[6,768,384]{2,1,0:T(8,128)(2,1)} %copy-done), kind=kLoop, calls=%fused_computation.2 | loop fusion | flops 2949120 | bytes 5898240 | tf_op jit(solution)/shard_map/add | solution.py:282
  154.7 0.9 pad_maximum_fusion.2
  155.5 0.9 collective-permute-done.15
  156.6 12.6 %collective-permute-done.18 = bf16[768,384]{1,0:T(8,128)(2,1)S(1)} collective-permute-done((bf16[768,384]{1,0:T(8,128)(2,1)S(1)}, bf16[768,384]{1,0:T(8,128)(2,1)S(1)}, u32[]{:S(2)}, u32[]{:S(2)}) %collective-permute-start.18) | collective-permute-done | bytes 589856 | tf_op jit(solution)/shard_map/ppermute | solution.py:139
  169.4 0.9 pad_maximum_fusion.4
  170.3 0.9 pad_maximum_fusion.3
  (118 shorter events, 5.2 us)
Async XLA Ops:
  7.2 66.6 %all-gather.2.cloned.1.call-start = ((), (), s32[]{:S(2)}) async-start(), calls=%async_computation | async-start | bytes 2949120 | tf_op jit(solution)/shard_map/all_gather | solution.py:219
  9.3 47.5 %copy-start.1 = (bf16[784,384]{1,0:T(8,128)(2,1)}, bf16[784,384]{1,0:T(8,128)(2,1)S(1)}, u32[]{:S(2)}) copy-start(bf16[784,384]{1,0:T(8,128)(2,1)S(1)} %pad_maximum_fusion.refs_0_) | copy-start | bytes 1806340
  9.3 10.8 %copy-start.38 = (s32[1,27]{1,0:T(1,128)S(1)}, s32[1,27]{1,0:T(1,128)}, u32[]{:S(2)}) copy-start(s32[1,27]{1,0:T(1,128)} %param.12) | copy-start | bytes 328
  9.4 15.4 %collective-permute-start = (bf16[784,384]{1,0:T(8,128)(2,1)S(1)}, bf16[784,384]{1,0:T(8,128)(2,1)S(1)}, u32[]{:S(2)}, u32[]{:S(2)}) collective-permute-start(bf16[784,384]{1,0:T(8,128)(2,1)S(1)} %pad_maximum_fusion.refs_0_), channel_id=1, source_target_pairs={{0,4},{4,0},{1,5},{5,1},{2,6},{6,2},{3,7},{7,3},{8,12},{12,8},{9,1... | collective-permute-start | bytes 1806344 | tf_op jit(solution)/shard_map/ppermute | solution.py:139
  11.5 20.6 %collective-permute-start.3 = (bf16[784,384]{1,0:T(8,128)(2,1)S(1)}, bf16[784,384]{1,0:T(8,128)(2,1)S(1)}, u32[]{:S(2)}, u32[]{:S(2)}) collective-permute-start(bf16[784,384]{1,0:T(8,128)(2,1)S(1)} %pad_maximum_fusion.refs_0_), channel_id=1, source_target_pairs={{8,0},{16,8},{24,16},{9,1},{17,9},{25,17},{10,2},{18,10},{26,18},{... | collective-permute-start | bytes 1806344 | tf_op jit(solution)/shard_map/ppermute | solution.py:134
  14.4 50.9 %copy-start.3 = (bf16[768,384]{1,0:T(8,128)(2,1)}, bf16[768,384]{1,0:T(8,128)(2,1)S(1)}, u32[]{:S(2)}) copy-start(bf16[768,384]{1,0:T(8,128)(2,1)S(1)} %pad_maximum_fusion.1.refs_0_) | copy-start | bytes 1769476
  14.4 50.2 %collective-permute-start.8 = (bf16[768,384]{1,0:T(8,128)(2,1)S(1)}, bf16[768,384]{1,0:T(8,128)(2,1)}, u32[]{:S(2)}, u32[]{:S(2)}) collective-permute-start(bf16[768,384]{1,0:T(8,128)(2,1)S(1)} %pad_maximum_fusion.1.refs_0_), channel_id=1, source_target_pairs={{8,0},{16,8},{24,16},{9,1},{17,9},{25,17},{10,2},{18,10},{26,18},{... | collective-permute-start | bytes 1769480 | tf_op jit(solution)/shard_map/ppermute | solution.py:134
  16.3 21.3 %collective-permute-start.5 = (bf16[768,384]{1,0:T(8,128)(2,1)S(1)}, bf16[768,384]{1,0:T(8,128)(2,1)}, u32[]{:S(2)}, u32[]{:S(2)}) collective-permute-start(bf16[768,384]{1,0:T(8,128)(2,1)S(1)} %pad_maximum_fusion.1.refs_0_), channel_id=1, source_target_pairs={{0,4},{4,0},{1,5},{5,1},{2,6},{6,2},{3,7},{7,3},{8,12},{12,8},{9,1... | collective-permute-start | bytes 1769480 | tf_op jit(solution)/shard_map/ppermute | solution.py:139
  16.4 25.6 %collective-permute-start.1 = (bf16[784,384]{1,0:T(8,128)(2,1)S(1)}, bf16[784,384]{1,0:T(8,128)(2,1)}, u32[]{:S(2)}, u32[]{:S(2)}) collective-permute-start(bf16[784,384]{1,0:T(8,128)(2,1)S(1)} %pad_maximum_fusion.refs_0_), channel_id=1, source_target_pairs={{0,8},{8,16},{16,24},{1,9},{9,17},{17,25},{2,10},{10,18},{18,26},{... | collective-permute-start | bytes 1806344 | tf_op jit(solution)/shard_map/ppermute | solution.py:134
  21.9 41.8 %copy-start.11 = (bf16[384,384]{1,0:T(8,128)(2,1)}, bf16[384,384]{1,0:T(8,128)(2,1)S(1)}, u32[]{:S(2)}) copy-start(bf16[384,384]{1,0:T(8,128)(2,1)S(1)} %get-tuple-element.65.query_ref) | copy-start | bytes 884740
  21.9 43.3 %copy-start.9 = (bf16[384,384]{1,0:T(8,128)(2,1)}, bf16[384,384]{1,0:T(8,128)(2,1)S(1)}, u32[]{:S(2)}) copy-start(bf16[384,384]{1,0:T(8,128)(2,1)S(1)} %get-tuple-element.66.query_ref) | copy-start | bytes 884740
  24.8 38.9 %copy-start.17 = (bf16[784,384]{1,0:T(8,128)(2,1)}, bf16[784,384]{1,0:T(8,128)(2,1)S(1)}, u32[]{:S(2)}) copy-start(bf16[784,384]{1,0:T(8,128)(2,1)S(1)} %collective-permute-done.refs_1_) | copy-start | bytes 1806340
  24.8 23.7 %collective-permute-start.4 = (bf16[784,384]{1,0:T(8,128)(2,1)S(1)}, bf16[784,384]{1,0:T(8,128)(2,1)}, u32[]{:S(2)}, u32[]{:S(2)}) collective-permute-start(bf16[784,384]{1,0:T(8,128)(2,1)S(1)} %collective-permute-done.refs_1_), channel_id=1, source_target_pairs={{8,0},{16,8},{24,16},{9,1},{17,9},{25,17},{10,2},{18,10},{26,18},{... | collective-permute-start | bytes 1806344 | tf_op jit(solution)/shard_map/ppermute | solution.py:134
  32.1 31.6 %copy-start.19 = (bf16[784,384]{1,0:T(8,128)(2,1)}, bf16[784,384]{1,0:T(8,128)(2,1)S(1)}, u32[]{:S(2)}) copy-start(bf16[784,384]{1,0:T(8,128)(2,1)S(1)} %collective-permute-done.3.refs_4_) | copy-start | bytes 1806340
  32.1 22.7 %collective-permute-start.2 = (bf16[784,384]{1,0:T(8,128)(2,1)S(1)}, bf16[784,384]{1,0:T(8,128)(2,1)S(1)}, u32[]{:S(2)}, u32[]{:S(2)}) collective-permute-start(bf16[784,384]{1,0:T(8,128)(2,1)S(1)} %collective-permute-done.refs_1_), channel_id=1, source_target_pairs={{0,8},{8,16},{16,24},{1,9},{9,17},{17,25},{2,10},{10,18},{18,26},{... | collective-permute-start | bytes 1806344 | tf_op jit(solution)/shard_map/ppermute | solution.py:134
  37.6 27.0 %collective-permute-start.6 = (bf16[768,384]{1,0:T(8,128)(2,1)S(1)}, bf16[768,384]{1,0:T(8,128)(2,1)S(1)}, u32[]{:S(2)}, u32[]{:S(2)}) collective-permute-start(bf16[768,384]{1,0:T(8,128)(2,1)S(1)} %pad_maximum_fusion.1.refs_0_), channel_id=1, source_target_pairs={{0,8},{8,16},{16,24},{1,9},{9,17},{17,25},{2,10},{10,18},{18,26},{... | collective-permute-start | bytes 1769480 | tf_op jit(solution)/shard_map/ppermute | solution.py:134
  42.0 22.6 %collective-permute-start.9 = (bf16[768,384]{1,0:T(8,128)(2,1)}, bf16[768,384]{1,0:T(8,128)(2,1)S(1)}, u32[]{:S(2)}, u32[]{:S(2)}) collective-permute-start(bf16[768,384]{1,0:T(8,128)(2,1)} %collective-permute-done.5.refs_1_), channel_id=1, source_target_pairs={{8,0},{16,8},{24,16},{9,1},{17,9},{25,17},{10,2},{18,10},{26,18},{... | collective-permute-start | bytes 1769480 | tf_op jit(solution)/shard_map/ppermute | solution.py:134
  48.5 16.1 %collective-permute-start.7 = (bf16[768,384]{1,0:T(8,128)(2,1)}, bf16[768,384]{1,0:T(8,128)(2,1)S(1)}, u32[]{:S(2)}, u32[]{:S(2)}) collective-permute-start(bf16[768,384]{1,0:T(8,128)(2,1)} %collective-permute-done.5.refs_1_), channel_id=1, source_target_pairs={{0,8},{8,16},{16,24},{1,9},{9,17},{17,25},{2,10},{10,18},{18,26},{... | collective-permute-start | bytes 1769480 | tf_op jit(solution)/shard_map/ppermute | solution.py:134
  54.8 8.9 %copy-start.21 = (bf16[784,384]{1,0:T(8,128)(2,1)}, bf16[784,384]{1,0:T(8,128)(2,1)S(1)}, u32[]{:S(2)}) copy-start(bf16[784,384]{1,0:T(8,128)(2,1)S(1)} %collective-permute-done.2.refs_3_) | copy-start | bytes 1806340
  64.6 7.6 %copy-start.23 = (bf16[768,384]{1,0:T(8,128)(2,1)}, bf16[768,384]{1,0:T(8,128)(2,1)S(1)}, u32[]{:S(2)}) copy-start(bf16[768,384]{1,0:T(8,128)(2,1)S(1)} %collective-permute-done.6.refs_2_) | copy-start | bytes 1769476
  64.6 7.6 %copy-start.25 = (bf16[768,384]{1,0:T(8,128)(2,1)}, bf16[768,384]{1,0:T(8,128)(2,1)S(1)}, u32[]{:S(2)}) copy-start(bf16[768,384]{1,0:T(8,128)(2,1)S(1)} %collective-permute-done.9.refs_5_) | copy-start | bytes 1769476
  65.2 7.0 %copy-start.27 = (bf16[768,384]{1,0:T(8,128)(2,1)}, bf16[768,384]{1,0:T(8,128)(2,1)S(1)}, u32[]{:S(2)}) copy-start(bf16[768,384]{1,0:T(8,128)(2,1)S(1)} %collective-permute-done.7.refs_3_) | copy-start | bytes 1769476
  78.7 5.1 %collective-permute-start.10 = (bf16[1536,768]{1,0:T(8,128)(2,1)}, bf16[1536,768]{1,0:T(8,128)(2,1)S(1)}, u32[]{:S(2)}, u32[]{:S(2)}) collective-permute-start(bf16[1536,768]{1,0:T(8,128)(2,1)} %convolution_convert_fusion), channel_id=1, source_target_pairs={{0,8},{8,0},{16,24},{24,16},{1,9},{9,1},{17,25},{25,17},{2,10},{10... | collective-permute-start | bytes 7077896 | tf_op jit(solution)/shard_map/ppermute | solution.py:139
  78.7 5.1 %copy-start.35 = (bf16[384,768]{1,0:T(8,128)(2,1)S(1)}, bf16[384,768]{1,0:T(8,128)(2,1)}, u32[]{:S(2)}) copy-start(bf16[384,768]{1,0:T(8,128)(2,1)} %copy-done.34) | copy-start | bytes 1769476
  85.3 3.9 %copy-start.33 = (f32[1536,768]{1,0:T(8,128)}, f32[1536,768]{1,0:T(8,128)S(1)}, u32[]{:S(2)}) copy-start(f32[1536,768]{1,0:T(8,128)S(1)} %convert_add_fusion) | copy-start | bytes 14155780
  85.3 3.8 %copy-start.12 = (bf16[384,384]{1,0:T(8,128)(2,1)S(1)}, bf16[384,384]{1,0:T(8,128)(2,1)}, u32[]{:S(2)}) copy-start(bf16[384,384]{1,0:T(8,128)(2,1)} %copy-done.11) | copy-start | bytes 884740
  85.3 3.8 %copy-start.18 = (bf16[784,384]{1,0:T(8,128)(2,1)S(1)}, bf16[784,384]{1,0:T(8,128)(2,1)}, u32[]{:S(2)}) copy-start(bf16[784,384]{1,0:T(8,128)(2,1)} %copy-done.17) | copy-start | bytes 1806340
  85.3 3.8 %copy-start.20 = (bf16[784,384]{1,0:T(8,128)(2,1)S(1)}, bf16[784,384]{1,0:T(8,128)(2,1)}, u32[]{:S(2)}) copy-start(bf16[784,384]{1,0:T(8,128)(2,1)} %copy-done.19) | copy-start | bytes 1806340
  85.3 3.8 %copy-start.22 = (bf16[784,384]{1,0:T(8,128)(2,1)S(1)}, bf16[784,384]{1,0:T(8,128)(2,1)}, u32[]{:S(2)}) copy-start(bf16[784,384]{1,0:T(8,128)(2,1)} %copy-done.21) | copy-start | bytes 1806340
  85.3 3.8 %copy-start.30 = (f32[384,384]{1,0:T(8,128)S(1)}, f32[384,384]{1,0:T(8,128)}, u32[]{:S(2)}) copy-start(f32[384,384]{1,0:T(8,128)} %copy-done.29) | copy-start | bytes 1769476
  86.3 2.8 %copy-start.2 = (bf16[784,384]{1,0:T(8,128)(2,1)S(1)}, bf16[784,384]{1,0:T(8,128)(2,1)}, u32[]{:S(2)}) copy-start(bf16[784,384]{1,0:T(8,128)(2,1)} %copy-done.1) | copy-start | bytes 1806340
  86.3 2.9 %copy-start.8 = (bf16[384,384]{1,0:T(8,128)(2,1)S(1)}, bf16[384,384]{1,0:T(8,128)(2,1)}, u32[]{:S(2)}) copy-start(bf16[384,384]{1,0:T(8,128)(2,1)} %copy-done.7) | copy-start | bytes 884740
  86.4 24.9 %collective-permute-start.11 = (bf16[384,768]{1,0:T(8,128)(2,1)S(1)}, bf16[384,768]{1,0:T(8,128)(2,1)S(1)}, u32[]{:S(2)}, u32[]{:S(2)}) collective-permute-start(bf16[384,768]{1,0:T(8,128)(2,1)S(1)} %get-tuple-element.24), channel_id=1, source_target_pairs={{0,4},{4,0},{8,12},{12,8},{16,20},{20,16},{24,28},{28,24},{1,5},{5... | collective-permute-start | bytes 1769480 | tf_op jit(solution)/shard_map/ppermute | solution.py:206
  87.7 23.6 %collective-permute-start.12 = (bf16[384,768]{1,0:T(8,128)(2,1)S(1)}, bf16[384,768]{1,0:T(8,128)(2,1)S(1)}, u32[]{:S(2)}, u32[]{:S(2)}) collective-permute-start(bf16[384,768]{1,0:T(8,128)(2,1)S(1)} %get-tuple-element.25), channel_id=1, source_target_pairs={{0,16},{4,20},{8,24},{12,28},{16,0},{20,4},{24,8},{28,12},{1,17},{... | collective-permute-start | bytes 1769480 | tf_op jit(solution)/shard_map/ppermute | solution.py:206
  87.8 50.0 %collective-permute-start.19 = (bf16[384,768]{1,0:T(8,128)(2,1)}, bf16[384,768]{1,0:T(8,128)(2,1)}, u32[]{:S(2)}, u32[]{:S(2)}) collective-permute-start(bf16[384,768]{1,0:T(8,128)(2,1)} %get-tuple-element.33), channel_id=1, source_target_pairs={{0,20},{4,16},{8,28},{12,24},{16,4},{20,0},{24,12},{28,8},{1,21},{... | collective-permute-start | bytes 1769480 | tf_op jit(solution)/shard_map/ppermute | solution.py:206
  103.8 8.5 %copy-start.4 = (bf16[768,384]{1,0:T(8,128)(2,1)S(1)}, bf16[768,384]{1,0:T(8,128)(2,1)}, u32[]{:S(2)}) copy-start(bf16[768,384]{1,0:T(8,128)(2,1)} %copy-done.3) | copy-start | bytes 1769476
  103.8 8.5 %copy-start.6 = (bf16[384,384]{1,0:T(8,128)(2,1)S(1)}, bf16[384,384]{1,0:T(8,128)(2,1)}, u32[]{:S(2)}) copy-start(bf16[384,384]{1,0:T(8,128)(2,1)} %copy-done.5) | copy-start | bytes 884740
  103.8 8.5 %copy-start.10 = (bf16[384,384]{1,0:T(8,128)(2,1)S(1)}, bf16[384,384]{1,0:T(8,128)(2,1)}, u32[]{:S(2)}) copy-start(bf16[384,384]{1,0:T(8,128)(2,1)} %copy-done.9) | copy-start | bytes 884740
  103.8 8.5 %copy-start.24 = (bf16[768,384]{1,0:T(8,128)(2,1)S(1)}, bf16[768,384]{1,0:T(8,128)(2,1)}, u32[]{:S(2)}) copy-start(bf16[768,384]{1,0:T(8,128)(2,1)} %copy-done.23) | copy-start | bytes 1769476
  103.9 8.5 %copy-start.26 = (bf16[768,384]{1,0:T(8,128)(2,1)S(1)}, bf16[768,384]{1,0:T(8,128)(2,1)}, u32[]{:S(2)}) copy-start(bf16[768,384]{1,0:T(8,128)(2,1)} %copy-done.25) | copy-start | bytes 1769476
  103.9 8.5 %copy-start.28 = (bf16[768,384]{1,0:T(8,128)(2,1)S(1)}, bf16[768,384]{1,0:T(8,128)(2,1)}, u32[]{:S(2)}) copy-start(bf16[768,384]{1,0:T(8,128)(2,1)} %copy-done.27) | copy-start | bytes 1769476
  103.9 8.5 %copy-start.32 = (f32[384,384]{1,0:T(8,128)S(1)}, f32[384,384]{1,0:T(8,128)}, u32[]{:S(2)}) copy-start(f32[384,384]{1,0:T(8,128)} %copy-done.31) | copy-start | bytes 1769476
  105.6 35.4 %collective-permute-start.13 = (bf16[2,768,384]{2,1,0:T(8,128)(2,1)}, bf16[2,768,384]{2,1,0:T(8,128)(2,1)}, u32[]{:S(2)}, u32[]{:S(2)}) collective-permute-start(bf16[2,768,384]{2,1,0:T(8,128)(2,1)} %get-tuple-element.37), channel_id=1, source_target_pairs={{8,0},{16,8},{24,16},{9,1},{17,9},{25,17},{10,2},{18,10},{26,18},{... | collective-permute-start | bytes 3538952 | tf_op jit(solution)/shard_map/ppermute | solution.py:134
  108.9 32.0 %collective-permute-start.14 = (bf16[2,768,384]{2,1,0:T(8,128)(2,1)}, bf16[2,768,384]{2,1,0:T(8,128)(2,1)}, u32[]{:S(2)}, u32[]{:S(2)}) collective-permute-start(bf16[2,768,384]{2,1,0:T(8,128)(2,1)} %get-tuple-element.38), channel_id=1, source_target_pairs={{0,8},{8,16},{16,24},{1,9},{9,17},{17,25},{2,10},{10,18},{18,26},{... | collective-permute-start | bytes 3538952 | tf_op jit(solution)/shard_map/ppermute | solution.py:134
  129.4 20.9 %collective-permute-start.16 = (bf16[2,768,384]{2,1,0:T(8,128)(2,1)}, bf16[2,768,384]{2,1,0:T(8,128)(2,1)}, u32[]{:S(2)}, u32[]{:S(2)}) collective-permute-start(bf16[2,768,384]{2,1,0:T(8,128)(2,1)} %get-tuple-element.39), channel_id=1, source_target_pairs={{8,0},{16,8},{24,16},{9,1},{17,9},{25,17},{10,2},{18,10},{26,18},{... | collective-permute-start | bytes 3538952 | tf_op jit(solution)/shard_map/ppermute | solution.py:134
  135.9 15.4 %collective-permute-start.17 = (bf16[2,768,384]{2,1,0:T(8,128)(2,1)}, bf16[2,768,384]{2,1,0:T(8,128)(2,1)}, u32[]{:S(2)}, u32[]{:S(2)}) collective-permute-start(bf16[2,768,384]{2,1,0:T(8,128)(2,1)} %get-tuple-element.40), channel_id=1, source_target_pairs={{0,8},{8,16},{16,24},{1,9},{9,17},{17,25},{2,10},{10,18},{18,26},{... | collective-permute-start | bytes 3538952 | tf_op jit(solution)/shard_map/ppermute | solution.py:134
  143.0 13.4 %collective-permute-start.15 = (bf16[768,384]{1,0:T(8,128)(2,1)S(1)}, bf16[768,384]{1,0:T(8,128)(2,1)S(1)}, u32[]{:S(2)}, u32[]{:S(2)}) collective-permute-start(bf16[768,384]{1,0:T(8,128)(2,1)S(1)} %fusion.10), channel_id=1, source_target_pairs={{0,4},{4,0},{1,5},{5,1},{2,6},{6,2},{3,7},{7,3},{8,12},{12,8},{9,1... | collective-permute-start | bytes 1769480 | tf_op jit(solution)/shard_map/ppermute | solution.py:139
  153.7 15.5 %collective-permute-start.18 = (bf16[768,384]{1,0:T(8,128)(2,1)S(1)}, bf16[768,384]{1,0:T(8,128)(2,1)S(1)}, u32[]{:S(2)}, u32[]{:S(2)}) collective-permute-start(bf16[768,384]{1,0:T(8,128)(2,1)S(1)} %fusion.11), channel_id=1, source_target_pairs={{0,4},{4,0},{1,5},{5,1},{2,6},{6,2},{3,7},{7,3},{8,12},{12,8},{9,1... | collective-permute-start | bytes 1769480 | tf_op jit(solution)/shard_map/ppermute | solution.py:139
  (12 other events, 15.8 us)
Sparse Core Ops, SparseCore 0:
  20.2 50.7 all-gather.1

commit v4 on v3

--- a/solution.py
+++ b/solution.py
@@ -9,7 +9,6 @@
 
 HDIM = 128
 TILE = 384
-CHUNKS = 2
 LOG2E = 1.4426950408889634
 
 neg_large = -1e30
@@ -210,8 +209,10 @@
 def on_device(queries, keys, values, out_grad, out_weight, window, counts):
     row_count, width_local = queries.shape
     heads_local = width_local // HDIM
-    chunks = CHUNKS if heads_local % CHUNKS == 0 and heads_local > CHUNKS else 1
-    width = width_local // chunks
+    first_heads = max(heads_local - heads_local // 3, min(heads_local, 2))
+    bounds = [(0, first_heads * HDIM), (first_heads * HDIM, width_local)]
+    bounds = [(low, high) for low, high in bounds if high > low]
+    chunks = len(bounds)
     time_size, height_size = lax.axis_size("tm"), lax.axis_size("height")
     time_place, height_place = lax.axis_index("tm"), lax.axis_index("height")
     sends = height_sends()
@@ -219,14 +220,15 @@
     full_grad = lax.all_gather(out_grad, "head", axis=1, tiled=True)
 
     def columns(x, chunk):
-        return x[:, chunk * width : (chunk + 1) * width]
+        low, high = bounds[chunk]
+        return x[:, low:high]
 
     packs = []
     for chunk in range(chunks):
         parts = [columns(keys, chunk), columns(values, chunk)]
         if chunk == 0:
             parts.append(
-                jnp.where(jnp.arange(width) < HDIM, counts // 16, counts % 16)[None]
+                jnp.where(jnp.arange(bounds[0][1]) < HDIM, counts // 16, counts % 16)[None]
                 .astype(jnp.bfloat16)
                 .repeat(16, axis=0)
             )
@@ -236,7 +238,7 @@
             near + [moved(x, "tm", 1) for x in near] + [moved(x, "tm", -1) for x in near]
         )
     count_all = [
-        (x[2 * TILE, 0].astype(jnp.int32) * 16 + x[2 * TILE, width - 1].astype(jnp.int32))
+        (x[2 * TILE, 0].astype(jnp.int32) * 16 + x[2 * TILE, bounds[0][1] - 1].astype(jnp.int32))
         for x in packs[0]
     ]
     positions = jnp.arange(TILE, dtype=jnp.int32)
@@ -269,6 +271,13 @@
     grad_out, sent = lax.optimization_barrier((grad_out, sent))
     got = exchanged(masks, sent)
     outs = []
+
+    def height_returned(query_out, final, height_sent):
+        for (_, give), x in zip(sends, height_sent):
+            final = final + give(x).astype(jnp.float32)
+        final = final.astype(jnp.bfloat16)
+        return query_out, final[:TILE], final[TILE:]
+
     for chunk in range(chunks):
         attended, total = ahead_of[chunk]
         grad_part = columns(grad_out, chunk)
@@ -277,14 +286,15 @@
         query_out, pair_out = backward(
             bias, columns(queries, chunk), grad_part, attended, total, packs[chunk]
         )
+        if chunk > 0:
+            pair_out, height_sent = lax.optimization_barrier((pair_out, height_sent))
+            outs.append(height_returned(kept_query, kept_own, height_sent))
         back = moved(pair_out[per : 2 * per], "tm", -1).astype(jnp.float32)
         ahead = moved(pair_out[2 * per :], "tm", 1).astype(jnp.float32)
         own = pair_out[:per].astype(jnp.float32) + back + ahead
-        final = own[0]
-        for place, (_, give) in enumerate(sends):
-            final = final + give(own[1 + place].astype(jnp.bfloat16)).astype(jnp.float32)
-        final = final.astype(jnp.bfloat16)
-        outs.append((query_out, final[:TILE], final[TILE:]))
+        height_sent = [own[1 + place].astype(jnp.bfloat16) for place in range(per - 1)]
+        kept_query, kept_own = query_out, own[0]
+    outs.append(height_returned(kept_query, kept_own, height_sent))
     joined = tuple(jnp.concatenate([out[i] for out in outs], axis=1) for i in range(3))
     weight_out = kept + sum(x.astype(jnp.float32) for x in got)
     return joined + (weight_out * token_share,)

time: 181 us -> 208 us (1.15); the launches traced: 178 us -> 207 us
  waiting for transfers between devices: 21.9 us -> 51.7 us
  matrix products: 9.42 us -> 14.5 us
  starting transfers between devices: 45.6 us -> 42.5 us
  other arithmetic: 10.6 us -> 7.87 us
    ppermute x12, waiting for transfers between devices: 7.94 us -> 24.7 us  [moved(): return lax.ppermute(x, axis, pairs)]
    ppermute x5, waiting for transfers between devices: 13.9 us -> 27 us  [swapped(): return lax.ppermute(x, axis, [(i, i ^ 1 << bit) for i in range(size)])]
    dot_general x2, matrix products: 4.33 us -> 9.44 us  [product(): lax.dot_general(part.reshape(rows, -1), attended, (((0,), (0,)), ((), ())...]
    ppermute x12, starting transfers between devices: 40 us -> 36.2 us  [moved(): return lax.ppermute(x, axis, pairs)]
    slice x2, local copies, waits for them, and re-layouts: 3.54 us -> 1.45 us  [on_device(): back = moved(pair_out[per:2 * per], 'tm', -1).astype(jnp.float32)]
    add x2, other arithmetic: 4.37 us -> 2.28 us  [on_device(): own = pair_out[:per].astype(jnp.float32) + back + ahead]
    unnamed x79 -> x51, local copies, waits for them, and re-layouts: 5.53 us -> 3.5 us
    slice x11 -> x20, local copies, waits for them, and re-layouts: 7.66 us -> 8.62 us  [the longest x6 6.22 us: on_device(): x[2 * TILE, bounds[0][1] - 1].astype(jnp.int32)]
  transfers between devices with their start and end apart: 21 -> 21, of which waited for: 5 -> 7; matrix products, arithmetic and copies ran while one was open for 14% -> 12% of each run, Pallas kernels for 24% -> 20%
where the time goes in v4:
time: 208 us; the launch traced here: 207 us
  waiting for transfers between devices  51.7 us (25%)
  starting transfers between devices  42.5 us (20%)
  Pallas kernels  41.7 us (20%)
  between operations  27.2 us (13%)
  local copies, waits for them, and re-layouts  21.8 us (10%)
  matrix products  14.5 us (7%)
  other arithmetic  7.87 us (4%)
    ppermute x12, starting transfers between devices, moved(): return lax.ppermute(x, axis, pairs)  36.2 us
    pallas_call x2, Pallas kernels, backward(): pl.pallas_call(functools.partial(backward_kernel, slots), grid=(heads,),...  28.6 us
    ppermute x5, waiting for transfers between devices, swapped(): return lax.ppermute(x, axis, [(i, i ^ 1 << bit) for i in range(size)])  27 us
    ppermute x12, waiting for transfers between devices, moved(): return lax.ppermute(x, axis, pairs)  24.7 us
    pallas_call x2, Pallas kernels, forward(): pl.pallas_call(functools.partial(forward_kernel, slots), grid=(heads,), i...  13.1 us
    dot_general x2, matrix products, product(): lax.dot_general(part.reshape(rows, -1), attended, (((0,), (0,)), ((), ())...  9.44 us
    slice x6, local copies, waits for them, and re-layouts, on_device(): x[2 * TILE, bounds[0][1] - 1].astype(jnp.int32)  6.22 us
    dot_general x1, matrix products, on_device(): jnp.dot(full_grad, out_weight, preferred_element_type=jnp.float32)  5.09 us
  transfers between devices with their start and end apart: 21, of which 7 were waited for; matrix products, arithmetic and copies ran while one was open for 12% of the time, Pallas kernels for 20%

profile of v4, /device:TPU:1, one launch (start us, length us, event | category | flops | bytes accessed | tf_op | source)
XLA Modules:
  0.0 207.3 jit_solution(5725489320520978344)
XLA Ops:
  8.4 2.1 %collective-permute-start = (bf16[784,512]{1,0:T(8,128)(2,1)S(1)}, bf16[784,512]{1,0:T(8,128)(2,1)S(1)}, u32[]{:S(2)}, u32[]{:S(2)}) collective-permute-start(bf16[784,512]{1,0:T(8,128)(2,1)S(1)} %pad_maximum_fusion.refs_0_), channel_id=1, source_target_pairs={{0,4},{4,0},{1,5},{5,1},{2,6},{6,2},{3,7},{7,3},{8,12},{12,8},{9,1... | collective-permute-start | bytes 2408456 | tf_op jit(solution)/shard_map/ppermute | solution.py:138
  10.5 2.9 %collective-permute-start.3 = (bf16[784,512]{1,0:T(8,128)(2,1)S(1)}, bf16[784,512]{1,0:T(8,128)(2,1)}, u32[]{:S(2)}, u32[]{:S(2)}) collective-permute-start(bf16[784,512]{1,0:T(8,128)(2,1)S(1)} %pad_maximum_fusion.refs_0_), channel_id=1, source_target_pairs={{8,0},{16,8},{24,16},{9,1},{17,9},{25,17},{10,2},{18,10},{26,18},{... | collective-permute-start | bytes 2408456 | tf_op jit(solution)/shard_map/ppermute | solution.py:133
  13.3 3.0 %collective-permute-start.1 = (bf16[784,512]{1,0:T(8,128)(2,1)S(1)}, bf16[784,512]{1,0:T(8,128)(2,1)}, u32[]{:S(2)}, u32[]{:S(2)}) collective-permute-start(bf16[784,512]{1,0:T(8,128)(2,1)S(1)} %pad_maximum_fusion.refs_0_), channel_id=1, source_target_pairs={{0,8},{8,16},{16,24},{1,9},{9,17},{17,25},{2,10},{10,18},{18,26},{... | collective-permute-start | bytes 2408456 | tf_op jit(solution)/shard_map/ppermute | solution.py:133
  16.8 11.3 %collective-permute-done.refs_1_ = bf16[784,512]{1,0:T(8,128)(2,1)S(1)} collective-permute-done((bf16[784,512]{1,0:T(8,128)(2,1)S(1)}, bf16[784,512]{1,0:T(8,128)(2,1)S(1)}, u32[]{:S(2)}, u32[]{:S(2)}) %collective-permute-start) | collective-permute-done | bytes 802848 | tf_op jit(solution)/shard_map/ppermute | solution.py:138
  28.1 4.0 %collective-permute-start.4 = (bf16[784,512]{1,0:T(8,128)(2,1)S(1)}, bf16[784,512]{1,0:T(8,128)(2,1)}, u32[]{:S(2)}, u32[]{:S(2)}) collective-permute-start(bf16[784,512]{1,0:T(8,128)(2,1)S(1)} %collective-permute-done.refs_1_), channel_id=1, source_target_pairs={{8,0},{16,8},{24,16},{9,1},{17,9},{25,17},{10,2},{18,10},{26,18},{... | collective-permute-start | bytes 2408456 | tf_op jit(solution)/shard_map/ppermute | solution.py:133
  32.1 0.7 constant_dynamic-slice_fusion.4
  32.7 3.6 %collective-permute-start.2 = (bf16[784,512]{1,0:T(8,128)(2,1)S(1)}, bf16[784,512]{1,0:T(8,128)(2,1)}, u32[]{:S(2)}, u32[]{:S(2)}) collective-permute-start(bf16[784,512]{1,0:T(8,128)(2,1)S(1)} %collective-permute-done.refs_1_), channel_id=1, source_target_pairs={{0,8},{8,16},{16,24},{1,9},{9,17},{17,25},{2,10},{10,18},{18,26},{... | collective-permute-start | bytes 2408456 | tf_op jit(solution)/shard_map/ppermute | solution.py:133
  36.9 0.9 slice.126.query_ref
  37.9 1.0 slice.125.query_ref
  44.1 3.3 %collective-permute-start.6 = (bf16[768,256]{1,0:T(8,128)(2,1)S(1)}, bf16[768,256]{1,0:T(8,128)(2,1)S(1)}, u32[]{:S(2)}, u32[]{:S(2)}) collective-permute-start(bf16[768,256]{1,0:T(8,128)(2,1)S(1)} %pad_maximum_fusion.4.refs_0_), channel_id=1, source_target_pairs={{0,8},{8,16},{16,24},{1,9},{9,17},{17,25},{2,10},{10,18},{18,26},{... | collective-permute-start | bytes 1179656 | tf_op jit(solution)/shard_map/ppermute | solution.py:133
  47.4 1.3 fusion.17
  50.0 1.9 collective-permute-start.8
  51.9 3.6 %collective-permute-start.7 = (bf16[768,256]{1,0:T(8,128)(2,1)S(1)}, bf16[768,256]{1,0:T(8,128)(2,1)S(1)}, u32[]{:S(2)}, u32[]{:S(2)}) collective-permute-start(bf16[768,256]{1,0:T(8,128)(2,1)S(1)} %collective-permute-done.5.refs_1_), channel_id=1, source_target_pairs={{0,8},{8,16},{16,24},{1,9},{9,17},{17,25},{2,10},{10,18},{18,26},{... | collective-permute-start | bytes 1179656 | tf_op jit(solution)/shard_map/ppermute | solution.py:133
  55.6 1.3 fusion.19
  60.1 1.9 collective-permute-start.9
  62.0 1.3 fusion.16
  64.6 1.3 fusion.18
  67.3 1.1 copy-done.3
  68.4 8.9 %shard_map.102 = (bf16[384,512]{1,0:T(8,128)(2,1)S(1)}, f32[384,512]{1,0:T(8,128)S(1)}) custom-call(f32[6,1,384]{2,1,0:T(1,128)S(1)} %constant_dynamic-update-slice_fusion.bias_ref, bf16[384,512]{1,0:T(8,128)(2,1)S(1)} %slice.125.query_ref, bf16[784,512]{1,0:T(8,128)(2,1)S(1)} %pad_maximum_fusion.refs_0_, bf16[784,512]{1,0:T(8,128)(2,1)S(1)} %copy-done.3, ...), custom_call_target="tpu_custom_call" | custom-call | flops 14495514624 | bytes 9437184 | tf_op jit(solution)/shard_map/pallas_call | solution.py:89
  77.4 0.8 constant_dynamic-update-slice_fusion.7
  78.3 4.2 %shard_map.103 = (bf16[384,256]{1,0:T(8,128)(2,1)S(1)}, f32[384,256]{1,0:T(8,128)S(1)}) custom-call(f32[6,1,384]{2,1,0:T(1,128)S(1)} %constant_dynamic-update-slice_fusion.bias_ref, bf16[384,256]{1,0:T(8,128)(2,1)S(1)} %slice.126.query_ref, bf16[768,256]{1,0:T(8,128)(2,1)S(1)} %pad_maximum_fusion.4.refs_0_, ...), custom_call_target="tpu_custom_call" | custom-call | flops 7247757312 | bytes 4718592 | tf_op jit(solution)/shard_map/pallas_call | solution.py:89
  82.5 0.7 constant_dynamic-update-slice_fusion.6
  83.9 2.6 %constant_dynamic-slice_fusion.3 = (bf16[384,768]{1,0:T(8,128)(2,1)S(1)}, bf16[384,768]{1,0:T(8,128)(2,1)S(1)}, bf16[384,768]{1,0:T(8,128)(2,1)S(1)}, bf16[384,768]{1,0:T(8,128)(2,1)}) fusion(bf16[384,3072]{1,0:T(8,128)(2,1)} %all-gather.2.cloned.1.call-done, s32[]{:T(128)S(6)} %select_n.142, s32[]{:T(128)S(6)} %select_n.145, s32[]{:T(128)S(6)} %select_n.144, ...), kind=kLoop, calls=%fused_computation.47 | loop fusion | bytes 4718608 | tf_op jit(solution)/shard_map/dynamic_slice | solution.py:179
  86.5 4.0 %convolution_convert_fusion = bf16[1536,768]{1,0:T(8,128)(2,1)} fusion(bf16[384,768]{1,0:T(8,128)(2,1)} %constant_dynamic-update-slice_fusion.6, bf16[384,768]{1,0:T(8,128)(2,1)S(1)} %get-tuple-element.46, bf16[384,768]{1,0:T(8,128)(2,1)S(1)} %get-tuple-element.47), kind=kOutput, calls=%fused_computation.1 | convolution fusion | flops 909508608 | bytes 4128768 | tf_op jit(solution)/shard_map/dot_general | solution.py:164
  90.5 5.1 %convolution_convert_fusion.1 = bf16[384,768]{1,0:T(8,128)(2,1)S(1)} fusion(bf16[384,3072]{1,0:T(8,128)(2,1)} %all-gather.2.cloned.1.call-done, bf16[3072,768]{1,0:T(8,128)(2,1)} %param.11), kind=kOutput, calls=%fused_computation.8 | convolution fusion | flops 1812234240 | bytes 7667712 | tf_op jit(solution)/shard_map/dot_general | solution.py:263
  95.6 5.5 %convert_add_fusion = f32[1536,768]{1,0:T(8,128)} fusion(bf16[1536,768]{1,0:T(8,128)(2,1)} %collective-permute-done.10, bf16[384,768]{1,0:T(8,128)(2,1)} %constant_dynamic-update-slice_fusion.6, bf16[384,768]{1,0:T(8,128)(2,1)S(1)} %copy-done.21, bf16[384,768]{1,0:T(8,128)(2,1)S(1)} %get-tuple-element.45), kind=kOutput, calls=%fused_computation | convolution fusion | flops 910688256 | bytes 8847360 | tf_op jit(solution)/shard_map/dot_general | solution.py:164
  101.1 3.1 %dynamic-slice_convert_fusion = (bf16[384,768]{1,0:T(8,128)(2,1)}, bf16[384,768]{1,0:T(8,128)(2,1)S(1)}, bf16[384,768]{1,0:T(8,128)(2,1)S(1)}) fusion(f32[1536,768]{1,0:T(8,128)} %convert_add_fusion, s32[]{:T(128)S(6)} %select_n.149, s32[]{:T(128)S(6)} %select_n.148, s32[]{:T(128)S(6)} %select_n.147), kind=kLoop, calls=%fused_computation.16 | loop fusion | bytes 3538956 | tf_op jit(solution)/shard_map/convert_element_type | solution.py:192
  104.2 1.2 collective-permute-start.11
  105.4 1.8 collective-permute-start.12
  107.3 19.3 %shard_map.104 = (bf16[384,512]{1,0:T(8,128)(2,1)S(1)}, bf16[6,768,512]{2,1,0:T(8,128)(2,1)S(1)}) custom-call(f32[6,1,384]{2,1,0:T(1,128)S(1)} %constant_dynamic-update-slice_fusion.bias_ref, bf16[384,512]{1,0:T(8,128)(2,1)S(1)} %slice.125.query_ref, bf16[384,512]{1,0:T(8,128)(2,1)S(1)} %slice.129.grad_ref, ...), custom_call_target="tpu_custom_call" | custom-call | flops 21743271936 | bytes 9437184 | tf_op jit(solution)/shard_map/pallas_call | solution.py:112
  126.9 2.6 %collective-permute-start.13 = (bf16[2,768,512]{2,1,0:T(8,128)(2,1)S(1)}, bf16[2,768,512]{2,1,0:T(8,128)(2,1)S(1)}, u32[]{:S(2)}, u32[]{:S(2)}) collective-permute-start(bf16[2,768,512]{2,1,0:T(8,128)(2,1)S(1)} %get-tuple-element.38), channel_id=1, source_target_pairs={{8,0},{16,8},{24,16},{9,1},{17,9},{25,17},{10,2},{18,10},{26,18},{... | collective-permute-start | bytes 4718600 | tf_op jit(solution)/shard_map/ppermute | solution.py:133
  129.5 3.1 %collective-permute-start.14 = (bf16[2,768,512]{2,1,0:T(8,128)(2,1)S(1)}, bf16[2,768,512]{2,1,0:T(8,128)(2,1)S(1)}, u32[]{:S(2)}, u32[]{:S(2)}) collective-permute-start(bf16[2,768,512]{2,1,0:T(8,128)(2,1)S(1)} %get-tuple-element.39), channel_id=1, source_target_pairs={{0,8},{8,16},{16,24},{1,9},{9,17},{17,25},{2,10},{10,18},{18,26},{... | collective-permute-start | bytes 4718600 | tf_op jit(solution)/shard_map/ppermute | solution.py:133
  132.7 0.8 copy-done.22
  133.6 9.3 %shard_map.105 = (bf16[384,256]{1,0:T(8,128)(2,1)S(1)}, bf16[6,768,256]{2,1,0:T(8,128)(2,1)S(1)}) custom-call(f32[6,1,384]{2,1,0:T(1,128)S(1)} %constant_dynamic-update-slice_fusion.bias_ref, bf16[384,256]{1,0:T(8,128)(2,1)S(1)} %slice.126.query_ref, bf16[384,256]{1,0:T(8,128)(2,1)S(1)} %slice.130.grad_ref, bf16[384,256]{1,0:T(8,128)(2,1)S(1)} %copy-done.1, ...), custom_call_target="tpu_custom_call" | custom-call | flops 10871635968 | bytes 4718592 | tf_op jit(solution)/shard_map/pallas_call | solution.py:112
  142.9 18.5 %collective-permute-done.13 = bf16[2,768,512]{2,1,0:T(8,128)(2,1)S(1)} collective-permute-done((bf16[2,768,512]{2,1,0:T(8,128)(2,1)S(1)}, bf16[2,768,512]{2,1,0:T(8,128)(2,1)S(1)}, u32[]{:S(2)}, u32[]{:S(2)}) %collective-permute-start.13) | collective-permute-done | bytes 1572896 | tf_op jit(solution)/shard_map/ppermute | solution.py:133
  161.4 1.2 collective-permute-done.14
  163.3 1.1 fusion.8
  164.4 1.2 fusion.15
  165.6 1.9 collective-permute-start.16
  167.5 4.4 %collective-permute-start.17 = (bf16[2,768,256]{2,1,0:T(8,128)(2,1)}, bf16[2,768,256]{2,1,0:T(8,128)(2,1)}, u32[]{:S(2)}, u32[]{:S(2)}) collective-permute-start(bf16[2,768,256]{2,1,0:T(8,128)(2,1)} %get-tuple-element.44), channel_id=1, source_target_pairs={{0,8},{8,16},{16,24},{1,9},{9,17},{17,25},{2,10},{10,18},{18,26},{... | collective-permute-start | bytes 2359304 | tf_op jit(solution)/shard_map/ppermute | solution.py:133
  172.3 3.1 %add_multiply_fusion = f32[384,768]{1,0:T(8,128)} fusion(bf16[384,768]{1,0:T(8,128)(2,1)} %collective-permute-done.19, bf16[384,768]{1,0:T(8,128)(2,1)} %copy-done.23, bf16[384,768]{1,0:T(8,128)(2,1)} %copy-done.22, f32[1536,768]{1,0:T(8,128)} %convert_add_fusion, s32[]{:T(128)S(6)} %select_n.150), kind=kLoop, calls=%fused_computation.15 | loop fusion | flops 2064384 | bytes 4128772 | tf_op jit(solution)/shard_map/mul | solution.py:300
  175.3 0.9 pad_maximum_fusion.1
  176.2 3.9 %collective-permute-done.16 = bf16[2,768,256]{2,1,0:T(8,128)(2,1)} collective-permute-done((bf16[2,768,256]{2,1,0:T(8,128)(2,1)}, bf16[2,768,256]{2,1,0:T(8,128)(2,1)}, u32[]{:S(2)}, u32[]{:S(2)}) %collective-permute-start.16) | collective-permute-done | bytes 786464 | tf_op jit(solution)/shard_map/ppermute | solution.py:133
  180.2 1.0 collective-permute-done.17
  181.1 1.6 convert_add_fusion.2
  183.1 8.6 %collective-permute-done.15 = bf16[768,512]{1,0:T(8,128)(2,1)S(1)} collective-permute-done((bf16[768,512]{1,0:T(8,128)(2,1)}, bf16[768,512]{1,0:T(8,128)(2,1)S(1)}, u32[]{:S(2)}, u32[]{:S(2)}) %collective-permute-start.15) | collective-permute-done | bytes 786464 | tf_op jit(solution)/shard_map/ppermute | solution.py:138
  192.1 7.2 %collective-permute-done.18 = bf16[768,256]{1,0:T(8,128)(2,1)S(1)} collective-permute-done((bf16[768,256]{1,0:T(8,128)(2,1)S(1)}, bf16[768,256]{1,0:T(8,128)(2,1)S(1)}, u32[]{:S(2)}, u32[]{:S(2)}) %collective-permute-start.18) | collective-permute-done | bytes 393248 | tf_op jit(solution)/shard_map/ppermute | solution.py:138
  199.4 1.1 pad_maximum_fusion.2
  (98 shorter events, 4.9 us)
Async XLA Ops:
  7.2 1.0 slice-start
  7.2 1.1 slice-start.2
  7.2 76.7 %all-gather.2.cloned.1.call-start = ((), (), s32[]{:S(2)}) async-start(), calls=%async_computation | async-start | bytes 2949120 | tf_op jit(solution)/shard_map/all_gather | solution.py:220
  8.0 8.4 %slice-start.1 = ((bf16[384,768]{1,0:T(8,128)(2,1)}), bf16[384,256]{1,0:T(8,128)(2,1)S(1)}, s32[]{:S(2)}) async-start(bf16[384,768]{1,0:T(8,128)(2,1)} %param.8), calls=%async_computation.2 | async-start | bytes 393216 | tf_op jit(solution)/shard_map/slice | solution.py:224
  8.0 8.4 %slice-start.3 = ((bf16[384,768]{1,0:T(8,128)(2,1)}), bf16[384,256]{1,0:T(8,128)(2,1)S(1)}, s32[]{:S(2)}) async-start(bf16[384,768]{1,0:T(8,128)(2,1)} %param.9), calls=%async_computation.4 | async-start | bytes 393216 | tf_op jit(solution)/shard_map/slice | solution.py:224
  8.3 23.8 %copy-start.24 = (s32[1,27]{1,0:T(1,128)S(1)}, s32[1,27]{1,0:T(1,128)}, u32[]{:S(2)}) copy-start(s32[1,27]{1,0:T(1,128)} %param.12) | copy-start | bytes 328
  8.4 19.7 %collective-permute-start = (bf16[784,512]{1,0:T(8,128)(2,1)S(1)}, bf16[784,512]{1,0:T(8,128)(2,1)S(1)}, u32[]{:S(2)}, u32[]{:S(2)}) collective-permute-start(bf16[784,512]{1,0:T(8,128)(2,1)S(1)} %pad_maximum_fusion.refs_0_), channel_id=1, source_target_pairs={{0,4},{4,0},{1,5},{5,1},{2,6},{6,2},{3,7},{7,3},{8,12},{12,8},{9,1... | collective-permute-start | bytes 2408456 | tf_op jit(solution)/shard_map/ppermute | solution.py:138
  10.5 33.6 %collective-permute-start.3 = (bf16[784,512]{1,0:T(8,128)(2,1)S(1)}, bf16[784,512]{1,0:T(8,128)(2,1)}, u32[]{:S(2)}, u32[]{:S(2)}) collective-permute-start(bf16[784,512]{1,0:T(8,128)(2,1)S(1)} %pad_maximum_fusion.refs_0_), channel_id=1, source_target_pairs={{8,0},{16,8},{24,16},{9,1},{17,9},{25,17},{10,2},{18,10},{26,18},{... | collective-permute-start | bytes 2408456 | tf_op jit(solution)/shard_map/ppermute | solution.py:133
  13.3 38.6 %collective-permute-start.1 = (bf16[784,512]{1,0:T(8,128)(2,1)S(1)}, bf16[784,512]{1,0:T(8,128)(2,1)}, u32[]{:S(2)}, u32[]{:S(2)}) collective-permute-start(bf16[784,512]{1,0:T(8,128)(2,1)S(1)} %pad_maximum_fusion.refs_0_), channel_id=1, source_target_pairs={{0,8},{8,16},{16,24},{1,9},{9,17},{17,25},{2,10},{10,18},{18,26},{... | collective-permute-start | bytes 2408456 | tf_op jit(solution)/shard_map/ppermute | solution.py:133
  16.4 33.5 %collective-permute-start.5 = (bf16[768,256]{1,0:T(8,128)(2,1)S(1)}, bf16[768,256]{1,0:T(8,128)(2,1)S(1)}, u32[]{:S(2)}, u32[]{:S(2)}) collective-permute-start(bf16[768,256]{1,0:T(8,128)(2,1)S(1)} %pad_maximum_fusion.4.refs_0_), channel_id=1, source_target_pairs={{0,4},{4,0},{1,5},{5,1},{2,6},{6,2},{3,7},{7,3},{8,12},{12,8},{9,1... | collective-permute-start | bytes 1179656 | tf_op jit(solution)/shard_map/ppermute | solution.py:138
  28.1 39.2 %copy-start.2 = (bf16[784,512]{1,0:T(8,128)(2,1)}, bf16[784,512]{1,0:T(8,128)(2,1)S(1)}, u32[]{:S(2)}) copy-start(bf16[784,512]{1,0:T(8,128)(2,1)S(1)} %collective-permute-done.refs_1_) | copy-start | bytes 2408452
  28.1 32.0 %collective-permute-start.4 = (bf16[784,512]{1,0:T(8,128)(2,1)S(1)}, bf16[784,512]{1,0:T(8,128)(2,1)}, u32[]{:S(2)}, u32[]{:S(2)}) collective-permute-start(bf16[784,512]{1,0:T(8,128)(2,1)S(1)} %collective-permute-done.refs_1_), channel_id=1, source_target_pairs={{8,0},{16,8},{24,16},{9,1},{17,9},{25,17},{10,2},{18,10},{26,18},{... | collective-permute-start | bytes 2408456 | tf_op jit(solution)/shard_map/ppermute | solution.py:133
  32.7 31.9 %collective-permute-start.2 = (bf16[784,512]{1,0:T(8,128)(2,1)S(1)}, bf16[784,512]{1,0:T(8,128)(2,1)}, u32[]{:S(2)}, u32[]{:S(2)}) collective-permute-start(bf16[784,512]{1,0:T(8,128)(2,1)S(1)} %collective-permute-done.refs_1_), channel_id=1, source_target_pairs={{0,8},{8,16},{16,24},{1,9},{9,17},{17,25},{2,10},{10,18},{18,26},{... | collective-permute-start | bytes 2408456 | tf_op jit(solution)/shard_map/ppermute | solution.py:133
  44.1 34.1 %collective-permute-start.6 = (bf16[768,256]{1,0:T(8,128)(2,1)S(1)}, bf16[768,256]{1,0:T(8,128)(2,1)S(1)}, u32[]{:S(2)}, u32[]{:S(2)}) collective-permute-start(bf16[768,256]{1,0:T(8,128)(2,1)S(1)} %pad_maximum_fusion.4.refs_0_), channel_id=1, source_target_pairs={{0,8},{8,16},{16,24},{1,9},{9,17},{17,25},{2,10},{10,18},{18,26},{... | collective-permute-start | bytes 1179656 | tf_op jit(solution)/shard_map/ppermute | solution.py:133
  50.0 28.3 %copy-start.5 = (bf16[768,256]{1,0:T(8,128)(2,1)}, bf16[768,256]{1,0:T(8,128)(2,1)S(1)}, u32[]{:S(2)}) copy-start(bf16[768,256]{1,0:T(8,128)(2,1)S(1)} %collective-permute-done.5.refs_1_) | copy-start | bytes 1179652
  50.0 28.2 %collective-permute-start.8 = (bf16[768,256]{1,0:T(8,128)(2,1)S(1)}, bf16[768,256]{1,0:T(8,128)(2,1)S(1)}, u32[]{:S(2)}, u32[]{:S(2)}) collective-permute-start(bf16[768,256]{1,0:T(8,128)(2,1)S(1)} %pad_maximum_fusion.4.refs_0_), channel_id=1, source_target_pairs={{8,0},{16,8},{24,16},{9,1},{17,9},{25,17},{10,2},{18,10},{26,18},{... | collective-permute-start | bytes 1179656 | tf_op jit(solution)/shard_map/ppermute | solution.py:133
  51.9 26.3 %collective-permute-start.7 = (bf16[768,256]{1,0:T(8,128)(2,1)S(1)}, bf16[768,256]{1,0:T(8,128)(2,1)S(1)}, u32[]{:S(2)}, u32[]{:S(2)}) collective-permute-start(bf16[768,256]{1,0:T(8,128)(2,1)S(1)} %collective-permute-done.5.refs_1_), channel_id=1, source_target_pairs={{0,8},{8,16},{16,24},{1,9},{9,17},{17,25},{2,10},{10,18},{18,26},{... | collective-permute-start | bytes 1179656 | tf_op jit(solution)/shard_map/ppermute | solution.py:133
  60.1 18.1 %collective-permute-start.9 = (bf16[768,256]{1,0:T(8,128)(2,1)S(1)}, bf16[768,256]{1,0:T(8,128)(2,1)S(1)}, u32[]{:S(2)}, u32[]{:S(2)}) collective-permute-start(bf16[768,256]{1,0:T(8,128)(2,1)S(1)} %collective-permute-done.5.refs_1_), channel_id=1, source_target_pairs={{8,0},{16,8},{24,16},{9,1},{17,9},{25,17},{10,2},{18,10},{26,18},{... | collective-permute-start | bytes 1179656 | tf_op jit(solution)/shard_map/ppermute | solution.py:133
  67.3 1.1 copy-start.3
  77.4 5.1 %copy-start.17 = (f32[384,512]{1,0:T(8,128)}, f32[384,512]{1,0:T(8,128)S(1)}, u32[]{:S(2)}) copy-start(f32[384,512]{1,0:T(8,128)S(1)} %get-tuple-element.24.total_ref) | copy-start | bytes 2359300
  78.2 4.3 %copy-start.7 = (bf16[768,256]{1,0:T(8,128)(2,1)}, bf16[768,256]{1,0:T(8,128)(2,1)S(1)}, u32[]{:S(2)}) copy-start(bf16[768,256]{1,0:T(8,128)(2,1)S(1)} %collective-permute-done.6.refs_2_) | copy-start | bytes 1179652
  78.2 4.3 %copy-start.9 = (bf16[768,256]{1,0:T(8,128)(2,1)}, bf16[768,256]{1,0:T(8,128)(2,1)S(1)}, u32[]{:S(2)}) copy-start(bf16[768,256]{1,0:T(8,128)(2,1)S(1)} %collective-permute-done.8.refs_4_) | copy-start | bytes 1179652
  78.2 4.3 %copy-start.11 = (bf16[768,256]{1,0:T(8,128)(2,1)}, bf16[768,256]{1,0:T(8,128)(2,1)S(1)}, u32[]{:S(2)}) copy-start(bf16[768,256]{1,0:T(8,128)(2,1)S(1)} %collective-permute-done.7.refs_3_) | copy-start | bytes 1179652
  78.3 4.2 %copy-start.13 = (bf16[768,256]{1,0:T(8,128)(2,1)}, bf16[768,256]{1,0:T(8,128)(2,1)S(1)}, u32[]{:S(2)}) copy-start(bf16[768,256]{1,0:T(8,128)(2,1)S(1)} %collective-permute-done.9.refs_5_) | copy-start | bytes 1179652
  82.5 4.0 %copy-start.15 = (f32[384,256]{1,0:T(8,128)}, f32[384,256]{1,0:T(8,128)S(1)}, u32[]{:S(2)}) copy-start(f32[384,256]{1,0:T(8,128)S(1)} %get-tuple-element.29.total_ref) | copy-start | bytes 1179652
  90.5 5.1 %collective-permute-start.10 = (bf16[1536,768]{1,0:T(8,128)(2,1)}, bf16[1536,768]{1,0:T(8,128)(2,1)}, u32[]{:S(2)}, u32[]{:S(2)}) collective-permute-start(bf16[1536,768]{1,0:T(8,128)(2,1)} %convolution_convert_fusion), channel_id=1, source_target_pairs={{0,8},{8,0},{16,24},{24,16},{1,9},{9,1},{17,25},{25,17},{2,10},{10... | collective-permute-start | bytes 7077896 | tf_op jit(solution)/shard_map/ppermute | solution.py:138
  90.5 5.1 %copy-start.21 = (bf16[384,768]{1,0:T(8,128)(2,1)S(1)}, bf16[384,768]{1,0:T(8,128)(2,1)}, u32[]{:S(2)}) copy-start(bf16[384,768]{1,0:T(8,128)(2,1)} %get-tuple-element.48) | copy-start | bytes 1769476
  101.1 6.2 %copy-start.4 = (bf16[784,512]{1,0:T(8,128)(2,1)S(1)}, bf16[784,512]{1,0:T(8,128)(2,1)}, u32[]{:S(2)}) copy-start(bf16[784,512]{1,0:T(8,128)(2,1)} %copy-done.2) | copy-start | bytes 2408452
  101.1 6.2 %copy-start.18 = (f32[384,512]{1,0:T(8,128)S(1)}, f32[384,512]{1,0:T(8,128)}, u32[]{:S(2)}) copy-start(f32[384,512]{1,0:T(8,128)} %copy-done.17) | copy-start | bytes 2359300
  104.2 28.6 %collective-permute-start.11 = (bf16[384,768]{1,0:T(8,128)(2,1)S(1)}, bf16[384,768]{1,0:T(8,128)(2,1)S(1)}, u32[]{:S(2)}, u32[]{:S(2)}) collective-permute-start(bf16[384,768]{1,0:T(8,128)(2,1)S(1)} %get-tuple-element.26), channel_id=1, source_target_pairs={{0,4},{4,0},{8,12},{12,8},{16,20},{20,16},{24,28},{28,24},{1,5},{5... | collective-permute-start | bytes 1769480 | tf_op jit(solution)/shard_map/ppermute | solution.py:205
  105.4 27.4 %collective-permute-start.12 = (bf16[384,768]{1,0:T(8,128)(2,1)S(1)}, bf16[384,768]{1,0:T(8,128)(2,1)S(1)}, u32[]{:S(2)}, u32[]{:S(2)}) collective-permute-start(bf16[384,768]{1,0:T(8,128)(2,1)S(1)} %get-tuple-element.27), channel_id=1, source_target_pairs={{0,16},{4,20},{8,24},{12,28},{16,0},{20,4},{24,8},{28,12},{1,17},{... | collective-permute-start | bytes 1769480 | tf_op jit(solution)/shard_map/ppermute | solution.py:205
  126.6 6.9 %copy-start.1 = (bf16[384,256]{1,0:T(8,128)(2,1)S(1)}, bf16[384,256]{1,0:T(8,128)(2,1)}, u32[]{:S(2)}) copy-start(bf16[384,256]{1,0:T(8,128)(2,1)} %copy-done) | copy-start | bytes 589828
  126.6 6.9 %copy-start.6 = (bf16[768,256]{1,0:T(8,128)(2,1)S(1)}, bf16[768,256]{1,0:T(8,128)(2,1)}, u32[]{:S(2)}) copy-start(bf16[768,256]{1,0:T(8,128)(2,1)} %copy-done.5) | copy-start | bytes 1179652
  126.6 6.9 %copy-start.8 = (bf16[768,256]{1,0:T(8,128)(2,1)S(1)}, bf16[768,256]{1,0:T(8,128)(2,1)}, u32[]{:S(2)}) copy-start(bf16[768,256]{1,0:T(8,128)(2,1)} %copy-done.7) | copy-start | bytes 1179652
  126.6 6.9 %copy-start.10 = (bf16[768,256]{1,0:T(8,128)(2,1)S(1)}, bf16[768,256]{1,0:T(8,128)(2,1)}, u32[]{:S(2)}) copy-start(bf16[768,256]{1,0:T(8,128)(2,1)} %copy-done.9) | copy-start | bytes 1179652
  126.7 6.9 %copy-start.12 = (bf16[768,256]{1,0:T(8,128)(2,1)S(1)}, bf16[768,256]{1,0:T(8,128)(2,1)}, u32[]{:S(2)}) copy-start(bf16[768,256]{1,0:T(8,128)(2,1)} %copy-done.11) | copy-start | bytes 1179652
  126.7 6.9 %copy-start.14 = (bf16[768,256]{1,0:T(8,128)(2,1)S(1)}, bf16[768,256]{1,0:T(8,128)(2,1)}, u32[]{:S(2)}) copy-start(bf16[768,256]{1,0:T(8,128)(2,1)} %copy-done.13) | copy-start | bytes 1179652
  126.7 6.9 %copy-start.16 = (f32[384,256]{1,0:T(8,128)S(1)}, f32[384,256]{1,0:T(8,128)}, u32[]{:S(2)}) copy-start(f32[384,256]{1,0:T(8,128)} %copy-done.15) | copy-start | bytes 1179652
  126.9 34.5 %collective-permute-start.13 = (bf16[2,768,512]{2,1,0:T(8,128)(2,1)S(1)}, bf16[2,768,512]{2,1,0:T(8,128)(2,1)S(1)}, u32[]{:S(2)}, u32[]{:S(2)}) collective-permute-start(bf16[2,768,512]{2,1,0:T(8,128)(2,1)S(1)} %get-tuple-element.38), channel_id=1, source_target_pairs={{8,0},{16,8},{24,16},{9,1},{17,9},{25,17},{10,2},{18,10},{26,18},{... | collective-permute-start | bytes 4718600 | tf_op jit(solution)/shard_map/ppermute | solution.py:133
  129.5 33.1 %collective-permute-start.14 = (bf16[2,768,512]{2,1,0:T(8,128)(2,1)S(1)}, bf16[2,768,512]{2,1,0:T(8,128)(2,1)S(1)}, u32[]{:S(2)}, u32[]{:S(2)}) collective-permute-start(bf16[2,768,512]{2,1,0:T(8,128)(2,1)S(1)} %get-tuple-element.39), channel_id=1, source_target_pairs={{0,8},{8,16},{16,24},{1,9},{9,17},{17,25},{2,10},{10,18},{18,26},{... | collective-permute-start | bytes 4718600 | tf_op jit(solution)/shard_map/ppermute | solution.py:133
  132.6 39.6 %collective-permute-start.19 = (bf16[384,768]{1,0:T(8,128)(2,1)}, bf16[384,768]{1,0:T(8,128)(2,1)}, u32[]{:S(2)}, u32[]{:S(2)}) collective-permute-start(bf16[384,768]{1,0:T(8,128)(2,1)} %get-tuple-element.37), channel_id=1, source_target_pairs={{0,20},{4,16},{8,28},{12,24},{16,4},{20,0},{24,12},{28,8},{1,21},{... | collective-permute-start | bytes 1769480 | tf_op jit(solution)/shard_map/ppermute | solution.py:205
  133.5 9.3 %copy-start.23 = (bf16[384,768]{1,0:T(8,128)(2,1)}, bf16[384,768]{1,0:T(8,128)(2,1)S(1)}, u32[]{:S(2)}) copy-start(bf16[384,768]{1,0:T(8,128)(2,1)S(1)} %collective-permute-done.12) | copy-start | bytes 1769476
  163.2 2.4 %copy-start.19 = (f32[2,768,512]{2,1,0:T(8,128)}, f32[2,768,512]{2,1,0:T(8,128)S(1)}, u32[]{:S(2)}) copy-start(f32[2,768,512]{2,1,0:T(8,128)S(1)} %convert_add_fusion.1) | copy-start | bytes 9437188
  165.6 14.6 %collective-permute-start.16 = (bf16[2,768,256]{2,1,0:T(8,128)(2,1)}, bf16[2,768,256]{2,1,0:T(8,128)(2,1)}, u32[]{:S(2)}, u32[]{:S(2)}) collective-permute-start(bf16[2,768,256]{2,1,0:T(8,128)(2,1)} %get-tuple-element.43), channel_id=1, source_target_pairs={{8,0},{16,8},{24,16},{9,1},{17,9},{25,17},{10,2},{18,10},{26,18},{... | collective-permute-start | bytes 2359304 | tf_op jit(solution)/shard_map/ppermute | solution.py:133
  167.5 13.6 %collective-permute-start.17 = (bf16[2,768,256]{2,1,0:T(8,128)(2,1)}, bf16[2,768,256]{2,1,0:T(8,128)(2,1)}, u32[]{:S(2)}, u32[]{:S(2)}) collective-permute-start(bf16[2,768,256]{2,1,0:T(8,128)(2,1)} %get-tuple-element.44), channel_id=1, source_target_pairs={{0,8},{8,16},{16,24},{1,9},{9,17},{17,25},{2,10},{10,18},{18,26},{... | collective-permute-start | bytes 2359304 | tf_op jit(solution)/shard_map/ppermute | solution.py:133
  171.9 19.8 %collective-permute-start.15 = (bf16[768,512]{1,0:T(8,128)(2,1)}, bf16[768,512]{1,0:T(8,128)(2,1)S(1)}, u32[]{:S(2)}, u32[]{:S(2)}) collective-permute-start(bf16[768,512]{1,0:T(8,128)(2,1)} %fusion.8), channel_id=1, source_target_pairs={{0,4},{4,0},{1,5},{5,1},{2,6},{6,2},{3,7},{7,3},{8,12},{12,8},{9,1... | collective-permute-start | bytes 2359304 | tf_op jit(solution)/shard_map/ppermute | solution.py:138
  176.2 15.5 %copy-start.20 = (f32[2,768,512]{2,1,0:T(8,128)S(1)}, f32[2,768,512]{2,1,0:T(8,128)}, u32[]{:S(2)}) copy-start(f32[2,768,512]{2,1,0:T(8,128)} %copy-done.19) | copy-start | bytes 9437188
  182.8 16.4 %collective-permute-start.18 = (bf16[768,256]{1,0:T(8,128)(2,1)S(1)}, bf16[768,256]{1,0:T(8,128)(2,1)S(1)}, u32[]{:S(2)}, u32[]{:S(2)}) collective-permute-start(bf16[768,256]{1,0:T(8,128)(2,1)S(1)} %fusion.11), channel_id=1, source_target_pairs={{0,4},{4,0},{1,5},{5,1},{2,6},{6,2},{3,7},{7,3},{8,12},{12,8},{9,1... | collective-permute-start | bytes 1179656 | tf_op jit(solution)/shard_map/ppermute | solution.py:138
  (2 other events, 1.5 us)
Sparse Core Ops, SparseCore 0:
  16.9 51.5 all-gather.1
